TPU v7x, 32 devices: a whole 2x2x4 slice. The times are simulated.
32 devices in a mesh: seq: 16 (over z, y, x), head: 2 (over core).
Axes of the slice: x: 2, y: 2, z: 4, core: 2. Of those that a mesh axis runs over, the one named last changes fastest.
Arguments:
- stream_in: bfloat16 [2048, 2048], P('seq'), may hold values from -6 to 6
- doc_start: int32 [2048], P('seq'), may hold values from 0 to 2047, as said below
- first_gain: float32 [2048], replicated, may hold values from 0.5 to 1.5
- w_query: bfloat16 [2048, 2048], P('seq', 'head'), may hold values from -0.125 to 0.125
- w_key: bfloat16 [2048, 2048], P('seq', 'head'), may hold values from -0.125 to 0.125
- w_value: bfloat16 [2048, 4096], P('seq', 'head'), may hold values from -0.125 to 0.125
- w_outgate: bfloat16 [2048, 4096], P('seq', 'head'), may hold values from -0.125 to 0.125
- w_decay: bfloat16 [2048, 8], P('seq', 'head'), may hold values from -0.125 to 0.125
- w_rate: bfloat16 [2048, 8], P('seq', 'head'), may hold values from -0.125 to 0.125
- conv_query: float32 [4, 2048], P(None, 'head'), may hold values from -3 to 3
- conv_key: float32 [4, 2048], P(None, 'head'), may hold values from -3 to 3
- conv_value: float32 [4, 4096], P(None, 'head'), may hold values from -3 to 3
- a_log: float32 [8], P('head'), may hold values from -1 to 1.5
- dt_bias: float32 [8], P('head'), may hold values from -6 to -2
- out_gain: float32 [512], replicated, may hold values from 0.5 to 1.5
- w_out: bfloat16 [4096, 2048], P('head', 'seq'), may hold values from -0.1875 to 0.1875
- second_gain: float32 [2048], replicated, may hold values from 0.5 to 1.5
- w_gate: bfloat16 [2048, 5632], P('seq', 'head'), may hold values from -0.125 to 0.125
- w_up: bfloat16 [2048, 5632], P('seq', 'head'), may hold values from -0.125 to 0.125
- w_down: bfloat16 [5632, 2048], P('head', 'seq'), may hold values from -0.078125 to 0.078125
- cotangent: bfloat16 [2048, 2048], P('seq'), may hold values from -6 to 6
Outputs:
- output: bfloat16 [2048, 2048], P('seq')
- grad_input: float32 [2048, 2048], P('seq')
- grad_first_gain: float32 [2048], replicated
- grad_w_query: float32 [2048, 2048], P('seq', 'head')
- grad_w_key: float32 [2048, 2048], P('seq', 'head')
- grad_w_value: float32 [2048, 4096], P('seq', 'head')
- grad_w_outgate: float32 [2048, 4096], P('seq', 'head')
- grad_w_decay: float32 [2048, 8], P('seq', 'head')
- grad_w_rate: float32 [2048, 8], P('seq', 'head')
- grad_conv_query: float32 [4, 2048], P(None, 'head')
- grad_conv_key: float32 [4, 2048], P(None, 'head')
- grad_conv_value: float32 [4, 4096], P(None, 'head')
- grad_a_log: float32 [8], P('head')
- grad_dt_bias: float32 [8], P('head')
- grad_out_gain: float32 [512], replicated
- grad_w_out: float32 [4096, 2048], P('head', 'seq')
- grad_second_gain: float32 [2048], replicated
- grad_w_gate: float32 [2048, 5632], P('seq', 'head')
- grad_w_up: float32 [2048, 5632], P('seq', 'head')
- grad_w_down: float32 [5632, 2048], P('head', 'seq')
Inputs may be any that keep to these rules, and one draw needn't show every extreme that they name: doc_start never falls along the stream, doc_start[t] <= t, and doc_start[t] = t where a document begins; positions 0 and 2047 each begin one; every document has at most 1024 tokens, and one has exactly 1024.
All inputs are finite; a program needn't handle non-finite values.
Results may differ from a plain program's by a relative error of at most 0.012.
Values may be sent and summed in bfloat16 or wider, within the bound.
No kernel may reach another device: no remote copies, remote signals or barrier semaphores. Data moves between devices by JAX's collectives and lax.ppermute only.
A program may use at most 640 MiB of HBM per device.

v0:
```python
import jax
import jax.numpy as jnp
from jax import lax
from jax.sharding import PartitionSpec as P

GROUP = 64


highest = lax.Precision.HIGHEST


def passed_along(value, axis, steps):
    count = lax.axis_size(axis)
    initial, last = (max(0, -steps), min(count, count - steps))
    return lax.ppermute(value, axis, [(source, source + steps) for source in range(initial, last)])


def prefix(value, axis, join, neutral, backward):
    count, mine = (lax.axis_size(axis), lax.axis_index(axis))
    pieces = jax.tree.map(lambda part: lax.all_gather(part, axis), value)
    if backward:
        pieces = jax.tree.map(lambda part: part[::-1], pieces)
        mine = count - 1 - mine
    so_far = jax.tree.map(
        lambda part, zero: jnp.full_like(part, 0) + jnp.asarray(zero, part.dtype), value, neutral
    )

    def step(position, so_far):
        longer = join(so_far, jax.tree.map(lambda part: part[position], pieces))
        return jax.tree.map(lambda new, old: jnp.where(position < mine, new, old), longer, so_far)

    return lax.fori_loop(0, count - 1, step, so_far)


def rounded(values):
    return lax.optimization_barrier(values.astype(jnp.bfloat16)).astype(jnp.float32)


def rms_norm(values, eps):
    return values * lax.rsqrt(jnp.mean(values * values, axis=-1, keepdims=True) + eps)


def outer_rows(left, right):
    return lax.dot_general(
        left, right, (((0,), (0,)), ((), ())), preferred_element_type=jnp.float32
    )


def back_proj(grad, weight):
    return lax.dot_general(
        grad, weight, (((1,), (1,)), ((), ())), preferred_element_type=jnp.float32
    )


def block_step(carried, pieces):
    q, k, values, write_rate, log_decay, starts, places = pieces
    cumulated = jnp.cumsum(log_decay, axis=0)
    keep_mask = (starts[:, None] <= places[None, :]) & (places[:, None] >= places[None, :])
    strict_mask = keep_mask & (places[:, None] > places[None, :])
    gap_log = cumulated[:, None, :] - cumulated[None, :, :]
    fading = jnp.exp(jnp.where(keep_mask[:, :, None], gap_log, -10000.0))
    fading = jnp.transpose(fading, (2, 0, 1))
    from_start = jnp.exp(cumulated) * (starts < places[0]).astype(jnp.float32)[:, None]
    key_key = jnp.einsum("thd,shd->hts", k, k, precision=highest)
    lower_part = key_key * fading * strict_mask.astype(jnp.float32)[None]
    rate_rows = write_rate.T
    system = jnp.eye(q.shape[0], dtype=jnp.float32)[None] + rate_rows[:, :, None] * lower_part
    key_state = jnp.einsum("thd,hde->hte", k, carried, precision=highest)
    right_side = rate_rows[:, :, None] * (
        jnp.transpose(values, (1, 0, 2)) - from_start.T[:, :, None] * key_state
    )
    new_values = jax.scipy.linalg.solve_triangular(
        system, right_side, lower=True, unit_diagonal=True
    )
    query_key = jnp.einsum("thd,shd->hts", q, k, precision=highest) * fading
    query_state = jnp.einsum("thd,hde->hte", q, carried, precision=highest)
    results = from_start.T[:, :, None] * query_state + jnp.einsum(
        "hts,hse->hte", query_key, new_values, precision=highest
    )
    last_row = fading[:, -1, :]
    new_state = from_start[-1][:, None, None] * carried + jnp.einsum(
        "hs,shd,hse->hde", last_row, k, new_values, precision=highest
    )
    return (new_state, jnp.transpose(results, (1, 0, 2)))


def run_chain(carried, q, k, values, write_rate, log_decay, starts, places):
    blocks = q.shape[0] // GROUP

    def split_rows(array):
        return array.reshape((blocks, GROUP) + array.shape[1:])

    pieces = (
        split_rows(q),
        split_rows(k),
        split_rows(values),
        split_rows(write_rate),
        split_rows(log_decay),
        split_rows(starts),
        split_rows(places),
    )
    last_state, results = lax.scan(jax.checkpoint(block_step), carried, pieces)
    return (last_state, results.reshape((q.shape[0],) + results.shape[2:]))


def mixing(q, k, v, write_rate, log_decay, starts, places):
    head_count, key_width = (q.shape[1], q.shape[2])
    zero_state = jnp.zeros((head_count, key_width, v.shape[2]), jnp.float32)
    base_state, base_out = run_chain(zero_state, q, k, v, write_rate, log_decay, starts, places)
    identity_map = jnp.broadcast_to(
        jnp.eye(key_width, dtype=jnp.float32), (head_count, key_width, key_width)
    )
    transfer, probe = run_chain(
        identity_map, q, k, jnp.zeros_like(k), write_rate, log_decay, starts, places
    )
    return (base_out, base_state, probe, transfer)


def prepare(
    ext_query,
    ext_key,
    ext_value,
    decay_raw,
    rate_raw,
    conv_query,
    conv_key,
    conv_value,
    a_log,
    dt_bias,
    starts,
    places,
):
    tok_rows = decay_raw.shape[0]
    head_count = decay_raw.shape[1]
    margin = conv_query.shape[0] - 1

    def filtered(extended, weight):
        summed = jnp.zeros((tok_rows, weight.shape[1]), jnp.float32)
        for offset in range(weight.shape[0]):
            valid = (places - offset >= starts).astype(jnp.float32)[:, None]
            summed = (
                summed
                + weight[offset] * extended[margin - offset : margin - offset + tok_rows] * valid
            )
        return jax.nn.silu(summed)

    q = filtered(ext_query, conv_query).reshape(tok_rows, head_count, -1)
    k = filtered(ext_key, conv_key).reshape(tok_rows, head_count, -1)
    v = filtered(ext_value, conv_value).reshape(tok_rows, head_count, -1)
    q = q * lax.rsqrt(jnp.sum(q * q, axis=-1, keepdims=True) + 1e-06) * q.shape[2] ** (-0.5)
    k = k * lax.rsqrt(jnp.sum(k * k, axis=-1, keepdims=True) + 1e-06)
    write_rate = jax.nn.sigmoid(rate_raw)
    log_decay = -jnp.exp(a_log) * jax.nn.softplus(decay_raw + dt_bias)
    return (q, k, v, write_rate, log_decay)


def out_gate_norm(core, gate_value, out_gain):
    normed = rms_norm(core, 1e-05) * out_gain
    return normed.reshape(gate_value.shape) * jax.nn.silu(gate_value)


def gain_norm(values, gain):
    return rms_norm(values, 1e-06) * gain


def combine_forward(earlier, later):
    return (
        jnp.einsum("hij,hjk->hik", later[0], earlier[0], precision=highest),
        jnp.einsum("hij,hjk->hik", later[0], earlier[1], precision=highest) + later[1],
    )


def combine_backward(earlier, later):
    return (
        jnp.einsum("hij,hjk->hik", earlier[0], later[0], precision=highest),
        later[1] + jnp.einsum("hji,hjk->hik", later[0], earlier[1], precision=highest),
    )


def on_device(
    stream_in,
    doc_start,
    first_gain,
    w_query,
    w_key,
    w_value,
    w_outgate,
    w_decay,
    w_rate,
    conv_query,
    conv_key,
    conv_value,
    a_log,
    dt_bias,
    out_gain,
    w_out,
    second_gain,
    w_gate,
    w_up,
    w_down,
    cotangent,
):
    full = (
        lax.all_gather(w_query, "seq", axis=0, tiled=True),
        lax.all_gather(w_key, "seq", axis=0, tiled=True),
        lax.all_gather(w_value, "seq", axis=0, tiled=True),
        lax.all_gather(w_outgate, "seq", axis=0, tiled=True),
        lax.all_gather(w_decay, "seq", axis=0, tiled=True),
        lax.all_gather(w_rate, "seq", axis=0, tiled=True),
        lax.all_gather(w_out, "seq", axis=1, tiled=True),
        lax.all_gather(w_gate, "seq", axis=0, tiled=True),
        lax.all_gather(w_up, "seq", axis=0, tiled=True),
        lax.all_gather(w_down, "seq", axis=1, tiled=True),
    )
    f_query, f_key, f_value, f_outgate, f_decay, f_rate, f_out, f_gate, f_up, f_down = full
    tok_rows = stream_in.shape[0]
    places = lax.axis_index("seq") * tok_rows + jnp.arange(tok_rows, dtype=jnp.int32)
    stream = stream_in.astype(jnp.float32)
    normed_one, norm_one_back = jax.vjp(gain_norm, stream, first_gain)
    hidden_one = normed_one.astype(jnp.bfloat16)
    hidden_wide = hidden_one.astype(jnp.float32)

    def project(weight):
        return jnp.dot(hidden_one, weight, preferred_element_type=jnp.float32)

    pre_query = project(f_query).astype(jnp.bfloat16)
    pre_key = project(f_key).astype(jnp.bfloat16)
    pre_value = project(f_value).astype(jnp.bfloat16)
    gate_value = project(f_outgate)
    decay_raw = jnp.dot(hidden_wide, f_decay.astype(jnp.float32), precision=highest)
    rate_raw = jnp.dot(hidden_wide, f_rate.astype(jnp.float32), precision=highest)
    margin = conv_query.shape[0] - 1
    wide_query = pre_query.shape[1]
    wide_key = pre_key.shape[1]
    tails = jnp.concatenate(
        [
            pre_query[tok_rows - margin :],
            pre_key[tok_rows - margin :],
            pre_value[tok_rows - margin :],
        ],
        axis=1,
    )
    received = passed_along(tails, "seq", 1)
    ext_query = jnp.concatenate([received[:, :wide_query], pre_query], axis=0).astype(jnp.float32)
    ext_key = jnp.concatenate(
        [received[:, wide_query : wide_query + wide_key], pre_key], axis=0
    ).astype(jnp.float32)
    ext_value = jnp.concatenate([received[:, wide_query + wide_key :], pre_value], axis=0).astype(
        jnp.float32
    )

    def local_prep(
        eq_rows, ek_rows, ev_rows, decay_in, rate_in, cq_taps, ck_taps, cv_taps, alog_in, bias_in
    ):
        return prepare(
            eq_rows,
            ek_rows,
            ev_rows,
            decay_in,
            rate_in,
            cq_taps,
            ck_taps,
            cv_taps,
            alog_in,
            bias_in,
            doc_start,
            places,
        )

    prepared, prep_back = jax.vjp(
        local_prep,
        ext_query,
        ext_key,
        ext_value,
        decay_raw,
        rate_raw,
        conv_query,
        conv_key,
        conv_value,
        a_log,
        dt_bias,
    )
    q = rounded(prepared[0])
    k = rounded(prepared[1])
    v = rounded(prepared[2])
    write_rate, log_decay = (prepared[3], prepared[4])

    def local_mix(q_in, k_in, v_in, rate_in, decay_in):
        return mixing(q_in, k_in, v_in, rate_in, decay_in, doc_start, places)

    mixed, mix_back = jax.vjp(local_mix, q, k, v, write_rate, log_decay)
    base_out, base_state, probe, transfer = mixed
    head_count, key_width = (q.shape[1], q.shape[2])
    identity_map = jnp.broadcast_to(
        jnp.eye(key_width, dtype=jnp.float32), (head_count, key_width, key_width)
    )
    zero_state = jnp.zeros_like(base_state)
    incoming = prefix(
        (transfer, base_state), "seq", combine_forward, (identity_map, zero_state), False
    )[1]
    core = base_out + jnp.einsum("thd,hde->the", probe, incoming, precision=highest)
    gated, gate_back = jax.vjp(out_gate_norm, core, gate_value, out_gain)
    gated_low = gated.astype(jnp.bfloat16)
    mixer_out = lax.psum(jnp.dot(gated_low, f_out, preferred_element_type=jnp.float32), "head")
    middle = stream + mixer_out
    normed_two, norm_two_back = jax.vjp(gain_norm, middle, second_gain)
    hidden_two = normed_two.astype(jnp.bfloat16)
    gate_pre = jnp.dot(hidden_two, f_gate, preferred_element_type=jnp.float32)
    up_pre = jnp.dot(hidden_two, f_up, preferred_element_type=jnp.float32)
    inner = (jax.nn.silu(gate_pre) * up_pre).astype(jnp.bfloat16)
    ffn_out = lax.psum(
        jnp.dot(inner, f_down, preferred_element_type=jnp.float32).astype(jnp.bfloat16), "head"
    ).astype(jnp.float32)
    output = (middle + ffn_out).astype(jnp.bfloat16)
    back_weights = (
        lax.all_gather(w_query, "seq", axis=0, tiled=True),
        lax.all_gather(w_key, "seq", axis=0, tiled=True),
        lax.all_gather(w_value, "seq", axis=0, tiled=True),
        lax.all_gather(w_outgate, "seq", axis=0, tiled=True),
        lax.all_gather(w_decay, "seq", axis=0, tiled=True),
        lax.all_gather(w_rate, "seq", axis=0, tiled=True),
        lax.all_gather(w_out, "seq", axis=1, tiled=True),
        lax.all_gather(w_gate, "seq", axis=0, tiled=True),
        lax.all_gather(w_up, "seq", axis=0, tiled=True),
        lax.all_gather(w_down, "seq", axis=1, tiled=True),
    )
    b_query, b_key, b_value, b_outgate, b_decay, b_rate, b_out, b_gate, b_up, b_down = back_weights
    grad_w_down = outer_rows(inner, cotangent)
    grad_inner = back_proj(cotangent, b_down)
    sigmoid_gate = jax.nn.sigmoid(gate_pre)
    grad_gate_pre = (
        grad_inner * up_pre * sigmoid_gate * (1.0 + gate_pre * (1.0 - sigmoid_gate))
    ).astype(jnp.bfloat16)
    grad_up_pre = (grad_inner * gate_pre * sigmoid_gate).astype(jnp.bfloat16)
    grad_w_gate = outer_rows(hidden_two, grad_gate_pre)
    grad_w_up = outer_rows(hidden_two, grad_up_pre)
    ffn_grads = (grad_w_gate, grad_w_up, grad_w_down)
    two_part = back_proj(grad_gate_pre, b_gate) + back_proj(grad_up_pre, b_up)
    grad_hidden_two = lax.psum(two_part, "head")
    grad_middle_norm, grad_second_gain = norm_two_back(grad_hidden_two)
    grad_middle = cotangent.astype(jnp.float32) + grad_middle_norm
    grad_mixer = grad_middle.astype(jnp.bfloat16)
    grad_w_out = outer_rows(gated_low, grad_mixer)
    grad_gated = back_proj(grad_mixer, b_out)
    grad_core, grad_gate_value, grad_out_part = gate_back(grad_gated)
    grad_gate_low = grad_gate_value.astype(jnp.bfloat16)
    local_pull = jnp.einsum("thd,the->hde", probe, grad_core, precision=highest)
    grad_probe = jnp.einsum("the,hde->thd", grad_core, incoming, precision=highest)
    pulled = prefix(
        (transfer, local_pull), "seq", combine_backward, (identity_map, zero_state), True
    )[1]
    grad_transfer = jnp.einsum("hde,hfe->hdf", pulled, incoming, precision=highest)
    grad_q, grad_k, grad_v, grad_rate, grad_decay = mix_back(
        (grad_core, pulled, grad_probe, grad_transfer)
    )
    (
        g_query,
        g_key,
        g_value,
        g_decay_raw,
        g_rate_raw,
        g_conv_query,
        g_conv_key,
        g_conv_value,
        g_a_log,
        g_dt_bias,
    ) = prep_back((grad_q, grad_k, grad_v, grad_rate, grad_decay))
    edges = jnp.concatenate([g_query[:margin], g_key[:margin], g_value[:margin]], axis=1)
    returned = passed_along(edges.astype(jnp.bfloat16), "seq", -1).astype(edges.dtype)

    def settle(grad_rows, lower_col, upper_col):
        own_rows = grad_rows[margin:]
        return jnp.concatenate(
            [
                own_rows[: tok_rows - margin],
                own_rows[tok_rows - margin :] + returned[:, lower_col:upper_col],
            ],
            axis=0,
        ).astype(jnp.bfloat16)

    grad_pre_query = settle(g_query, 0, wide_query)
    grad_pre_key = settle(g_key, wide_query, wide_query + wide_key)
    grad_pre_value = settle(g_value, wide_query + wide_key, returned.shape[1])
    grad_w_query = outer_rows(hidden_one, grad_pre_query)
    grad_w_key = outer_rows(hidden_one, grad_pre_key)
    grad_w_value = outer_rows(hidden_one, grad_pre_value)
    grad_w_outgate = outer_rows(hidden_one, grad_gate_low)
    grad_w_decay = lax.dot_general(
        hidden_wide, g_decay_raw, (((0,), (0,)), ((), ())), precision=highest
    )
    grad_w_rate = lax.dot_general(
        hidden_wide, g_rate_raw, (((0,), (0,)), ((), ())), precision=highest
    )
    one_part = (
        back_proj(grad_pre_query, b_query)
        + back_proj(grad_pre_key, b_key)
        + back_proj(grad_pre_value, b_value)
        + back_proj(grad_gate_low, b_outgate)
    )
    one_part = one_part + lax.dot_general(
        g_decay_raw, b_decay.astype(jnp.float32), (((1,), (1,)), ((), ())), precision=highest
    )
    one_part = one_part + lax.dot_general(
        g_rate_raw, b_rate.astype(jnp.float32), (((1,), (1,)), ((), ())), precision=highest
    )
    grad_hidden_one, grad_out_heads = lax.psum((one_part, grad_out_part), "head")
    grad_stream_norm, grad_first_part = norm_one_back(grad_hidden_one)
    grad_input = grad_middle + grad_stream_norm
    summed_grads = (
        lax.psum_scatter(grad_w_query, "seq", scatter_dimension=0, tiled=True),
        lax.psum_scatter(grad_w_key, "seq", scatter_dimension=0, tiled=True),
        lax.psum_scatter(grad_w_value, "seq", scatter_dimension=0, tiled=True),
        lax.psum_scatter(grad_w_outgate, "seq", scatter_dimension=0, tiled=True),
        lax.psum_scatter(grad_w_decay, "seq", scatter_dimension=0, tiled=True),
        lax.psum_scatter(grad_w_rate, "seq", scatter_dimension=0, tiled=True),
        lax.psum_scatter(grad_w_out, "seq", scatter_dimension=1, tiled=True),
        lax.psum_scatter(ffn_grads[0], "seq", scatter_dimension=0, tiled=True),
        lax.psum_scatter(ffn_grads[1], "seq", scatter_dimension=0, tiled=True),
        lax.psum_scatter(ffn_grads[2], "seq", scatter_dimension=1, tiled=True),
    )
    small = lax.psum(
        (
            grad_first_part,
            grad_second_gain,
            grad_out_heads,
            g_conv_query,
            g_conv_key,
            g_conv_value,
            g_a_log,
            g_dt_bias,
        ),
        "seq",
    )
    return (
        output,
        grad_input,
        small[0],
        summed_grads[0],
        summed_grads[1],
        summed_grads[2],
        summed_grads[3],
        summed_grads[4],
        summed_grads[5],
        small[3],
        small[4],
        small[5],
        small[6],
        small[7],
        small[2],
        summed_grads[6],
        small[1],
        summed_grads[7],
        summed_grads[8],
        summed_grads[9],
    )


def solution(mesh):
    in_specs = (
        P("seq", None),
        P("seq"),
        P(),
        P("seq", "head"),
        P("seq", "head"),
        P("seq", "head"),
        P("seq", "head"),
        P("seq", "head"),
        P("seq", "head"),
        P(None, "head"),
        P(None, "head"),
        P(None, "head"),
        P("head"),
        P("head"),
        P(),
        P("head", "seq"),
        P(),
        P("seq", "head"),
        P("seq", "head"),
        P("head", "seq"),
        P("seq", None),
    )
    out_specs = (
        P("seq", None),
        P("seq", None),
        P(),
        P("seq", "head"),
        P("seq", "head"),
        P("seq", "head"),
        P("seq", "head"),
        P("seq", "head"),
        P("seq", "head"),
        P(None, "head"),
        P(None, "head"),
        P(None, "head"),
        P("head"),
        P("head"),
        P(),
        P("head", "seq"),
        P(),
        P("seq", "head"),
        P("seq", "head"),
        P("head", "seq"),
    )
    return jax.shard_map(
        on_device, mesh=mesh, in_specs=in_specs, out_specs=out_specs, check_vma=False
    )
```

profile of v0, /device:TPU:0, one launch (start us, length us, event | category | flops | bytes accessed | tf_op | source)
XLA Modules:
  0.0 5705.3 jit_solution(17015504445847904796)
XLA Ops:
  9.5 42.7 all_gather.60
  52.2 36.2 all_gather.64
  98.1 69.2 %all-gather.15.cloned.1.call-done = bf16[2048,1024]{1,0:T(8,128)(2,1)} async-done(((bf16[128,1024]{1,0:T(8,128)(2,1)}), bf16[2048,1024]{1,0:T(8,128)(2,1)}) %all-gather.15.cloned.1.call-update) | async-done | bytes 4194320 | tf_op jit(solution)/shard_map/all_gather | solution.py:204
  170.3 111.3 %all-gather.19.cloned.1.call-done = bf16[2048,2048]{1,0:T(8,128)(2,1)} async-done(((bf16[128,2048]{1,0:T(8,128)(2,1)}), bf16[2048,2048]{1,0:T(8,128)(2,1)}) %all-gather.19.cloned.1.call-update) | async-done | bytes 8388624 | tf_op jit(solution)/shard_map/all_gather | solution.py:206
  298.1 65.4 %while.108 = (s32[]{:T(128)}, f32[4,256,256]{2,1,0:T(8,128)S(1)}, f32[2,64,4,256]{3,1,0,2:T(8,128)S(1)}, f32[2,4,256,256]{3,2,1,0:T(8,128)}, f32[2,64,4]{2,1,0:T...) while((s32[]{:T(128)}, f32[4,256,256]{2,1,0:T(8,128)S(1)}, ...), condition=%wide.region_8.11_spmd.clone, body=%wide.region_6.10_spmd.clone.sunk | while | flops 806498752 | bytes 10578897 | solution.py:102
  306.7 20.4 custom-call.50
  339.4 20.4 custom-call.50
  370.4 79.0 %while.109 = (s32[]{:T(128)}, f32[4,256,512]{2,1,0:T(8,128)S(1)}, f32[2,64,4,512]{3,1,0,2:T(8,128)}, f32[2,4,256,512]{3,2,1,0:T(8,128)}, f32[2,64,4]{2,1,0:T(8,1...) while((s32[]{:T(128)}, f32[4,256,512]{2,1,0:T(8,128)S(1)}, ...), condition=%wide.region_5.7_spmd.clone, body=%wide.region_3.6_spmd.clone.sunk | while | flops 1514091008 | bytes 19429344 | solution.py:102
  380.9 19.7 custom-call.51
  420.6 19.7 custom-call.51
  455.1 100.5 %all-gather.31.cloned.1.call-done = f32[64,256,256]{2,1,0:T(8,128)} async-done(((f32[4,256,256]{2,1,0:T(8,128)}), f32[64,256,256]{2,1,0:T(8,128)}) %all-gather.31.cloned.1.call-update) | async-done | bytes 16777232 | tf_op jit(solution)/shard_map/all_gather | solution.py:20
  555.6 351.7 %all-gather.33.cloned.1.call-done = f32[64,256,512]{2,1,0:T(8,128)} async-done(((f32[4,256,512]{2,1,0:T(8,128)}), f32[64,256,512]{2,1,0:T(8,128)}) %all-gather.33.cloned.1.call-update) | async-done | bytes 33554448 | tf_op jit(solution)/shard_map/all_gather | solution.py:20
  907.3 105.5 %while.110 = (s32[]{:T(128)}, f32[4,256,512]{2,1,0:T(8,128)}, s32[]{:T(128)}, f32[16,4,256,256]{3,2,1,0:T(8,128)}, f32[16,4,256,512]{3,2,1,0:T(8,128)}, /*index=5*/s32[]{:T(128)}, s32[]{:T(128)}) while((s32[]{:T(128)}, f32[4,256,512]{2,1,0:T(8,128)}, s32[]{:T(128)}, f32[16,4,256,256]{3,2,1,0:T(8,128)}, ...), condition=%wide.region_10.13_spmd.clone, body=%wide.region_9.12_spmd.clone.sunk | while | flops 1612709888 | bytes 13634151 | solution.py:32
  916.0 5.5 fusion.811
  923.1 5.4 fusion.811
  937.2 5.5 fusion.811
  951.3 5.4 fusion.811
  965.3 5.5 fusion.811
  979.4 5.4 fusion.811
  1021.9 6.1 multiply_convert_fusion.4
  1027.9 136.3 %all-gather.23.cloned.1.call-done = bf16[2048,2048]{1,0:T(8,128)(2,1)} async-done(((bf16[2048,128]{1,0:T(8,128)(2,1)}), bf16[2048,2048]{1,0:T(8,128)(2,1)}) %all-gather.23.cloned.1.call-update) | async-done | bytes 8388624 | tf_op jit(solution)/shard_map/all_gather | solution.py:210
  1164.3 5.6 fusion.386
  1172.2 15.7 all-reduce.35.cloned.1.call-done
  1190.5 143.9 %all-gather.25.cloned.1.call-done = bf16[2048,2816]{1,0:T(8,128)(2,1)} async-done(((bf16[128,2816]{1,0:T(8,128)(2,1)}), bf16[2048,2816]{1,0:T(8,128)(2,1)}) %all-gather.25.cloned.1.call-update) | async-done | bytes 11534352 | tf_op jit(solution)/shard_map/all_gather | solution.py:211
  1334.3 7.0 fusion.387
  1341.4 136.3 %all-gather.27.cloned.1.call-done = bf16[2048,2816]{1,0:T(8,128)(2,1)} async-done(((bf16[128,2816]{1,0:T(8,128)(2,1)}), bf16[2048,2816]{1,0:T(8,128)(2,1)}) %all-gather.27.cloned.1.call-update) | async-done | bytes 11534352 | tf_op jit(solution)/shard_map/all_gather | solution.py:212
  1477.7 7.1 fusion.388
  1484.8 176.8 %all-gather.29.cloned.1.call-done = bf16[2816,2048]{1,0:T(8,128)(2,1)} async-done(((bf16[2816,128]{1,0:T(8,128)(2,1)}), bf16[2816,2048]{1,0:T(8,128)(2,1)}) %all-gather.29.cloned.1.call-update) | async-done | bytes 11534352 | tf_op jit(solution)/shard_map/all_gather | solution.py:213
  1661.6 10.3 multiply_convert_fusion
  1671.9 8.6 fusion.389
  1685.4 7.3 convolution_convert_fusion.1
  1693.0 10.3 all-reduce.39.cloned.1.call-done
  1705.3 20.8 all-reduce.37.cloned.1.call-done
  1728.9 8.0 fusion.324
  1745.6 18.0 copy.484
  1763.5 11.7 rev.7
  1782.8 7.3 fusion.393
  1790.1 305.9 %all-gather.35.cloned.1.call-done = f32[64,256,512]{2,1,0:T(8,128)} async-done(((f32[4,256,512]{2,1,0:T(8,128)}), f32[64,256,512]{2,1,0:T(8,128)}) %all-gather.35.cloned.1.call-update) | async-done | bytes 33554448 | tf_op jit(solution)/shard_map/all_gather | solution.py:20
  2096.0 22.9 rev.6
  2118.9 99.3 %while.111 = (s32[]{:T(128)}, f32[4,256,512]{2,1,0:T(8,128)S(1)}, s32[]{:T(128)}, f32[16,4,256,512]{3,2,1,0:T(8,128)}, f32[16,4,256,256]{2,3,1,0:T(8,128)}, /*index=5*/s32[]{:T(128)}, s32[]{:T(128)}) while((s32[]{:T(128)}, f32[4,256,512]{2,1,0:T(8,128)S(1)}, s32[]{:T(128)}, f32[16,4,256,512]{3,2,1,0:T(8,128)}, ...), condition=%wide.region_19.22_spmd.clone, body=%wide.region_18.21_spmd.clone.sunk | while | flops 1612709888 | bytes 13634151 | solution.py:32
  2226.9 153.1 %while.107 = (s32[]{:T(128)}, f32[4,256,512]{2,1,0:T(8,128)S(1)}, f32[2,64,4,256]{3,1,0,2:T(8,128)}, f32[2,64,4,256]{3,1,0,2:T(8,128)}, f32[2,64,4,512]{3,2,1,0:...) while((s32[]{:T(128)}, f32[4,256,512]{2,1,0:T(8,128)S(1)}, ...), condition=%wide.region_41.45_spmd, body=%wide.region_31.44_spmd.sunk | while | flops 4046188800 | bytes 118335152 | solution.py:102
  2244.9 21.0 custom-call.49
  2321.2 21.0 custom-call.49
  2382.9 107.4 %while.106 = (s32[]{:T(128)}, f32[4,256,256]{2,1,0:T(8,128)}, f32[2,64,4,256]{3,1,0,2:T(8,128)}, f32[2,64,4,256]{3,1,0,2:T(8,128)}, f32[2,64,4]{1,2,0:T(4,128)},...) while((s32[]{:T(128)}, f32[4,256,256]{2,1,0:T(8,128)}, ...), condition=%wide.region_30.34_spmd, body=%wide.region_20.33_spmd.sunk | while | flops 2181034240 | bytes 53573988 | solution.py:102
  2391.0 20.3 custom-call.48
  2444.6 20.3 custom-call.48
  2513.6 6.4 fusion.318
  2530.2 8.2 fusion.352
  2539.8 8.3 fusion.319
  2549.4 9.4 fusion.394
  2559.9 9.4 fusion.395
  2570.6 9.3 fusion.396
  2598.6 8.2 fusion.317
  2606.8 21.2 reduce-scatter.31.cloned.1.call-done
  2629.5 74.8 %reduce-scatter.33.cloned.1.call-done = f32[128,4]{1,0:T(8,128)} async-done(((f32[2048,4]{1,0:T(8,128)}), f32[128,4]{1,0:T(8,128)}) %reduce-scatter.33.cloned.1.call-update) | async-done | bytes 2064
  2707.0 343.0 %reduce-scatter.21.cloned.1.call-done = f32[128,2048]{1,0:T(8,128)} async-done(((f32[2048,2048]{1,0:T(8,128)}), f32[128,2048]{1,0:T(8,128)}) %reduce-scatter.21.cloned.1.call-update) | async-done | bytes 1048592 | tf_op jit(solution)/shard_map/reduce_scatter | solution.py:413
  3050.0 354.9 %reduce-scatter.23.cloned.1.call-done = f32[2048,128]{1,0:T(8,128)} async-done(((f32[2048,2048]{1,0:T(8,128)}), f32[2048,128]{1,0:T(8,128)}) %reduce-scatter.23.cloned.1.call-update) | async-done | bytes 1048592 | tf_op jit(solution)/shard_map/reduce_scatter | solution.py:416
  3404.9 481.4 %reduce-scatter.25.cloned.1.call-done = f32[128,2816]{1,0:T(8,128)} async-done(((f32[2048,2816]{1,0:T(8,128)}), f32[128,2816]{1,0:T(8,128)}) %reduce-scatter.25.cloned.1.call-update) | async-done | bytes 1441808 | tf_op jit(solution)/shard_map/reduce_scatter | solution.py:417
  3886.3 482.7 %reduce-scatter.27.cloned.1.call-done = f32[128,2816]{1,0:T(8,128)} async-done(((f32[2048,2816]{1,0:T(8,128)}), f32[128,2816]{1,0:T(8,128)}) %reduce-scatter.27.cloned.1.call-update) | async-done | bytes 1441808 | tf_op jit(solution)/shard_map/reduce_scatter | solution.py:418
  4368.9 482.7 %reduce-scatter.29.cloned.1.call-done = f32[2816,128]{1,0:T(8,128)} async-done(((f32[2816,2048]{1,0:T(8,128)}), f32[2816,128]{1,0:T(8,128)}) %reduce-scatter.29.cloned.1.call-update) | async-done | bytes 1441808 | tf_op jit(solution)/shard_map/reduce_scatter | solution.py:419
  4851.6 121.2 %all-reduce.43.cloned.1.call-done = (f32[2048]{0:T(1024)}, f32[4,1024]{1,0:T(4,128)}, f32[4,1024]{1,0:T(4,128)}, f32[4,2048]{1,0:T(4,128)}, f32[4]{0:T(128)}, /*index=5*/f32[4]{0:T(128)}, f32[512]{0:T(512)}, f32[2048]{0:T(1024)}) async-done(((f32[2048]{0:T(1024)}, f32[4,1024]{1,0:T(4,128)}, f32[4,1024]{1,0:T(4,128)}, f32[4,2048]{1,0:T(4,128)}, f32[4]{0:T(128)}, /*index=5*/f32[4]{0:T(128)}, f32[512]{0:T(512)}, ...) | async-done | bytes 84016 | tf_op jit(solution)/shard_map/psum | solution.py:421
  4972.9 180.6 %reduce-scatter.15.cloned.1.call-done = f32[128,1024]{1,0:T(8,128)} async-done(((f32[2048,1024]{1,0:T(8,128)}), f32[128,1024]{1,0:T(8,128)}) %reduce-scatter.15.cloned.1.call-update) | async-done | bytes 524304 | tf_op jit(solution)/shard_map/reduce_scatter | solution.py:410
  5153.4 183.1 %reduce-scatter.17.cloned.1.call-done = f32[128,1024]{1,0:T(8,128)} async-done(((f32[2048,1024]{1,0:T(8,128)}), f32[128,1024]{1,0:T(8,128)}) %reduce-scatter.17.cloned.1.call-update) | async-done | bytes 524304 | tf_op jit(solution)/shard_map/reduce_scatter | solution.py:411
  5336.6 351.6 %reduce-scatter.19.cloned.1.call-done = f32[128,2048]{1,0:T(8,128)} async-done(((f32[2048,2048]{1,0:T(8,128)}), f32[128,2048]{1,0:T(8,128)}) %reduce-scatter.19.cloned.1.call-update) | async-done | bytes 1048592 | tf_op jit(solution)/shard_map/reduce_scatter | solution.py:412
  (1139 shorter events, 576.2 us)
Async XLA Ops:
  7.2 87.0 %copy-start.14 = (bf16[128,2048]{1,0:T(8,128)(2,1)S(1)}, bf16[128,2048]{1,0:T(8,128)(2,1)}, u32[]{:S(2)}) copy-start(bf16[128,2048]{1,0:T(8,128)(2,1)} %param.39) | copy-start | bytes 1572868
  7.2 87.0 %copy-start.80 = (f32[2048]{0:T(1024)S(1)}, f32[2048]{0:T(1024)}, u32[]{:S(2)}) copy-start(f32[2048]{0:T(1024)} %param.41) | copy-start | bytes 24580
  7.2 87.0 %copy-start.197 = (f32[4]{0:T(128)S(1)}, f32[4]{0:T(128)}, u32[]{:S(2)}) copy-start(f32[4]{0:T(128)} %param.52) | copy-start | bytes 52
  7.2 87.9 %all-gather.17.cloned.1.call-start = ((), (), s32[]{:S(2)}) async-start(), calls=%async_computation.11 | async-start | bytes 4456448 | tf_op jit(solution)/shard_map/all_gather | solution.py:205
  8.0 159.4 %all-gather.15.cloned.1.call-start = ((), (), s32[]{:S(2)}) async-start(), calls=%async_computation.10 | async-start | bytes 4456448 | tf_op jit(solution)/shard_map/all_gather | solution.py:204
  8.7 272.9 %all-gather.19.cloned.1.call-start = ((), (), s32[]{:S(2)}) async-start(), calls=%async_computation.12 | async-start | bytes 8912896 | tf_op jit(solution)/shard_map/all_gather | solution.py:206
  9.4 546.2 %all-gather.31.cloned.1.call-start = ((), (), s32[]{:S(2)}) async-start(), calls=%async_computation.30 | async-start | bytes 17825792 | tf_op jit(solution)/shard_map/all_gather | solution.py:20
  52.2 45.9 copy-start.145
  88.3 9.8 copy-start.143
  90.3 931.6 %copy-start.131 = (f32[128]{0:T(128)}, f32[128]{0:T(128)S(1)}, u32[]{:S(2)}) copy-start(f32[128]{0:T(128)S(1)} %fusion.339) | copy-start | bytes 1540
  91.0 274.1 %copy-start.169 = (f32[128]{0:T(128)}, f32[128]{0:T(128)S(1)}, u32[]{:S(2)}) copy-start(f32[128]{0:T(128)S(1)} %get-tuple-element.1679) | copy-start | bytes 1540
  91.0 274.1 %copy-start.171 = (f32[128]{0:T(128)}, f32[128]{0:T(128)S(1)}, u32[]{:S(2)}) copy-start(f32[128]{0:T(128)S(1)} %get-tuple-element.1680) | copy-start | bytes 1540
  91.0 274.2 %copy-start.173 = (f32[128]{0:T(128)}, f32[128]{0:T(128)S(1)}, u32[]{:S(2)}) copy-start(f32[128]{0:T(128)S(1)} %get-tuple-element.1681) | copy-start | bytes 1540
  91.0 274.2 %copy-start.175 = (f32[128]{0:T(128)}, f32[128]{0:T(128)S(1)}, u32[]{:S(2)}) copy-start(f32[128]{0:T(128)S(1)} %get-tuple-element.1682) | copy-start | bytes 1540
  91.9 200.4 %copy-start.152 = (f32[1,1024]{1,0:T(1,128)}, f32[1,1024]{1,0:T(1,128)S(1)}, u32[]{:S(2)}) copy-start(f32[1,1024]{1,0:T(1,128)S(1)} %get-tuple-element.1668) | copy-start | bytes 12292
  91.9 200.4 %copy-start.154 = (f32[1,1024]{1,0:T(1,128)}, f32[1,1024]{1,0:T(1,128)S(1)}, u32[]{:S(2)}) copy-start(f32[1,1024]{1,0:T(1,128)S(1)} %get-tuple-element.1669) | copy-start | bytes 12292
  91.9 200.4 %copy-start.156 = (f32[1,1024]{1,0:T(1,128)}, f32[1,1024]{1,0:T(1,128)S(1)}, u32[]{:S(2)}) copy-start(f32[1,1024]{1,0:T(1,128)S(1)} %get-tuple-element.1670) | copy-start | bytes 12292
  91.9 200.4 %copy-start.158 = (f32[1,1024]{1,0:T(1,128)}, f32[1,1024]{1,0:T(1,128)S(1)}, u32[]{:S(2)}) copy-start(f32[1,1024]{1,0:T(1,128)S(1)} %get-tuple-element.1671) | copy-start | bytes 12292
  92.8 202.3 %copy-start.160 = (f32[1,1024]{1,0:T(1,128)}, f32[1,1024]{1,0:T(1,128)S(1)}, u32[]{:S(2)}) copy-start(f32[1,1024]{1,0:T(1,128)S(1)} %get-tuple-element.1664) | copy-start | bytes 12292
  92.8 202.3 %copy-start.162 = (f32[1,1024]{1,0:T(1,128)}, f32[1,1024]{1,0:T(1,128)S(1)}, u32[]{:S(2)}) copy-start(f32[1,1024]{1,0:T(1,128)S(1)} %get-tuple-element.1665) | copy-start | bytes 12292
  92.8 202.3 %copy-start.164 = (f32[1,1024]{1,0:T(1,128)}, f32[1,1024]{1,0:T(1,128)S(1)}, u32[]{:S(2)}) copy-start(f32[1,1024]{1,0:T(1,128)S(1)} %get-tuple-element.1666) | copy-start | bytes 12292
  92.8 202.3 %copy-start.166 = (f32[1,1024]{1,0:T(1,128)}, f32[1,1024]{1,0:T(1,128)S(1)}, u32[]{:S(2)}) copy-start(f32[1,1024]{1,0:T(1,128)S(1)} %get-tuple-element.1667) | copy-start | bytes 12292
  94.2 197.2 %copy-start.181 = (f32[128,4]{0,1:T(4,128)}, f32[128,4]{0,1:T(4,128)S(1)}, u32[]{:S(2)}) copy-start(f32[128,4]{0,1:T(4,128)S(1)} %fusion.293) | copy-start | bytes 6148
  170.3 119.8 %copy-start.194 = (s32[128]{0:T(128)S(1)}, s32[128]{0:T(128)}, u32[]{:S(2)}) copy-start(s32[128]{0:T(128)} %param.40) | copy-start | bytes 1540
  286.3 5.8 collective-permute-start
  298.1 66.8 %copy-start.168 = (f32[4,2048]{1,0:T(4,128)S(1)}, f32[4,2048]{1,0:T(4,128)}, u32[]{:S(2)}) copy-start(f32[4,2048]{1,0:T(4,128)} %param.50) | copy-start | bytes 98308
  364.5 542.8 %all-gather.33.cloned.1.call-start = ((), (), s32[]{:S(2)}) async-start(), calls=%async_computation.31 | async-start | bytes 35651584 | tf_op jit(solution)/shard_map/all_gather | solution.py:20
  450.8 571.1 %all-gather.21.cloned.1.call-start = ((), (), s32[]{:S(2)}) async-start(), calls=%async_computation.13 | async-start | bytes 8912896 | tf_op jit(solution)/shard_map/all_gather | solution.py:207
  451.4 712.9 %all-gather.23.cloned.1.call-start = ((), (), s32[]{:S(2)}) async-start(), calls=%async_computation.14 | async-start | bytes 8912896 | tf_op jit(solution)/shard_map/all_gather | solution.py:210
  452.1 735.7 %all-reduce.35.cloned.1.call-start = ((), (), s32[]{:S(2)}) async-start(), calls=%async_computation.15 | async-start | bytes 2097152 | tf_op jit(solution)/shard_map/psum | solution.py:304
  907.3 105.5 %copy-start.64 = (f32[2,64,4,256]{3,1,0,2:T(8,128)S(1)}, f32[2,64,4,256]{3,1,0,2:T(8,128)}, u32[]{:S(2)}) copy-start(f32[2,64,4,256]{3,1,0,2:T(8,128)} %copy-done.63) | copy-start | bytes 1572868
  1027.9 141.9 %copy-start.72 = (bf16[128,2048]{1,0:T(8,128)(2,1)}, bf16[128,2048]{1,0:T(8,128)(2,1)S(1)}, u32[]{:S(2)}) copy-start(bf16[128,2048]{1,0:T(8,128)(2,1)S(1)} %get-tuple-element.1687) | copy-start | bytes 1572868
  1169.9 164.5 %all-gather.25.cloned.1.call-start = ((), (), s32[]{:S(2)}) async-start(), calls=%async_computation.16 | async-start | bytes 12255232 | tf_op jit(solution)/shard_map/all_gather | solution.py:211
  1170.6 19.7 copy-start.142
  1170.6 307.1 %all-gather.27.cloned.1.call-start = ((), (), s32[]{:S(2)}) async-start(), calls=%async_computation.17 | async-start | bytes 12255232 | tf_op jit(solution)/shard_map/all_gather | solution.py:212
  1171.2 490.3 %all-gather.29.cloned.1.call-start = ((), (), s32[]{:S(2)}) async-start(), calls=%async_computation.18 | async-start | bytes 12255232 | tf_op jit(solution)/shard_map/all_gather | solution.py:213
  1172.0 531.3 %all-reduce.39.cloned.1.call-start = ((), (), s32[]{:S(2)}) async-start(), calls=%async_computation.20 | async-start | bytes 2097152 | tf_op jit(solution)/shard_map/psum | solution.py:339
  1190.5 287.3 %copy-start.45 = (bf16[128,2048]{1,0:T(8,128)(2,1)}, bf16[128,2048]{1,0:T(8,128)(2,1)S(1)}, u32[]{:S(2)}) copy-start(bf16[128,2048]{1,0:T(8,128)(2,1)S(1)} %multiply_convert_fusion.3) | copy-start | bytes 1572868
  1341.4 320.2 %copy-start.104 = (bf16[128,2048]{1,0:T(8,128)(2,1)S(1)}, bf16[128,2048]{1,0:T(8,128)(2,1)}, u32[]{:S(2)}) copy-start(bf16[128,2048]{1,0:T(8,128)(2,1)} %param.59) | copy-start | bytes 1572868
  1661.6 18.9 slice-start
  1661.6 18.9 slice-start.1
  1671.9 8.7 slice-start.2
  1685.3 40.8 all-reduce.37.cloned.1.call-start
  1685.4 17.9 copy-start.51
  1692.7 403.3 %all-gather.35.cloned.1.call-start = ((), (), s32[]{:S(2)}) async-start(), calls=%async_computation.32 | async-start | bytes 35651584 | tf_op jit(solution)/shard_map/all_gather | solution.py:20
  1743.8 842.2 %all-reduce.41.cloned.1.call-start = ((), (), s32[]{:S(2)}) async-start(), calls=%async_computation.21 | async-start | bytes 2097152 | tf_op jit(solution)/shard_map/psum | solution.py:406
  2390.8 25.1 copy-start.19
  2444.4 25.1 copy-start.19
  2506.1 5.8 collective-permute-start.1
  2508.7 11.3 copy-start.90
  2508.8 12.8 copy-start.88
  2526.5 101.5 %reduce-scatter.31.cloned.1.call-start = ((), (), s32[]{:S(2)}) async-start(), calls=%async_computation.33 | async-start | bytes 1114112
  2528.3 175.9 %reduce-scatter.33.cloned.1.call-start = ((), (), s32[]{:S(2)}) async-start(), calls=%async_computation.34 | async-start | bytes 1114112
  2530.1 519.9 %reduce-scatter.21.cloned.1.call-start = ((), (), s32[]{:S(2)}) async-start(), calls=%async_computation.25 | async-start | bytes 17825792 | tf_op jit(solution)/shard_map/reduce_scatter | solution.py:413
  2538.4 866.4 %reduce-scatter.23.cloned.1.call-start = ((), (), s32[]{:S(2)}) async-start(), calls=%async_computation.26 | async-start | bytes 17825792 | tf_op jit(solution)/shard_map/reduce_scatter | solution.py:416
  2548.1 1338.1 %reduce-scatter.25.cloned.1.call-start = ((), (), s32[]{:S(2)}) async-start(), calls=%async_computation.27 | async-start | bytes 24510464 | tf_op jit(solution)/shard_map/reduce_scatter | solution.py:417
  2558.8 1810.1 %reduce-scatter.27.cloned.1.call-start = ((), (), s32[]{:S(2)}) async-start(), calls=%async_computation.28 | async-start | bytes 24510464 | tf_op jit(solution)/shard_map/reduce_scatter | solution.py:418
  2569.4 2282.3 %reduce-scatter.29.cloned.1.call-start = ((), (), s32[]{:S(2)}) async-start(), calls=%async_computation.29 | async-start | bytes 24510464 | tf_op jit(solution)/shard_map/reduce_scatter | solution.py:419
  2580.0 2392.9 %all-reduce.43.cloned.1.call-start = ((), (), s32[]{:S(2)}) async-start(), calls=%async_computation.35 | async-start | bytes 169984 | tf_op jit(solution)/shard_map/psum | solution.py:421
  2588.3 2565.2 %reduce-scatter.15.cloned.1.call-start = ((), (), s32[]{:S(2)}) async-start(), calls=%async_computation.22 | async-start | bytes 8912896 | tf_op jit(solution)/shard_map/reduce_scatter | solution.py:410
  2593.0 2743.6 %reduce-scatter.17.cloned.1.call-start = ((), (), s32[]{:S(2)}) async-start(), calls=%async_computation.23 | async-start | bytes 8912896 | tf_op jit(solution)/shard_map/reduce_scatter | solution.py:411
  2598.5 3089.6 %reduce-scatter.19.cloned.1.call-start = ((), (), s32[]{:S(2)}) async-start(), calls=%async_computation.24 | async-start | bytes 17825792 | tf_op jit(solution)/shard_map/reduce_scatter | solution.py:412
  2606.8 99.0 %copy-start.193 = (f32[128]{0:T(128)S(1)}, f32[128]{0:T(128)}, u32[]{:S(2)}) copy-start(f32[128]{0:T(128)} %copy-done.192) | copy-start | bytes 1540
  2606.8 99.0 %copy-start.70 = (f32[128,2048]{1,0:T(8,128)S(1)}, f32[128,2048]{1,0:T(8,128)}, u32[]{:S(2)}) copy-start(f32[128,2048]{1,0:T(8,128)} %all-reduce.41.cloned.1.call-done) | copy-start | bytes 3145732
  (252 other events, 670.4 us)
Sparse Core Ops, SparseCore 0:
  10.8 78.8 all-gather.16
  92.5 74.7 all-gather.14
  170.1 111.4 all-gather.18
  364.6 190.9 all-gather.30
  558.2 349.0 all-gather.32
  909.9 111.0 all-gather.20
  1023.7 140.5 all-gather.22
  1170.0 17.7 all-reduce.34
  1191.0 143.3 all-gather.24
  1337.3 140.3 all-gather.26
  1480.8 180.7 all-gather.28
  1685.4 17.7 all-reduce.38
  1706.2 19.9 all-reduce.36
  1743.9 352.0 all-gather.34
  2526.6 19.5 all-reduce.40
  2548.9 79.0 reduce-scatter.30
  2630.2 74.0 reduce-scatter.32
  2707.0 342.9 reduce-scatter.20
  3052.9 351.9 reduce-scatter.22
  3407.6 478.6 reduce-scatter.24
  3889.1 479.7 reduce-scatter.26
  4371.8 479.7 reduce-scatter.28
  4859.8 113.0 all-reduce.42
  4975.6 177.8 reduce-scatter.14
  5156.3 180.2 reduce-scatter.16
  5339.3 348.7 reduce-scatter.18
where the time goes:
time: 5720 us; the launch traced here: 5710 us
  waiting for transfers between devices  4660 us (81%)
  matrix products  494 us (9%)
  other arithmetic  220 us (4%)
  local copies, waits for them, and re-layouts  218 us (4%)
  blocking collectives  81.9 us (1%)
    all_gather x3, waiting for transfers between devices, prefix(): pieces = jax.tree.map(lambda part: lax.all_gather(part, axis), value)  758 us
    reduce_scatter x1, waiting for transfers between devices, on_device(): lax.psum_scatter(ffn_grads[1], 'seq', scatter_dimension=0, tiled=True)  483 us
    reduce_scatter x1, waiting for transfers between devices, on_device(): lax.psum_scatter(ffn_grads[2], 'seq', scatter_dimension=1, tiled=True)  483 us
    reduce_scatter x1, waiting for transfers between devices, on_device(): lax.psum_scatter(ffn_grads[0], 'seq', scatter_dimension=0, tiled=True)  481 us
    reduce_scatter x1, waiting for transfers between devices, on_device(): lax.psum_scatter(grad_w_out, 'seq', scatter_dimension=1, tiled=True)  355 us
    reduce_scatter x1, waiting for transfers between devices, on_device(): lax.psum_scatter(grad_w_value, 'seq', scatter_dimension=0, tiled=True)  352 us
    reduce_scatter x1, waiting for transfers between devices, on_device(): lax.psum_scatter(grad_w_outgate, 'seq', scatter_dimension=0, tiled=True)  343 us
    reduce_scatter x1, waiting for transfers between devices, on_device(): lax.psum_scatter(grad_w_key, 'seq', scatter_dimension=0, tiled=True)  183 us
  transfers between devices with their start and end apart: 28, of which 24 were waited for; matrix products, arithmetic and copies ran while one was open for 6% of the time, Pallas kernels for 0%

commit v1 on v0

v1 whole, which is shorter than its diff:
```python
import functools

import jax
import jax.numpy as jnp
from jax import lax
from jax.experimental import pallas as pl
from jax.experimental.pallas import tpu as pltpu
from jax.sharding import PartitionSpec as P

highest = lax.Precision.HIGHEST
bf16 = jnp.bfloat16
f32 = jnp.float32


def mm(left, right):
    return jnp.dot(left, right, preferred_element_type=f32)


def mm_nt(left, right):
    return lax.dot_general(left, right, (((1,), (1,)), ((), ())), preferred_element_type=f32)


def mm_tn(left, right):
    return lax.dot_general(left, right, (((0,), (0,)), ((), ())), preferred_element_type=f32)


def exact(spec, *operands):
    return jnp.einsum(spec, *operands, precision=highest)


def gather_tokens(rows):
    return lax.all_gather(rows, ("seq", "head"), axis=0, tiled=True)


def scatter_tokens(partial, rows):
    count, pair = lax.axis_size("seq"), lax.axis_size("head")
    low = partial.astype(bf16).reshape(count, pair, rows, partial.shape[1])
    low = lax.psum_scatter(low, "head", scatter_dimension=1, tiled=False)
    low = lax.psum_scatter(low, "seq", scatter_dimension=0, tiled=False)
    return low.astype(f32)


def cols_to_slices(weight):
    return lax.all_to_all(weight, "seq", split_axis=1, concat_axis=0, tiled=True)


def slices_to_cols(grad):
    return lax.all_to_all(grad, "seq", split_axis=0, concat_axis=1, tiled=True)


def member_groups(members):
    count = lax.axis_size("seq")
    return [[j * members + m for m in range(members)] for j in range(count // members)]


def chunked(array, width):
    return array.reshape((array.shape[0] // width, width) + array.shape[1:])


def split(array):
    high = array.astype(bf16)
    return high, (array - high.astype(f32)).astype(bf16)


def dot(left, right, dims):
    return lax.dot_general(left, right, (dims, ((), ())), preferred_element_type=f32)


NN = ((1,), (0,))
NT = ((1,), (1,))
TN = ((0,), (0,))


def dot2(left, right, dims):
    high, low = split(left)
    return dot(high, right, dims) + dot(low, right, dims)


def dot3(left, right, dims):
    lh, ll = split(left)
    rh, rl = split(right)
    return dot(lh, rh, dims) + (dot(lh, rl, dims) + dot(ll, rh, dims))


def unit_inverse(system, width):
    rows = lax.broadcasted_iota(jnp.int32, (width, width), 0)
    cols = lax.broadcasted_iota(jnp.int32, (width, width), 1)
    inverse = jnp.where(rows == cols, 1.0, 0.0)
    block = 1
    while block < width:
        mask = ((rows // block) % 2 == 1) & (cols // block == rows // block - 1)
        step = jnp.where(mask, system, 0.0)
        if block == 1:
            inverse = inverse - step
        else:
            inverse = inverse - dot3(dot3(inverse, step, NN), inverse, NN)
        block *= 2
    return inverse


CUM, RATE, BEGIN, FIRST = 0, 1, 2, 3


def chunk_masks(width, first):
    rows = lax.broadcasted_iota(jnp.int32, (width, width), 0)
    cols = lax.broadcasted_iota(jnp.int32, (width, width), 1)
    keep = (first <= cols.astype(f32)) & (rows >= cols)
    return keep, keep & (rows > cols)


def forward_kernel(
    group, q_ref, k_ref, v_ref, col_ref, row_ref, out_ref, inv_ref, invk_ref, state_ref, new_ref, carry
):
    @pl.when(pl.program_id(0) == 0)
    def _():
        carry[...] = jnp.zeros_like(carry)

    width = q_ref.shape[1]
    prepared = []
    for i in range(group):
        q, k, v = q_ref[i], k_ref[i], v_ref[i]
        cols, rows = col_ref[i], row_ref[i]
        cum, rate = cols[:, CUM : CUM + 1], cols[:, RATE : RATE + 1]
        begin, first = cols[:, BEGIN : BEGIN + 1], cols[:, FIRST : FIRST + 1]
        keep, strict = chunk_masks(width, first)
        fading = jnp.exp(jnp.where(keep, cum - rows[CUM : CUM + 1], -10000.0))
        key_key = dot(k, k, NT)
        inverse = unit_inverse(jnp.where(strict, rate * key_key * fading, 0.0), width)
        inv_ref[i] = inverse
        scaled = inverse * rows[RATE : RATE + 1]
        inv_v = dot2(scaled, v, NN)
        inv_k = dot2(scaled * rows[BEGIN : BEGIN + 1], k, NN)
        invk_ref[i] = inv_k
        attend = dot(q, k, NT) * fading
        token = lax.broadcasted_iota(jnp.int32, (width, 1), 0).astype(f32)
        last = jnp.exp(
            jnp.where(first[width - 1 :] <= token, cum[width - 1 :] - cum, -10000.0)
        )
        prepared.append((q, k, inv_v, inv_k, attend, begin, last))
    state = carry[...]
    for i in range(group):
        q, k, inv_v, inv_k, attend, begin, last = prepared[i]
        state_ref[i] = state
        new = inv_v - dot3(inv_k, state, NN)
        new_ref[i] = new
        high, low = split(state)
        out_ref[i] = begin * (dot(q, high, NN) + dot(q, low, NN)) + dot3(attend, new, NN)
        high, low = split(last * new)
        state = begin[width - 1 :] * state + (dot(k, high, TN) + dot(k, low, TN))
    carry[...] = state


def backward_kernel(
    group,
    grad_ref,
    q_ref,
    k_ref,
    v_ref,
    col_ref,
    row_ref,
    inv_ref,
    invk_ref,
    state_ref,
    new_ref,
    gq_ref,
    gk_ref,
    gv_ref,
    gcol_ref,
    grow_ref,
    carry,
):
    @pl.when(pl.program_id(0) == 0)
    def _():
        carry[...] = jnp.zeros_like(carry)

    width = q_ref.shape[1]
    prepared = []
    for i in range(group):
        q, k, grad = q_ref[i], k_ref[i], grad_ref[i]
        cols, rows = col_ref[i], row_ref[i]
        cum, rate = cols[:, CUM : CUM + 1], cols[:, RATE : RATE + 1]
        begin, first = cols[:, BEGIN : BEGIN + 1], cols[:, FIRST : FIRST + 1]
        keep, strict = chunk_masks(width, first)
        fading = jnp.exp(jnp.where(keep, cum - rows[CUM : CUM + 1], -10000.0))
        query_key = dot(q, k, NT)
        att_grad = dot3(query_key * fading, grad, TN)
        high, low = split(begin * grad)
        inv_k = invk_ref[i]
        base = (dot(q, high, TN) + dot(q, low, TN)) - dot3(inv_k, att_grad, TN)
        token = lax.broadcasted_iota(jnp.int32, (width, 1), 0).astype(f32)
        last = jnp.exp(
            jnp.where(first[width - 1 :] <= token, cum[width - 1 :] - cum, -10000.0)
        )
        prepared.append((q, k, grad, fading, strict, query_key, att_grad, base, rate, begin, last))
    pull = carry[...]
    chained = [None] * group
    for i in reversed(range(group)):
        q, k, grad, fading, strict, query_key, att_grad, base, rate, begin, last = prepared[i]
        high, low = split(pull)
        back = last * (dot(k, high, NN) + dot(k, low, NN))
        chained[i] = (pull, att_grad + back)
        pull = begin[width - 1 :] * pull + base - dot3(invk_ref[i], back, TN)
    carry[...] = pull
    lanes = lax.broadcasted_iota(jnp.int32, gcol_ref.shape[1:], 1)
    token = lax.broadcasted_iota(jnp.int32, (width, 1), 0)
    for i in range(group):
        q, k, grad, fading, strict, query_key, att_grad, base, rate, begin, last = prepared[i]
        pull, grad_new = chained[i]
        v, state, new = v_ref[i].astype(f32), state_ref[i], new_ref[i]
        grad_rhs = dot3(inv_ref[i], grad_new, TN)
        sh, sl = split(state)
        key_state = dot(k, sh, NN) + dot(k, sl, NN)
        query_state = dot(q, sh, NN) + dot(q, sl, NN)
        inside = v - begin * key_state
        grad_att = dot3(grad, new, NT)
        grad_system = jnp.where(strict, -dot3(grad_rhs, new, NT), 0.0)
        lower_fade = jnp.where(strict, dot(k, k, NT) * fading, 0.0)
        grad_rate = jnp.sum(grad_system * lower_fade, axis=1, keepdims=True) + jnp.sum(
            grad_rhs * inside, axis=1, keepdims=True
        )
        grad_lower = rate * grad_system
        grad_v = rate * grad_rhs
        gv_ref[i] = grad_v
        grad_begin = jnp.sum(grad * query_state - grad_v * key_state, axis=1, keepdims=True)
        qh, ql = split(fading * grad_att)
        kh, kl = split(fading * grad_lower)
        gq_ref[i] = begin * dot3(grad, state, NT) + (dot(qh, k, NN) + dot(ql, k, NN))
        pull_k = dot3(new, pull, NT)
        gk_ref[i] = (
            (dot(qh, q, TN) + dot(ql, q, TN))
            + (dot(kh, k, NN) + dot(kl, k, NN))
            + (dot(kh, k, TN) + dot(kl, k, TN))
            - begin * dot3(grad_v, state, NT)
            + last * pull_k
        )
        grad_last = jnp.sum(jnp.sum(pull * state, axis=1, keepdims=True), axis=0, keepdims=True)
        last_part = last * jnp.sum(pull_k * k.astype(f32), axis=1, keepdims=True)
        faded = grad_att * query_key * fading + grad_lower * lower_fade
        grad_cum = jnp.sum(faded, axis=1, keepdims=True) - last_part + grad_begin * begin
        at_end = jnp.sum(last_part, axis=0, keepdims=True) + grad_last * begin[width - 1 :]
        grad_cum = grad_cum + jnp.where(token == width - 1, at_end, 0.0)
        gcol_ref[i] = jnp.where(lanes == 0, grad_cum, jnp.where(lanes == 1, grad_rate, 0.0))
        grow_ref[i] = jnp.broadcast_to(jnp.sum(faded, axis=0, keepdims=True), grow_ref.shape[1:])


def blocks_of(group, array, order):
    tail = array.shape[1:]
    zeros = (0,) * len(tail)
    return pl.BlockSpec((group,) + tail, lambda i: (order(i),) + zeros)


def chunk_group(chunks):
    return 4 if chunks % 4 == 0 else 1


def shape_of(*dims):
    return jax.ShapeDtypeStruct(dims, f32)


def recurrence_forward(q, k, v, cols, rows):
    chunks, width, key_width = q.shape
    value = v.shape[2]
    group = chunk_group(chunks)
    outs = [
        shape_of(chunks, width, value),
        shape_of(chunks, width, width),
        shape_of(chunks, width, key_width),
        shape_of(chunks, key_width, value),
        shape_of(chunks, width, value),
    ]
    return pl.pallas_call(
        functools.partial(forward_kernel, group),
        grid=(chunks // group,),
        in_specs=[blocks_of(group, a, lambda i: i) for a in (q, k, v, cols, rows)],
        out_specs=[blocks_of(group, a, lambda i: i) for a in outs],
        out_shape=outs,
        scratch_shapes=[pltpu.VMEM((key_width, value), f32)],
        compiler_params=pltpu.CompilerParams(vmem_limit_bytes=48 * 2**20),
        name="delta_forward",
    )(q, k, v, cols, rows)


def recurrence_backward(grad, q, k, v, cols, rows, kept):
    chunks, width, key_width = q.shape
    value = v.shape[2]
    group = chunk_group(chunks)
    steps = chunks // group
    outs = [
        shape_of(chunks, width, key_width),
        shape_of(chunks, width, key_width),
        shape_of(chunks, width, value),
        shape_of(chunks, width, 8),
        shape_of(chunks, 8, width),
    ]
    args = (grad, q, k, v, cols, rows) + tuple(kept)
    return pl.pallas_call(
        functools.partial(backward_kernel, group),
        grid=(steps,),
        in_specs=[blocks_of(group, a, lambda i: steps - 1 - i) for a in args],
        out_specs=[blocks_of(group, a, lambda i: steps - 1 - i) for a in outs],
        out_shape=outs,
        scratch_shapes=[pltpu.VMEM((key_width, value), f32)],
        compiler_params=pltpu.CompilerParams(vmem_limit_bytes=48 * 2**20),
        name="delta_backward",
    )(*args)


def shifted(array, offset):
    if offset == 0:
        return array
    if offset > 0:
        return jnp.pad(array[:-offset], ((offset, 0), (0, 0)))
    return jnp.pad(array[-offset:], ((0, -offset), (0, 0)))


def filtered(pre, taps, valid):
    wide = pre.astype(f32)
    total = taps[0] * wide
    for offset in range(1, taps.shape[0]):
        total = total + taps[offset] * shifted(wide, offset) * valid[offset]
    return total


def filtered_back(grad, pre, taps, valid):
    wide = pre.astype(f32)
    total = taps[0] * grad
    grad_taps = [jnp.sum(grad * wide, axis=0)]
    for offset in range(1, taps.shape[0]):
        part = grad * valid[offset]
        total = total + taps[offset] * shifted(part, -offset)
        grad_taps.append(jnp.sum(part * shifted(wide, offset), axis=0))
    return total, jnp.stack(grad_taps)


def silu_back(grad, z):
    s = jax.nn.sigmoid(z)
    return grad * s * (1.0 + z * (1.0 - s))


def unit_back(grad, conv, inv, scale):
    inner = jnp.sum(grad * conv, axis=1, keepdims=True)
    return scale * (inv * grad - inv * inv * inv * inner * conv)


def norm_back(grad, values, inv, gain):
    normed = values * inv
    e = grad * gain
    return inv * (e - normed * jnp.mean(e * normed, axis=-1, keepdims=True)), jnp.sum(
        grad * normed, axis=0
    )


def on_device(
    stream_in,
    doc_start,
    first_gain,
    w_query,
    w_key,
    w_value,
    w_outgate,
    w_decay,
    w_rate,
    conv_query,
    conv_key,
    conv_value,
    a_log,
    dt_bias,
    out_gain,
    w_out,
    second_gain,
    w_gate,
    w_up,
    w_down,
    cotangent,
):
    count, pair = lax.axis_size("seq"), lax.axis_size("head")
    me, core_id = lax.axis_index("seq"), lax.axis_index("head")
    tok_rows, model = stream_in.shape
    heads = a_log.shape[0]
    members = count // heads
    head_id, member = me // members, me % members
    groups = member_groups(members)
    key_width = w_query.shape[1] // heads
    value_width = w_value.shape[1] // heads
    slice_width = value_width // members
    tokens = tok_rows * count
    rows = tok_rows // pair
    ff_slice = w_gate.shape[1] // count

    def own_rows(array):
        return lax.dynamic_slice_in_dim(array, core_id * rows, rows, 0)

    def pick(array, start, width, axis):
        return lax.dynamic_slice_in_dim(array, start, width, axis)

    s_query = lax.all_gather(
        cols_to_slices(w_query), "seq", axis=1, tiled=True, axis_index_groups=groups
    )
    s_key = lax.all_gather(
        cols_to_slices(w_key), "seq", axis=1, tiled=True, axis_index_groups=groups
    )
    s_value = cols_to_slices(w_value)
    s_outgate = cols_to_slices(w_outgate)
    thin = lax.all_gather(jnp.concatenate([w_decay, w_rate], axis=1), "seq", axis=0, tiled=True)
    s_decay = pick(thin, head_id, 1, 1)
    s_rate = pick(thin, heads + head_id, 1, 1)
    s_mixer = jnp.concatenate([s_query, s_key, s_value, s_outgate, s_decay, s_rate], axis=1)
    s_out = slices_to_cols(w_out)
    s_ffn = jnp.concatenate([cols_to_slices(w_gate), cols_to_slices(w_up)], axis=1)
    s_down = slices_to_cols(w_down)

    stream = own_rows(stream_in).astype(f32)
    inv_one = lax.rsqrt(jnp.mean(stream * stream, axis=-1, keepdims=True) + 1e-6)
    hidden_one = gather_tokens((stream * inv_one * first_gain).astype(bf16))
    cot_rows = own_rows(cotangent)
    cot_all = gather_tokens(cot_rows)
    starts = lax.all_gather(doc_start, "seq", axis=0, tiled=True)
    places = jnp.arange(tokens, dtype=jnp.int32)

    projected = mm(hidden_one, s_mixer)
    bounds = [0, key_width, 2 * key_width, 2 * key_width + slice_width]
    bounds.append(bounds[-1] + slice_width)
    pre_query = projected[:, bounds[0] : bounds[1]].astype(bf16)
    pre_key = projected[:, bounds[1] : bounds[2]].astype(bf16)
    pre_value = projected[:, bounds[2] : bounds[3]].astype(bf16)
    gate_value = projected[:, bounds[3] : bounds[4]]
    decay_raw = projected[:, bounds[4]]
    rate_raw = projected[:, bounds[4] + 1]

    taps_q = pick(conv_query, head_id * key_width, key_width, 1)
    taps_k = pick(conv_key, head_id * key_width, key_width, 1)
    taps_v = pick(conv_value, me * slice_width, slice_width, 1)
    valid = [
        (places - offset >= starts).astype(f32)[:, None] for offset in range(conv_query.shape[0])
    ]
    z_q = filtered(pre_query, taps_q, valid)
    z_k = filtered(pre_key, taps_k, valid)
    z_v = filtered(pre_value, taps_v, valid)
    c_q, c_k, c_v = jax.nn.silu(z_q), jax.nn.silu(z_k), jax.nn.silu(z_v)
    scale = key_width ** (-0.5)
    inv_q = lax.rsqrt(jnp.sum(c_q * c_q, axis=1, keepdims=True) + 1e-6)
    inv_k = lax.rsqrt(jnp.sum(c_k * c_k, axis=1, keepdims=True) + 1e-6)
    q = (c_q * inv_q * scale).astype(bf16)
    k = (c_k * inv_k).astype(bf16)
    v = c_v.astype(bf16)
    rate = jax.nn.sigmoid(rate_raw)
    own_a = -jnp.exp(pick(a_log, head_id, 1, 0))
    soft_in = decay_raw + pick(dt_bias, head_id, 1, 0)
    log_decay = own_a * jax.nn.softplus(soft_in)

    cut = tok_rows
    cum = jnp.cumsum(chunked(log_decay, cut), axis=1)
    chunk_begin = jnp.arange(0, tokens, cut, dtype=jnp.int32)[:, None]
    from_before = (chunked(starts, cut) < chunk_begin).astype(f32)
    first = jnp.maximum(chunked(starts, cut) - chunk_begin, 0).astype(f32)
    rows_in = jnp.stack([cum, chunked(rate, cut), jnp.exp(cum) * from_before, first], axis=1)
    rows_in = jnp.concatenate([rows_in, jnp.zeros_like(rows_in)], axis=1)
    cols_in = jnp.swapaxes(rows_in, 1, 2)
    chunks = [chunked(part, cut) for part in (q, k, v)] + [cols_in, rows_in]
    out, *kept = recurrence_forward(*chunks)
    core = out.reshape(tokens, slice_width)

    own_gain = pick(out_gain, member * slice_width, slice_width, 0)
    square = lax.psum(jnp.sum(core * core, axis=1), "seq", axis_index_groups=groups)
    inv_core = lax.rsqrt(square / value_width + 1e-5)[:, None]
    normed_core = core * inv_core
    silu_gate = jax.nn.silu(gate_value)
    gated = (normed_core * own_gain * silu_gate).astype(bf16)

    middle = stream + scatter_tokens(mm(gated, s_out), rows)
    inv_two = lax.rsqrt(jnp.mean(middle * middle, axis=-1, keepdims=True) + 1e-6)
    hidden_two = gather_tokens((middle * inv_two * second_gain).astype(bf16))

    gate_up = mm(hidden_two, s_ffn)
    gate_pre, up_pre = gate_up[:, :ff_slice], gate_up[:, ff_slice:]
    sig = jax.nn.sigmoid(gate_pre)
    silu_pre = gate_pre * sig
    inner = (silu_pre * up_pre).astype(bf16)
    ffn_out = scatter_tokens(mm(inner, s_down), rows)
    output = (middle + ffn_out).astype(bf16)
    grad_inner = mm_nt(cot_all, s_down)
    grad_gate_pre = (grad_inner * up_pre * sig * (1.0 + gate_pre * (1.0 - sig))).astype(bf16)
    grad_up_pre = (grad_inner * silu_pre).astype(bf16)
    grad_gate_up = jnp.concatenate([grad_gate_pre, grad_up_pre], axis=1)
    grad_two = scatter_tokens(mm_nt(grad_gate_up, s_ffn), rows)
    g_down = mm_tn(inner, cot_all)
    g_ffn = mm_tn(hidden_two, grad_gate_up)

    grad_back, grad_second = norm_back(grad_two, middle, inv_two, second_gain)
    grad_middle = cot_rows.astype(f32) + grad_back
    grad_mixer = gather_tokens(grad_middle.astype(bf16))
    g_out = mm_tn(gated, grad_mixer)
    grad_gated = mm_nt(grad_mixer, s_out)

    grad_scaled = grad_gated * silu_gate
    grad_out_gain = jnp.sum(grad_scaled * normed_core, axis=0)
    e = grad_scaled * own_gain
    dots = lax.psum(jnp.sum(e * normed_core, axis=1), "seq", axis_index_groups=groups)
    grad_core = inv_core * (e - normed_core * (dots / value_width)[:, None])
    grad_gate = silu_back(grad_gated * normed_core * own_gain, gate_value).astype(bf16)

    grad_q, grad_k, grad_v, grad_cols, grad_rows = recurrence_backward(
        chunked(grad_core, cut), *chunks, kept
    )
    grad_q = grad_q.reshape(tokens, key_width)
    grad_k = grad_k.reshape(tokens, key_width)
    grad_v = grad_v.reshape(tokens, slice_width)
    grad_cum = grad_cols[:, :, 0] - grad_rows[:, 0]
    grad_log = jnp.cumsum(grad_cum[:, ::-1], axis=1)[:, ::-1].reshape(-1)
    grad_rate_raw = grad_cols[:, :, 1].reshape(-1) * rate * (1.0 - rate)
    grad_a = jnp.sum(grad_log * log_decay)
    grad_decay_raw = grad_log * own_a * jax.nn.sigmoid(soft_in)
    grad_bias = jnp.sum(grad_decay_raw)

    grad_zq = silu_back(unit_back(grad_q, c_q, inv_q, scale), z_q)
    grad_zk = silu_back(unit_back(grad_k, c_k, inv_k, 1.0), z_k)
    grad_zv = silu_back(grad_v, z_v)
    gp_query, g_taps_q = filtered_back(grad_zq, pre_query, taps_q, valid)
    gp_key, g_taps_k = filtered_back(grad_zk, pre_key, taps_k, valid)
    gp_value, g_taps_v = filtered_back(grad_zv, pre_value, taps_v, valid)

    grad_proj = jnp.concatenate(
        [
            gp_query.astype(bf16),
            gp_key.astype(bf16),
            gp_value.astype(bf16),
            grad_gate,
            grad_decay_raw.astype(bf16)[:, None],
            grad_rate_raw.astype(bf16)[:, None],
        ],
        axis=1,
    )
    grad_one = scatter_tokens(mm_nt(grad_proj, s_mixer), rows)
    g_proj = mm_tn(hidden_one, grad_proj[:, : bounds[4]])
    grad_stream, grad_first = norm_back(grad_one, stream, inv_one, first_gain)
    grad_input = grad_middle + grad_stream

    def summed_slices(part):
        part = lax.psum_scatter(
            part.astype(bf16),
            "seq",
            scatter_dimension=1,
            tiled=True,
            axis_index_groups=groups,
        )
        return slices_to_cols(part).astype(f32)

    gw_query = summed_slices(g_proj[:, bounds[0] : bounds[1]])
    gw_key = summed_slices(g_proj[:, bounds[1] : bounds[2]])
    gw_value = slices_to_cols(g_proj[:, bounds[2] : bounds[3]].astype(bf16)).astype(f32)
    gw_outgate = slices_to_cols(g_proj[:, bounds[3] : bounds[4]].astype(bf16)).astype(f32)
    gw_out = cols_to_slices(g_out.astype(bf16)).astype(f32)
    gw_gate = slices_to_cols(g_ffn[:, :ff_slice].astype(bf16)).astype(f32)
    gw_up = slices_to_cols(g_ffn[:, ff_slice:].astype(bf16)).astype(f32)
    gw_down = cols_to_slices(g_down.astype(bf16)).astype(f32)

    thin_grads = lax.all_gather(jnp.stack([grad_decay_raw, grad_rate_raw]), "seq")
    thin_grads = jnp.sum(thin_grads.reshape(heads, members, 2, tokens), axis=1)
    own_cols = pick(hidden_one, me * w_decay.shape[0], w_decay.shape[0], 1).astype(f32)
    thin_grads = jnp.einsum("td,hgt->gdh", own_cols, thin_grads, precision=highest)

    def placed(part, start, width, axis):
        shape = list(part.shape)
        shape[axis] = width
        return lax.dynamic_update_slice_in_dim(jnp.zeros(shape, f32), part, start, axis)

    small = lax.psum(
        (
            placed(g_taps_q, head_id * key_width, conv_query.shape[1], 1),
            placed(g_taps_k, head_id * key_width, conv_key.shape[1], 1),
            placed(g_taps_v, me * slice_width, conv_value.shape[1], 1),
            placed(grad_a[None], head_id, heads, 0),
            placed(grad_bias[None], head_id, heads, 0),
        ),
        "seq",
    )
    gains = lax.psum(
        (
            grad_first,
            grad_second,
            placed(grad_out_gain, member * slice_width, value_width, 0),
        ),
        ("seq", "head"),
    )
    return (
        lax.all_gather(output, "head", axis=0, tiled=True),
        lax.all_gather(grad_input, "head", axis=0, tiled=True),
        gains[0],
        gw_query,
        gw_key,
        gw_value,
        gw_outgate,
        thin_grads[0],
        thin_grads[1],
        small[0],
        small[1],
        small[2],
        small[3],
        small[4],
        gains[2],
        gw_out,
        gains[1],
        gw_gate,
        gw_up,
        gw_down,
    )


def solution(mesh):
    in_specs = (
        P("seq", None),
        P("seq"),
        P(),
        P("seq", "head"),
        P("seq", "head"),
        P("seq", "head"),
        P("seq", "head"),
        P("seq", "head"),
        P("seq", "head"),
        P(None, "head"),
        P(None, "head"),
        P(None, "head"),
        P("head"),
        P("head"),
        P(),
        P("head", "seq"),
        P(),
        P("seq", "head"),
        P("seq", "head"),
        P("head", "seq"),
        P("seq", None),
    )
    out_specs = (
        P("seq", None),
        P("seq", None),
        P(),
        P("seq", "head"),
        P("seq", "head"),
        P("seq", "head"),
        P("seq", "head"),
        P("seq", "head"),
        P("seq", "head"),
        P(None, "head"),
        P(None, "head"),
        P(None, "head"),
        P("head"),
        P("head"),
        P(),
        P("head", "seq"),
        P(),
        P("seq", "head"),
        P("seq", "head"),
        P("head", "seq"),
    )
    return jax.shard_map(
        on_device, mesh=mesh, in_specs=in_specs, out_specs=out_specs, check_vma=False
    )
```

time: 5720 us -> 1420 us (0.25)
  waiting for transfers between devices: 4660 us -> 729 us
  matrix products: 494 us -> 97.9 us
  other arithmetic: 220 us -> 66 us
  blocking collectives: 81.9 us -> 213 us
  local copies, waits for them, and re-layouts: 218 us -> 148 us
  starting transfers between devices: 7.45 us -> 76.2 us
  Pallas kernels: 0 us -> 66.6 us
    reduce_scatter x8, waiting for transfers between devices: 2860 us -> 334 us  [the longest x4 283 us: scatter_tokens(): low = lax.psum_scatter(low, 'seq', scatter_dimension=0, tiled=False)]
    all_gather x11 -> x7, waiting for transfers between devices: 1530 us -> 186 us  [the longest x4 186 us: gather_tokens(): return lax.all_gather(rows, ('seq', 'head'), axis=0, tiled=True)]
    dot_general x154 -> x13, matrix products: 474 us -> 97.9 us  [the longest x4 37 us: mm_nt(): lax.dot_general(left, right, (((1,), (1,)), ((), ())), preferred_element_...]
    another operation x54 -> x2, other arithmetic: 172 us -> 0.57 us  [the longest x1 0.28 us: on_device(): grad_log = jnp.cumsum(grad_cum[:, ::-1], axis=1)[:, ::-1].reshape(-1)]
    all_to_all x0 -> x14, waiting for transfers between devices: none -> 137 us  [the longest x6 88.8 us: cols_to_slices(): lax.all_to_all(weight, 'seq', split_axis=1, concat_axis=0, tiled=True)]
    psum x5 -> x1, waiting for transfers between devices: 168 us -> 64.6 us  [on_device(): lax.psum((placed(g_taps_q, head_id * key_width, conv_query.shape[1], 1),...]
    unnamed x28 -> x20, waiting for transfers between devices: 101 us -> 7.59 us
    all_to_all x0 -> x14, starting transfers between devices: none -> 74.5 us  [the longest x8 42 us: slices_to_cols(): return lax.all_to_all(grad, 'seq', split_axis=0, concat_axis=1, tiled=True)]
  transfers between devices with their start and end apart: 28 -> 32, of which waited for: 24 -> 20; matrix products, arithmetic and copies ran while one was open for 6% -> 9% of each run, Pallas kernels for 0% -> 0%
where the time goes in v1:
time: 1420 us; the launch traced here: 1410 us
  waiting for transfers between devices  729 us (51%)
  blocking collectives  213 us (15%)
  local copies, waits for them, and re-layouts  148 us (10%)
  matrix products  97.9 us (7%)
  starting transfers between devices  76.2 us (5%)
  Pallas kernels  66.6 us (5%)
  other arithmetic  66 us (5%)
  between operations  16.5 us (1%)
    reduce_scatter x4, waiting for transfers between devices, scatter_tokens(): low = lax.psum_scatter(low, 'seq', scatter_dimension=0, tiled=False)  283 us
    all_gather x4, waiting for transfers between devices, gather_tokens(): return lax.all_gather(rows, ('seq', 'head'), axis=0, tiled=True)  186 us
    all_to_all x6, waiting for transfers between devices, cols_to_slices(): lax.all_to_all(weight, 'seq', split_axis=1, concat_axis=0, tiled=True)  88.8 us
    psum x1, waiting for transfers between devices, on_device(): lax.psum((placed(g_taps_q, head_id * key_width, conv_query.shape[1], 1),...  64.6 us
    reduce_scatter x4, waiting for transfers between devices, scatter_tokens(): low = lax.psum_scatter(low, 'head', scatter_dimension=1, tiled=False)  50.8 us
    all_to_all x8, waiting for transfers between devices, slices_to_cols(): return lax.all_to_all(grad, 'seq', split_axis=0, concat_axis=1, tiled=True)  48.3 us
    all_gather x1, blocking collectives, on_device(): lax.all_gather(jnp.stack([grad_decay_raw, grad_rate_raw]), 'seq')  44 us
    pallas_call x1, Pallas kernels, recurrence_forward(): pl.pallas_call(functools.partial(forward_kernel, group), grid=(chunks //...  42.9 us
  transfers between devices with their start and end apart: 32, of which 20 were waited for; matrix products, arithmetic and copies ran while one was open for 9% of the time, Pallas kernels for 0%

profile of v1, /device:TPU:0, one launch (start us, length us, event | category | flops | bytes accessed | tf_op | source)
XLA Modules:
  0.0 1413.4 jit_solution(7673108105522851771)
XLA Ops:
  8.4 18.0 %all_to_all.256 = bf16[128,16,64]{0,2,1:T(8,128)(2,1)S(1)} all-to-all(bf16[128,16,64]{0,2,1:T(8,128)(2,1)S(1)} %bitcast.313), channel_id=1, replica_groups=mesh['seq'=16,'head'=2] {'seq'}, dimensions={1} | all-to-all | bytes 524288 | tf_op jit(solution)/shard_map/all_to_all | solution.py:44
  28.4 12.6 all_to_all.257
  43.0 3.7 all-to-all-start.4
  47.6 13.4 all-to-all-done.4
  61.1 3.8 all-to-all-start.2
  68.6 40.7 %all-gather.1 = s32[16,1,128]{2,1,0:T(1,128)S(1)} all-gather(s32[1,1,128]{2,1,0:T(1,128)S(1)} %bitcast.360), channel_id=1, replica_groups=mesh['seq'=16,'head'=2] {'seq'}, dimensions={0}, use_global_device_ids=true | all-gather | bytes 8704 | tf_op jit(solution)/shard_map/all_gather | solution.py:417
  109.3 36.1 %all_gather.39 = bf16[2048,8]{0,1:T(8,128)(2,1)S(1)} all-gather(bf16[128,8]{0,1:T(8,128)(2,1)S(1)} %pad_maximum_fusion.3), channel_id=1, replica_groups=mesh['seq'=16,'head'=2] {'seq'}, dimensions={0}, use_global_device_ids=true | all-gather | bytes 34816 | tf_op jit(solution)/shard_map/all_gather | solution.py:404
  146.4 3.8 all-to-all-start.3
  152.2 15.3 %all-to-all-done.3 = bf16[128,16,128]{0,2,1:T(8,128)(2,1)S(1)} async-done(((bf16[128,16,128]{0,2,1:T(8,128)(2,1)}), bf16[128,16,128]{0,2,1:T(8,128)(2,1)S(1)}, u32[]{:S(2)}, u32[]{:S(2)}) %all-to-all-start.3) | async-done | bytes 524320 | tf_op jit(solution)/shard_map/all_to_all | solution.py:44
  168.1 13.8 concatenate.22
  181.9 10.2 fusion.59
  199.2 4.5 multiply_convert_fusion.7
  205.0 8.8 multiply_reduce_fusion.10
  221.0 42.9 %delta_forward.1 = (f32[16,128,128]{2,1,0:T(8,128)S(1)}, f32[16,128,128]{2,1,0:T(8,128)S(1)}, f32[16,128,256]{2,1,0:T(8,128)}, f32[16,256,128]{2,1,0:T(8,128)}, f32[16,128,128]{2,1,0:T(8,128)S(1)}) custom-call(bf16[16,128,256]{2,1,0:T(8,128)(2,1)S(1)} %bitcast.253, bf16[16,128,256]{2,1,0:T(8,128)(2,1)S(1)} %bitcast.255, bf16[16,128,128]{2,1,0:T(8,128)(2,1)S(1)} %bitcast.257, ...), custom_call_target="tpu_custom_call" | custom-call | tf_op jit(solution)/shard_map/delta_forward/pallas_call | solution.py:271
  266.3 10.6 psum.70
  281.3 5.7 convolution_convert_fusion.3
  287.0 8.3 copy.260
  295.4 18.5 %reduce-scatter.15.cloned.1.call-done = bf16[16,1,64,2048]{3,2,0,1:T(8,128)(2,1)} async-done(((bf16[16,2,64,2048]{3,2,0,1:T(8,128)(2,1)}), bf16[16,1,64,2048]{3,2,0,1:T(8,128)(2,1)}) %reduce-scatter.15.cloned.1.call-update) | async-done | bytes 4194320 | tf_op jit(solution)/shard_map/reduce_scatter | solution.py:38
  314.0 98.6 %reduce-scatter.17.cloned.1.call-done = bf16[1,64,2048]{2,1,0:T(8,128)(2,1)} async-done(((bf16[16,64,2048]{2,1,0:T(8,128)(2,1)}), bf16[1,64,2048]{2,1,0:T(8,128)(2,1)}) %reduce-scatter.17.cloned.1.call-update) | async-done | bytes 262160 | tf_op jit(solution)/shard_map/reduce_scatter | solution.py:39
  419.5 5.3 all-to-all-start.5
  427.0 21.3 %all-to-all-done.5 = bf16[128,16,176]{0,2,1:T(8,128)(2,1)} async-done(((bf16[128,16,176]{0,2,1:T(8,128)(2,1)}), bf16[128,16,176]{0,2,1:T(8,128)(2,1)}, u32[]{:S(2)}, u32[]{:S(2)}) %all-to-all-start.5) | async-done | bytes 720928 | tf_op jit(solution)/shard_map/all_to_all | solution.py:44
  448.4 4.9 all-to-all-start.6
  455.3 22.7 %all-to-all-done.6 = bf16[128,16,176]{0,2,1:T(8,128)(2,1)} async-done(((bf16[128,16,176]{0,2,1:T(8,128)(2,1)}), bf16[128,16,176]{0,2,1:T(8,128)(2,1)}, u32[]{:S(2)}, u32[]{:S(2)}) %all-to-all-start.6) | async-done | bytes 720928 | tf_op jit(solution)/shard_map/all_to_all | solution.py:44
  478.1 5.1 all-to-all-start.7
  485.5 37.3 %all-gather.17.cloned.1.call-done = bf16[2048,2048]{1,0:T(8,128)(2,1)} async-done(((bf16[64,2048]{1,0:T(8,128)(2,1)}), bf16[2048,2048]{1,0:T(8,128)(2,1)}) %all-gather.17.cloned.1.call-update) | async-done | bytes 8388624 | tf_op jit(solution)/shard_map/all_gather | solution.py:32
  522.7 8.5 fusion.60
  531.2 71.9 %all-gather.19.cloned.1.call-done = bf16[2048,2048]{1,0:T(8,128)(2,1)} async-done(((bf16[64,2048]{1,0:T(8,128)(2,1)}), bf16[2048,2048]{1,0:T(8,128)(2,1)}) %all-gather.19.cloned.1.call-update) | async-done | bytes 8388624 | tf_op jit(solution)/shard_map/all_gather | solution.py:32
  603.1 8.6 multiply_convert_fusion.3
  611.7 6.8 convolution_convert_fusion.1
  618.5 8.3 copy.267
  626.9 15.5 %reduce-scatter.23.cloned.1.call-done = bf16[16,1,64,2048]{3,2,0,1:T(8,128)(2,1)} async-done(((bf16[16,2,64,2048]{3,2,0,1:T(8,128)(2,1)}), bf16[16,1,64,2048]{3,2,0,1:T(8,128)(2,1)}) %reduce-scatter.23.cloned.1.call-update) | async-done | bytes 4194320 | tf_op jit(solution)/shard_map/reduce_scatter | solution.py:38
  642.4 98.6 %reduce-scatter.25.cloned.1.call-done = bf16[1,64,2048]{2,1,0:T(8,128)(2,1)} async-done(((bf16[16,64,2048]{2,1,0:T(8,128)(2,1)}), bf16[1,64,2048]{2,1,0:T(8,128)(2,1)}) %reduce-scatter.25.cloned.1.call-update) | async-done | bytes 262160 | tf_op jit(solution)/shard_map/reduce_scatter | solution.py:39
  744.6 77.2 %all-gather.21.cloned.1.call-done = bf16[2048,2048]{1,0:T(8,128)(2,1)} async-done(((bf16[64,2048]{1,0:T(8,128)(2,1)}), bf16[2048,2048]{1,0:T(8,128)(2,1)}) %all-gather.21.cloned.1.call-update) | async-done | bytes 8388624 | tf_op jit(solution)/shard_map/all_gather | solution.py:32
  821.7 8.1 multiply_reduce_fusion.12
  829.8 9.3 psum.71
  839.1 3.7 multiply_convert_fusion.5
  846.6 23.7 %delta_backward.1 = (f32[16,128,256]{2,1,0:T(8,128)}, f32[16,128,256]{2,1,0:T(8,128)}, f32[16,128,128]{2,1,0:T(8,128)S(1)}, f32[16,128,8]{2,1,0:T(8,128)S(1)}, f32[16,8,128]{2,1,0:T(8,128)S(1)}) custom-call(f32[16,128,128]{2,1,0:T(8,128)S(1)} %bitcast.260, bf16[16,128,256]{2,1,0:T(8,128)(2,1)S(1)} %bitcast.254, bf16[16,128,256]{2,1,0:T(8,128)(2,1)S(1)} %bitcast.256, ...), custom_call_target="tpu_custom_call" | custom-call | tf_op jit(solution)/shard_map/delta_backward/pallas_call | solution.py:296
  910.9 10.7 concatenate.26
  921.6 13.6 convolution_convert_fusion
  935.2 8.3 copy.276
  943.7 7.9 convolution_convert_fusion.2
  951.6 10.1 copy.266
  962.6 16.8 %reduce-scatter.19.cloned.1.call-done = bf16[16,1,64,2048]{3,2,0,1:T(8,128)(2,1)} async-done(((bf16[16,2,64,2048]{3,2,0,1:T(8,128)(2,1)}), bf16[16,1,64,2048]{3,2,0,1:T(8,128)(2,1)}) %reduce-scatter.19.cloned.1.call-update) | async-done | bytes 4194320 | tf_op jit(solution)/shard_map/reduce_scatter | solution.py:38
  979.4 5.4 fusion.10
  985.8 6.6 convolution_convert_fusion.5
  994.4 6.9 all-to-all-start.14
  1001.3 10.5 convolution_convert_fusion.4
  1011.7 13.4 all-to-all-done.14
  1025.1 7.3 all-to-all-start.15
  1038.0 17.4 %all-to-all-done.15 = bf16[176,16,128]{2,0,1:T(8,128)(2,1)} async-done(((bf16[176,16,128]{2,0,1:T(8,128)(2,1)}), bf16[176,16,128]{2,0,1:T(8,128)(2,1)}, u32[]{:S(2)}, u32[]{:S(2)}) %all-to-all-start.15) | async-done | bytes 720928 | tf_op jit(solution)/shard_map/all_to_all | solution.py:44
  1055.4 8.5 all-to-all-start.13
  1065.4 4.7 fusion.11
  1071.1 16.9 %all-to-all-done.13 = bf16[16,128,176]{1,2,0:T(8,128)(2,1)S(1)} async-done(((bf16[16,128,176]{1,2,0:T(8,128)(2,1)}), bf16[16,128,176]{1,2,0:T(8,128)(2,1)S(1)}, u32[]{:S(2)}, u32[]{:S(2)}) %all-to-all-start.13) | async-done | bytes 720928 | tf_op jit(solution)/shard_map/all_to_all | solution.py:48
  1088.0 7.4 all-to-all-start.12
  1097.6 12.0 all-to-all-done.12
  1109.7 4.2 all-to-all-start.10
  1122.1 85.8 %reduce-scatter.21.cloned.1.call-done = bf16[1,64,2048]{2,1,0:T(8,128)(2,1)} async-done(((bf16[16,64,2048]{2,1,0:T(8,128)(2,1)}), bf16[1,64,2048]{2,1,0:T(8,128)(2,1)}) %reduce-scatter.21.cloned.1.call-update) | async-done | bytes 262160 | tf_op jit(solution)/shard_map/reduce_scatter | solution.py:39
  1210.2 5.0 all-to-all-start.11
  1215.2 44.0 %all-gather.2 = f32[16,2,2048]{2,1,0:T(2,128)S(1)} all-gather(f32[1,2,2048]{2,1,0:T(2,128)S(1)} %maximum_bitcast_fusion), channel_id=2, replica_groups=mesh['seq'=16,'head'=2] {'seq'}, dimensions={0}, use_global_device_ids=true | all-gather | bytes 278528 | tf_op jit(solution)/shard_map/all_gather | solution.py:557
  1269.5 6.6 reduce-scatter.31.cloned.1.call-done
  1278.3 5.1 all-to-all-start.8
  1288.7 4.6 all-to-all-done.8
  1296.5 39.3 %all-reduce.18 = (f32[2048]{0:T(1024)}, f32[512]{0:T(512)}, f32[2048]{0:T(1024)}) all-reduce(f32[2048]{0:T(1024)S(1)} %get-tuple-element.146, f32[512]{0:T(512)S(1)} %dynamic_update_slice.23, f32[2048]{0:T(1024)S(1)} %get-tuple-element.144), channel_id=1, replica_groups=mesh['seq'=16,'head'=2] {'seq','head'}, use_global_device_ids=true, to_apply=%region_23.24 | all-reduce | flops 4608 | bytes 36864 | tf_op jit(solution)/shard_map/psum | solution.py:577
  1335.8 64.6 %all-reduce.22.cloned.1.call-done = (f32[4,1024]{1,0:T(4,128)}, f32[4,1024]{1,0:T(4,128)}, f32[4,2048]{1,0:T(4,128)}, f32[4]{0:T(128)}, f32[4]{0:T(128)}) async-done(((f32[4,1024]{1,0:T(4,128)}, f32[4,1024]{1,0:T(4,128)}, f32[4,2048]{1,0:T(4,128)}, f32[4]{0:T(128)}, f32[4]{0:T(128)}), (f32[4,1024]{1,0:T(4,128)}, f32[4,1024]{1,0:T(4,128)}, f32[4,2048]{1,0:T(4,128)}, f32[4]{0:T(128)}, ...) | async-done | bytes 65584 | tf_op jit(solution)/shard_map/psum | solution.py:567
  (323 shorter events, 147.5 us)
Async XLA Ops:
  7.2 138.3 %copy-start = (f32[4,2048]{1,0:T(4,128)S(1)}, f32[4,2048]{1,0:T(4,128)}, u32[]{:S(2)}) copy-start(f32[4,2048]{1,0:T(4,128)} %param.32) | copy-start | bytes 98308
  7.2 34.6 %copy-start.26 = (bf16[128,2048]{1,0:T(8,128)(2,1)S(1)}, bf16[128,2048]{1,0:T(8,128)(2,1)}, u32[]{:S(2)}) copy-start(bf16[128,2048]{1,0:T(8,128)(2,1)} %param.21) | copy-start | bytes 1572868
  7.2 34.8 %copy-start.42 = (f32[2048]{0:T(1024)S(1)}, f32[2048]{0:T(1024)}, u32[]{:S(2)}) copy-start(f32[2048]{0:T(1024)} %param.23) | copy-start | bytes 24580
  7.2 160.8 %all-gather.13.cloned.1.call-start = ((), (), s32[]{:S(2)}) async-start(), calls=%async_computation.27 | async-start | bytes 1310720 | tf_op jit(solution)/shard_map/all_gather | solution.py:396
  27.2 19.5 %copy-start.37 = (bf16[128,2048]{1,0:T(8,128)(2,1)S(1)}, bf16[128,2048]{1,0:T(8,128)(2,1)}, u32[]{:S(2)}) copy-start(bf16[128,2048]{1,0:T(8,128)(2,1)} %param.26) | copy-start | bytes 1572868
  27.2 140.9 %all-gather.15.cloned.1.call-start = ((), (), s32[]{:S(2)}) async-start(), calls=%async_computation.28 | async-start | bytes 1310720 | tf_op jit(solution)/shard_map/all_gather | solution.py:399
  41.8 140.2 %all-gather.11.cloned.1.call-start = ((), (), s32[]{:S(2)}) async-start(), calls=%async_computation.26 | async-start | bytes 8650752 | tf_op jit(solution)/shard_map/all_gather | solution.py:32
  41.8 23.1 %copy-start.56 = (f32[4]{0:T(128)S(1)}, f32[4]{0:T(128)}, u32[]{:S(2)}) copy-start(f32[4]{0:T(128)} %param.34) | copy-start | bytes 52
  41.8 23.7 %copy-start.57 = (f32[4]{0:T(128)S(1)}, f32[4]{0:T(128)}, u32[]{:S(2)}) copy-start(f32[4]{0:T(128)} %param.33) | copy-start | bytes 52
  41.8 25.0 %copy-start.38 = (bf16[128,2048]{1,0:T(8,128)(2,1)S(1)}, bf16[128,2048]{1,0:T(8,128)(2,1)}, u32[]{:S(2)}) copy-start(bf16[128,2048]{1,0:T(8,128)(2,1)} %param.27) | copy-start | bytes 1572868
  42.9 25.7 %copy-start.55 = (s32[128]{0:T(128)S(1)}, s32[128]{0:T(128)}, u32[]{:S(2)}) copy-start(s32[128]{0:T(128)} %param.22) | copy-start | bytes 1540
  42.9 66.4 %copy-start.51 = (bf16[128,4]{0,1:T(4,128)(2,1)S(1)}, bf16[128,4]{0,1:T(4,128)(2,1)}, u32[]{:S(2)}) copy-start(bf16[128,4]{0,1:T(4,128)(2,1)} %param.29) | copy-start | bytes 3076
  42.9 66.4 %copy-start.52 = (bf16[128,4]{0,1:T(4,128)(2,1)S(1)}, bf16[128,4]{0,1:T(4,128)(2,1)}, u32[]{:S(2)}) copy-start(bf16[128,4]{0,1:T(4,128)(2,1)} %param.28) | copy-start | bytes 3076
  43.0 18.1 %all-to-all-start.4 = ((bf16[16,128,128]{2,1,0:T(8,128)(2,1)}), bf16[16,128,128]{2,1,0:T(8,128)(2,1)S(1)}, u32[]{:S(2)}, u32[]{:S(2)}) async-start(bf16[16,128,128]{2,1,0:T(8,128)(2,1)} %bitcast.35), calls=%async_computation.4 | async-start | bytes 1048576 | tf_op jit(solution)/shard_map/all_to_all | solution.py:48
  61.1 85.3 %all-to-all-start.2 = ((bf16[128,16,128]{0,2,1:T(8,128)(2,1)}), bf16[128,16,128]{0,2,1:T(8,128)(2,1)S(1)}, u32[]{:S(2)}, u32[]{:S(2)}) async-start(bf16[128,16,128]{0,2,1:T(8,128)(2,1)} %bitcast.5), calls=%async_computation.2 | async-start | bytes 1048576 | tf_op jit(solution)/shard_map/all_to_all | solution.py:44
  146.4 21.2 %all-to-all-start.3 = ((bf16[128,16,128]{0,2,1:T(8,128)(2,1)}), bf16[128,16,128]{0,2,1:T(8,128)(2,1)S(1)}, u32[]{:S(2)}, u32[]{:S(2)}) async-start(bf16[128,16,128]{0,2,1:T(8,128)(2,1)} %bitcast.8), calls=%async_computation.3 | async-start | bytes 1048576 | tf_op jit(solution)/shard_map/all_to_all | solution.py:44
  150.2 163.7 %reduce-scatter.15.cloned.1.call-start = ((), (), s32[]{:S(2)}) async-start(), calls=%async_computation.29 | async-start | bytes 12582912 | tf_op jit(solution)/shard_map/reduce_scatter | solution.py:38
  192.1 4.5 copy-start.36
  195.8 9.2 copy-start.9
  281.3 5.7 copy-start.24
  295.3 117.2 %reduce-scatter.17.cloned.1.call-start = ((), (), s32[]{:S(2)}) async-start(), calls=%async_computation.30 | async-start | bytes 4456448 | tf_op jit(solution)/shard_map/reduce_scatter | solution.py:39
  313.9 99.8 %copy-start.40 = (f32[2048]{0:T(1024)S(1)}, f32[2048]{0:T(1024)}, u32[]{:S(2)}) copy-start(f32[2048]{0:T(1024)} %param.37) | copy-start | bytes 24580
  313.9 208.8 %all-gather.17.cloned.1.call-start = ((), (), s32[]{:S(2)}) async-start(), calls=%async_computation.31 | async-start | bytes 8650752 | tf_op jit(solution)/shard_map/all_gather | solution.py:32
  415.5 187.6 %all-gather.19.cloned.1.call-start = ((), (), s32[]{:S(2)}) async-start(), calls=%async_computation.34 | async-start | bytes 8650752 | tf_op jit(solution)/shard_map/all_gather | solution.py:32
  419.5 28.8 %all-to-all-start.5 = ((bf16[128,16,176]{0,2,1:T(8,128)(2,1)}), bf16[128,16,176]{0,2,1:T(8,128)(2,1)}, u32[]{:S(2)}, u32[]{:S(2)}) async-start(bf16[128,16,176]{0,2,1:T(8,128)(2,1)} %bitcast.297), calls=%async_computation.7 | async-start | bytes 1441792 | tf_op jit(solution)/shard_map/all_to_all | solution.py:44
  448.4 29.7 %all-to-all-start.6 = ((bf16[128,16,176]{0,2,1:T(8,128)(2,1)}), bf16[128,16,176]{0,2,1:T(8,128)(2,1)}, u32[]{:S(2)}, u32[]{:S(2)}) async-start(bf16[128,16,176]{0,2,1:T(8,128)(2,1)} %bitcast.295), calls=%async_computation.8 | async-start | bytes 1441792 | tf_op jit(solution)/shard_map/all_to_all | solution.py:44
  478.1 53.1 %all-to-all-start.7 = ((bf16[16,176,128]{2,1,0:T(8,128)(2,1)}), bf16[16,176,128]{2,1,0:T(8,128)(2,1)}, u32[]{:S(2)}, u32[]{:S(2)}) async-start(bf16[16,176,128]{2,1,0:T(8,128)(2,1)} %bitcast.315), calls=%async_computation.9 | async-start | bytes 1441792 | tf_op jit(solution)/shard_map/all_to_all | solution.py:48
  483.2 159.2 %reduce-scatter.23.cloned.1.call-start = ((), (), s32[]{:S(2)}) async-start(), calls=%async_computation.35 | async-start | bytes 12582912 | tf_op jit(solution)/shard_map/reduce_scatter | solution.py:38
  603.1 8.6 copy-start.39
  611.7 6.8 copy-start.60
  611.7 6.8 copy-start.62
  626.8 114.3 %reduce-scatter.25.cloned.1.call-start = ((), (), s32[]{:S(2)}) async-start(), calls=%async_computation.36 | async-start | bytes 4456448 | tf_op jit(solution)/shard_map/reduce_scatter | solution.py:39
  642.4 179.3 %all-gather.21.cloned.1.call-start = ((), (), s32[]{:S(2)}) async-start(), calls=%async_computation.37 | async-start | bytes 8650752 | tf_op jit(solution)/shard_map/all_gather | solution.py:32
  744.5 217.3 %reduce-scatter.27.cloned.1.call-start = ((), (), s32[]{:S(2)}) async-start(), calls=%async_computation.38 | async-start | bytes 12582912 | tf_op jit(solution)/shard_map/reduce_scatter | solution.py:38
  943.5 35.9 %reduce-scatter.19.cloned.1.call-start = ((), (), s32[]{:S(2)}) async-start(), calls=%async_computation.32 | async-start | bytes 12582912 | tf_op jit(solution)/shard_map/reduce_scatter | solution.py:38
  961.8 159.0 %reduce-scatter.29.cloned.1.call-start = ((), (), s32[]{:S(2)}) async-start(), calls=%async_computation.39 | async-start | bytes 4456448 | tf_op jit(solution)/shard_map/reduce_scatter | solution.py:39
  962.5 245.3 %reduce-scatter.21.cloned.1.call-start = ((), (), s32[]{:S(2)}) async-start(), calls=%async_computation.33 | async-start | bytes 4456448 | tf_op jit(solution)/shard_map/reduce_scatter | solution.py:39
  979.4 6.4 copy-start.61
  979.4 6.4 copy-start.63
  994.4 30.8 %all-to-all-start.14 = ((bf16[16,128,176]{1,2,0:T(8,128)(2,1)}), bf16[16,128,176]{1,2,0:T(8,128)(2,1)}, u32[]{:S(2)}, u32[]{:S(2)}) async-start(bf16[16,128,176]{1,2,0:T(8,128)(2,1)} %bitcast.296), calls=%async_computation.22 | async-start | bytes 1441792 | tf_op jit(solution)/shard_map/all_to_all | solution.py:48
  1025.1 30.3 %all-to-all-start.15 = ((bf16[176,16,128]{2,0,1:T(8,128)(2,1)}), bf16[176,16,128]{2,0,1:T(8,128)(2,1)}, u32[]{:S(2)}, u32[]{:S(2)}) async-start(bf16[176,16,128]{2,0,1:T(8,128)(2,1)} %bitcast.293), calls=%async_computation.23 | async-start | bytes 1441792 | tf_op jit(solution)/shard_map/all_to_all | solution.py:44
  1032.5 226.9 %reduce-scatter.33.cloned.1.call-start = ((), (), s32[]{:S(2)}) async-start(), calls=%async_computation.42 | async-start | bytes 1310720
  1055.4 10.0 copy-start.25
  1055.4 32.5 %all-to-all-start.13 = ((bf16[16,128,176]{1,2,0:T(8,128)(2,1)}), bf16[16,128,176]{1,2,0:T(8,128)(2,1)S(1)}, u32[]{:S(2)}, u32[]{:S(2)}) async-start(bf16[16,128,176]{1,2,0:T(8,128)(2,1)} %bitcast.294), calls=%async_computation.21 | async-start | bytes 1441792 | tf_op jit(solution)/shard_map/all_to_all | solution.py:48
  1063.9 212.2 %reduce-scatter.31.cloned.1.call-start = ((), (), s32[]{:S(2)}) async-start(), calls=%async_computation.41 | async-start | bytes 1310720
  1088.0 21.7 %all-to-all-start.12 = ((bf16[128,16,128]{2,0,1:T(8,128)(2,1)}), bf16[128,16,128]{2,0,1:T(8,128)(2,1)S(1)}, u32[]{:S(2)}, u32[]{:S(2)}) async-start(bf16[128,16,128]{2,0,1:T(8,128)(2,1)} %bitcast.243), calls=%async_computation.20 | async-start | bytes 1048576 | tf_op jit(solution)/shard_map/all_to_all | solution.py:44
  1109.7 4.2 copy-start.31
  1109.7 100.5 %all-to-all-start.10 = ((bf16[16,128,128]{2,1,0:T(8,128)(2,1)}), bf16[16,128,128]{2,1,0:T(8,128)(2,1)}, u32[]{:S(2)}, u32[]{:S(2)}) async-start(bf16[16,128,128]{2,1,0:T(8,128)(2,1)} %bitcast.70), calls=%async_computation.18 | async-start | bytes 1048576 | tf_op jit(solution)/shard_map/all_to_all | solution.py:48
  1113.9 221.8 %all-gather.23.cloned.1.call-start = ((), (), s32[]{:S(2)}) async-start(), calls=%async_computation.40 | async-start | bytes 1572864 | tf_op jit(solution)/shard_map/all_gather | solution.py:587
  1116.8 4.0 copy-start.43
  1116.9 91.0 %copy-start.27 = (bf16[1,64,2048]{2,1,0:T(8,128)(2,1)S(1)}, bf16[1,64,2048]{2,1,0:T(8,128)(2,1)}, u32[]{:S(2)}) copy-start(bf16[1,64,2048]{2,1,0:T(8,128)(2,1)} %reduce-scatter.17.cloned.1.call-done) | copy-start | bytes 786436
  1116.9 91.0 %copy-start.29 = (bf16[1,64,2048]{2,1,0:T(8,128)(2,1)S(1)}, bf16[1,64,2048]{2,1,0:T(8,128)(2,1)}, u32[]{:S(2)}) copy-start(bf16[1,64,2048]{2,1,0:T(8,128)(2,1)} %reduce-scatter.25.cloned.1.call-done) | copy-start | bytes 786436
  1116.9 91.0 %copy-start.35 = (bf16[128,2048]{1,0:T(8,128)(2,1)S(1)}, bf16[128,2048]{1,0:T(8,128)(2,1)}, u32[]{:S(2)}) copy-start(bf16[128,2048]{1,0:T(8,128)(2,1)} %param.41) | copy-start | bytes 1572868
  1120.8 89.4 %copy-start.45 = (f32[4,1024]{1,0:T(4,128)}, f32[4,1024]{1,0:T(4,128)S(1)}, u32[]{:S(2)}) copy-start(f32[4,1024]{1,0:T(4,128)S(1)} %maximum_dynamic-update-slice_fusion.1) | copy-start | bytes 49156
  1210.2 51.3 %all-to-all-start.11 = ((bf16[16,128,128]{2,1,0:T(8,128)(2,1)}), bf16[16,128,128]{2,1,0:T(8,128)(2,1)S(1)}, u32[]{:S(2)}, u32[]{:S(2)}) async-start(bf16[16,128,128]{2,1,0:T(8,128)(2,1)} %bitcast.72), calls=%async_computation.19 | async-start | bytes 1048576 | tf_op jit(solution)/shard_map/all_to_all | solution.py:48
  1215.2 51.7 %copy-start.44 = (f32[4,1024]{1,0:T(4,128)}, f32[4,1024]{1,0:T(4,128)S(1)}, u32[]{:S(2)}) copy-start(f32[4,1024]{1,0:T(4,128)S(1)} %maximum_dynamic-update-slice_fusion) | copy-start | bytes 49156
  1261.5 16.8 %all-to-all-start.9 = ((bf16[16,128,64]{1,2,0:T(8,128)(2,1)}), bf16[16,128,64]{1,2,0:T(8,128)(2,1)S(1)}, u32[]{:S(2)}, u32[]{:S(2)}) async-start(bf16[16,128,64]{1,2,0:T(8,128)(2,1)} %copy.280), calls=%async_computation.17 | async-start | bytes 524288 | tf_op jit(solution)/shard_map/all_to_all | solution.py:48
  1265.0 135.3 %all-reduce.22.cloned.1.call-start = ((), (), s32[]{:S(2)}) async-start(), calls=%async_computation.43 | async-start | bytes 133120 | tf_op jit(solution)/shard_map/psum | solution.py:567
  1267.4 17.0 %copy-start.32 = (bf16[128,16,128]{2,0,1:T(8,128)(2,1)S(1)}, bf16[128,16,128]{2,0,1:T(8,128)(2,1)}, u32[]{:S(2)}) copy-start(bf16[128,16,128]{2,0,1:T(8,128)(2,1)} %copy-done.31) | copy-start | bytes 1572868
  1278.3 15.0 %all-to-all-start.8 = ((bf16[16,128,64]{1,2,0:T(8,128)(2,1)}), bf16[16,128,64]{1,2,0:T(8,128)(2,1)S(1)}, u32[]{:S(2)}, u32[]{:S(2)}) async-start(bf16[16,128,64]{1,2,0:T(8,128)(2,1)} %copy.278), calls=%async_computation.16 | async-start | bytes 524288 | tf_op jit(solution)/shard_map/all_to_all | solution.py:48
  1293.3 113.0 %copy-start.1 = (f32[4,2048]{1,0:T(4,128)S(1)}, f32[4,2048]{1,0:T(4,128)}, u32[]{:S(2)}) copy-start(f32[4,2048]{1,0:T(4,128)} %param.32) | copy-start | bytes 98308
  1400.3 4.3 copy-start.46
  1400.4 4.9 copy-start.59
  1400.4 5.4 copy-start.58
  (32 other events, 68.2 us)
Sparse Core Ops, SparseCore 0:
  27.3 31.1 all-gather.12
  60.9 29.5 all-gather.14
  93.9 81.0 all-gather.10
  295.4 18.3 reduce-scatter.14
  316.1 96.3 reduce-scatter.16
  416.3 106.4 all-gather.16
  526.6 76.4 all-gather.18
  626.9 15.3 reduce-scatter.22
  644.7 96.3 reduce-scatter.24
  744.6 77.0 all-gather.20
  943.6 15.3 reduce-scatter.26
  961.9 17.3 reduce-scatter.18
  981.6 121.1 reduce-scatter.28
  1104.9 102.8 reduce-scatter.20
  1211.2 31.8 reduce-scatter.32
  1246.6 29.4 reduce-scatter.30
  1278.1 8.5 all-gather.22
  1293.4 106.8 all-reduce.21

commit v2 on v1

v2 whole, which is shorter than its diff:
```python
import functools

import jax
import jax.numpy as jnp
from jax import lax
from jax.experimental import pallas as pl
from jax.experimental.pallas import tpu as pltpu
from jax.sharding import PartitionSpec as P

bf16 = jnp.bfloat16
f32 = jnp.float32
LANES = 128
VMEM_LIMIT = 56 * 2**20


def mm(left, right):
    return jnp.dot(left, right, preferred_element_type=f32)


def mm_nt(left, right):
    return lax.dot_general(left, right, (((1,), (1,)), ((), ())), preferred_element_type=f32)


def mm_tn(left, right):
    return lax.dot_general(left, right, (((0,), (0,)), ((), ())), preferred_element_type=f32)


def near(count):
    return count == 16


def across(value, offset):
    count = lax.axis_size("seq")
    return lax.ppermute(value, "seq", [(i, i ^ offset) for i in range(count)])


def other_core(value):
    return lax.ppermute(value, "head", [(0, 1), (1, 0)])


def after(value, *others):
    return lax.optimization_barrier((value, others))[0]


ALL, PAIR = (1, 2, 3), (2,)


def block_places():
    count = lax.axis_size("seq")
    blocks = jnp.arange(count, dtype=jnp.int32)
    if not near(count):
        return jnp.concatenate([blocks, jnp.zeros((1,), jnp.int32)])
    apart = blocks ^ lax.axis_index("seq")
    flip = lax.axis_index("head").astype(jnp.int32)
    return jnp.concatenate([(apart % 4) * 4 + apart // 4, flip[None]])


def exchanged(blocks):
    groups = [[4 * z + j for j in range(4)] for z in range(4)]
    return lax.all_to_all(
        blocks, "seq", split_axis=0, concat_axis=0, tiled=True, axis_index_groups=groups
    )


def to_all(value):
    return jnp.broadcast_to(value[None], (4,) + value.shape)


def gather_z(rows, zs=ALL):
    if not near(lax.axis_size("seq")):
        return [rows]
    own = rows[None]
    moved = [across(own, 4 * z) for z in zs], across(own, 1), across(own, 2)
    along_z, x_first, y_first = after(moved)
    return own, along_z, x_first, y_first


def gather_xy(state):
    if not near(lax.axis_size("seq")):
        return state
    own, along_z, x_first, y_first = state
    rest = jnp.concatenate(along_z, axis=0)
    x_rest, y_rest, corner = after((across(rest, 1), across(rest, 2), across(y_first, 1)))
    return own, rest, x_first, x_rest, y_first, y_rest, corner


def gather_corner(sides):
    if not near(lax.axis_size("seq")):
        return sides
    half = sides[1].shape[0] // 2
    x_rest, y_rest = sides[3], sides[5]
    corner = [across(y_rest[:half], 1)] if half else []
    return list(sides) + corner + [across(x_rest[half:], 2)]


def gather_end(parts):
    if not near(lax.axis_size("seq")):
        out = lax.all_gather(lax.all_gather(parts[0], "seq"), "head")
        return out[0], out[1]
    mine = jnp.concatenate(parts, axis=0)
    return mine, other_core(mine)


def scatter_begin(left, right, dims):
    blocks, rows = left[0].shape[:2]
    mine, theirs = (part.reshape(blocks * rows, -1) for part in left)

    def product(part):
        return lax.dot_general(part, right, (dims, ((), ())), preferred_element_type=f32)

    if not near(lax.axis_size("seq")):
        low = jnp.stack([product(mine), product(theirs)]).astype(bf16)
        low = lax.psum_scatter(low.reshape(2, blocks, rows, -1), "head", scatter_dimension=0)
        return low, low
    size = blocks // 2 * rows
    sent = [product(theirs[size * half : size * (half + 1)]).astype(bf16) for half in (0, 1)]
    total = [None, None]
    for half in (1, 0):
        part = product(mine[size * half : size * (half + 1)])
        total[half] = part + other_core(sent[half]).astype(f32)
    half, quarter = size // 2, size // 4
    groups = [total[group // 2][(group % 2) * half :][:half] for group in range(4)]
    return [[part[:quarter], part[quarter:]] for part in groups], sent[0]


def scatter_corner(halves, hold=()):
    if not near(lax.axis_size("seq")):
        return halves, halves
    low = [part.astype(bf16) for part in halves[3]]
    if hold:
        low[0] = after(low[0], *hold)
    mid = low[0].shape[1] // 2
    moved = [None, None]
    for half in (1, 0):
        moved[half] = across(low[half][:, :mid], 1), across(low[half][:, mid:], 2)
    return (halves, moved), low[0]


def scatter_xy(state):
    if not near(lax.axis_size("seq")):
        return state, state
    halves, moved = state
    columns = [None, None]
    for half in (1, 0):
        by_x, by_y = (part.astype(f32) for part in moved[half])
        mid = by_x.shape[1]
        y_part = halves[2][half] + jnp.pad(by_x, ((0, 0), (0, mid)))
        x_part = halves[1][half] + jnp.pad(by_y, ((0, 0), (mid, 0)))
        x_low, y_low = x_part.astype(bf16), y_part.astype(bf16)
        columns[half] = halves[0][half], across(x_low, 1), across(y_low, 2)
    return columns, y_low


def scatter_z(columns, rows, zs=ALL):
    if not near(lax.axis_size("seq")):
        return lax.psum_scatter(columns, "seq", scatter_dimension=0).astype(f32), columns
    summed = [base + x.astype(f32) + y.astype(f32) for base, x, y in columns]
    parts = [part[at : at + rows] for part in summed for at in range(0, part.shape[0], rows)]
    total = parts[0]
    for part, z in reversed(list(zip(parts[1:], zs))):
        low = part.astype(bf16)
        total = total + across(low, 4 * z).astype(f32)
    return total, low


def neighbour_slices(part, axis, cuts):
    if not near(lax.axis_size("seq")):
        return [None] * cuts
    return [across(piece, 4) for piece in jnp.split(part, cuts, axis=axis)]


def with_slices(part, pieces, axis):
    if pieces[0] is None:
        return part
    return jnp.concatenate([part] + pieces, axis=axis)


def neighbour_parts(part, axis, cuts):
    if not near(lax.axis_size("seq")):
        return part, []
    size = part.shape[axis] // 2
    mine, theirs = (lax.slice_in_dim(part, at, at + size, axis=axis) for at in (0, size))
    pieces = jnp.split(theirs.astype(bf16), cuts, axis=axis)
    return mine, [across(piece, 4) for piece in pieces]


def add_parts(mine, pieces, axis):
    if not pieces:
        return mine
    return mine + jnp.concatenate([piece.astype(f32) for piece in pieces], axis=axis)


def as_tiles(array, count):
    rows = array.shape[0] // count
    tiles = array.reshape(count, rows, -1, LANES)
    return jnp.swapaxes(tiles, 1, 2).reshape(count, -1, LANES)


def from_tiles(tiles, rows):
    count = tiles.shape[0]
    tiles = tiles.reshape(count, -1, rows, LANES)
    return jnp.swapaxes(tiles, 1, 2).reshape(count, rows, -1)


def all_to_all(blocks):
    return lax.all_to_all(blocks, "seq", split_axis=0, concat_axis=0, tiled=True)


def in_order(parts, place):
    count = parts[0].shape[0]
    return tuple(jnp.take(part, place[:count], axis=0) for part in parts)


def stream_order(parts, place):
    count, rows = parts[0].shape[:2]
    mine, theirs = in_order(parts, place)
    straight = place[count] == 0
    low, high = jnp.where(straight, mine, theirs), jnp.where(straight, theirs, mine)
    return jnp.concatenate([low, high], axis=1)


def both_halves(rows):
    theirs = other_core(rows)
    first = lax.axis_index("head") == 0
    return jnp.concatenate([jnp.where(first, rows, theirs), jnp.where(first, theirs, rows)], axis=0)


def sum_members(value, members):
    count = lax.axis_size("seq")
    if not near(count):
        groups = [[j * members + m for m in range(members)] for j in range(count // members)]
        return lax.psum(value, "seq", axis_index_groups=groups)
    return value + across(value, 1) + across(value, 2) + across(value, 3)


def sum_stream(value):
    count = lax.axis_size("seq")
    if not near(count):
        return lax.psum(value, "seq")
    for offset in (1, 2, 4, 8):
        value = value + across(value, offset)
    return value


def to_slices(blocks):
    out = lax.all_to_all(blocks, "seq", split_axis=1, concat_axis=0, tiled=True)
    return out.reshape((-1, blocks.shape[2]))


def from_slices(grad, rows):
    blocks = grad.reshape((-1, rows, grad.shape[1]))
    return lax.all_to_all(blocks, "seq", split_axis=0, concat_axis=0, tiled=True)


def widened(array, width, axis):
    pads = [(0, 0)] * array.ndim
    pads[axis] = (0, width - array.shape[axis])
    return jnp.pad(array, pads)


def split(array):
    high = array.astype(bf16)
    return high, (array - high.astype(f32)).astype(bf16)


def dot(left, right, dims):
    return lax.dot_general(left, right, (dims, ((), ())), preferred_element_type=f32)


NN = ((1,), (0,))
NT = ((1,), (1,))
TN = ((0,), (0,))


def dot2(left, right, dims):
    high, low = split(left)
    return dot(high, right, dims) + dot(low, right, dims)


def dot3(left, right, dims):
    lh, ll = split(left)
    rh, rl = split(right)
    return dot(lh, rh, dims) + (dot(lh, rl, dims) + dot(ll, rh, dims))


def exact_sum(selector, array):
    high, low = split(array)
    rest = (array - high.astype(f32) - low.astype(f32)).astype(bf16)
    return dot(selector, high, NN) + dot(selector, low, NN) + dot(selector, rest, NN)


def square_iota(width):
    rows = lax.broadcasted_iota(jnp.int32, (width, width), 0)
    return rows, lax.broadcasted_iota(jnp.int32, (width, width), 1)


def unit_inverses(systems, width):
    rows, cols = square_iota(width)
    inverses = [jnp.where(rows == cols, 1.0, 0.0)] * len(systems)
    block = 1
    while block < width:
        mask = ((rows // block) % 2 == 1) & (cols // block == rows // block - 1)
        steps = [jnp.where(mask, system, 0.0) for system in systems]
        if block > 1:
            steps = [dot3(inverse, step, NN) for inverse, step in zip(inverses, steps)]
            steps = [dot3(step, inverse, NN) for inverse, step in zip(inverses, steps)]
        inverses = [inverse - step for inverse, step in zip(inverses, steps)]
        block *= 2
    return inverses


def in_lanes(width, *columns):
    lanes = lax.broadcasted_iota(jnp.int32, (width, LANES), 1)
    out = jnp.zeros((width, LANES), f32)
    for place, column in enumerate(columns):
        out = jnp.where(lanes == place, column, out)
    return out


def lane(array, place):
    return array[:, place : place + 1]


def as_column(row):
    return lane(jnp.broadcast_to(row, (LANES, LANES)).T, 0)


CUM, RATE, BEGIN, LOG, SOFT = 0, 1, 2, 3, 4


def chunk_masks(width, first):
    rows, cols = square_iota(width)
    keep = (first <= cols.astype(f32)) & (rows >= cols)
    return keep, keep & (rows > cols)


def fade(width, cols, rows, start):
    first = jnp.maximum(start, 0.0)
    keep, strict = chunk_masks(width, first)
    cum = lane(cols, CUM)
    fading = jnp.exp(jnp.where(keep, cum - rows[CUM : CUM + 1], -10000.0))
    token = lax.broadcasted_iota(jnp.int32, (width, 1), 0).astype(f32)
    last = jnp.exp(jnp.where(first[width - 1 :] <= token, cum[width - 1 :] - cum, -10000.0))
    return fading, strict, last


def halves_of(low, high, flip):
    return jnp.where(flip == 0, low, high), jnp.where(flip == 0, high, low)


def whole_chunk(mine_ref, theirs_ref, place, flip):
    return jnp.concatenate(halves_of(mine_ref[place], theirs_ref[place], flip), axis=0)


def silu_back(grad, z):
    s = jax.nn.sigmoid(z)
    return grad * s * (1.0 + z * (1.0 - s))


def forward_kernel(group, key_width, place_ref, *refs):
    mine_refs, theirs_refs, refs = refs[:group], refs[group : 2 * group], refs[2 * group :]
    (start_ref, taps_ref, head_ref, core_ref, square_ref, z_ref, q_ref, k_ref, v_ref, col_ref) = refs[:10]
    inv_ref, invk_ref, state_ref, new_ref, carry, ext = refs[10:]
    step = pl.program_id(0)
    width = core_ref.shape[1]
    wide = z_ref.shape[2]
    flip = place_ref[place_ref.shape[0] - 1]

    @pl.when(step == 0)
    def _():
        carry[...] = jnp.zeros_like(carry)
        ext[...] = jnp.zeros_like(ext)

    ext[0, 0:8] = ext[group - 1, width : width + 8]
    token = lax.broadcasted_iota(jnp.int32, (width, 1), 0).astype(f32)
    rows_id, cols_id = square_iota(width)
    triangle = jnp.where(rows_id >= cols_id, 1.0, 0.0).astype(bf16)
    own_a, bias = head_ref[0:1, 0:1], head_ref[0:1, 1:2]
    prepared = []
    for i in range(group):
        x = whole_chunk(mine_refs[i], theirs_refs[i], 0, flip)
        pre = x[:, :wide].astype(bf16).astype(f32)
        ext[i, 8 : 8 + width] = pre
        if i + 1 < group:
            ext[i + 1, 0:8] = pre[width - 8 :]
        start = start_ref[i][:, 0:1]
        z = taps_ref[0:1] * pre
        for offset in range(1, 4):
            valid = jnp.where(token - offset >= start, 1.0, 0.0)
            z = z + taps_ref[offset : offset + 1] * ext[i, 8 - offset : 8 - offset + width] * valid
        z_ref[i] = z
        conv = z * jax.nn.sigmoid(z)
        cq, ck = conv[:, :key_width], conv[:, key_width : 2 * key_width]
        q = cq * lax.rsqrt(jnp.sum(cq * cq, axis=1, keepdims=True) + 1e-6) * key_width ** (-0.5)
        k = ck * lax.rsqrt(jnp.sum(ck * ck, axis=1, keepdims=True) + 1e-6)
        q, k, v = q.astype(bf16), k.astype(bf16), conv[:, 2 * key_width :].astype(bf16)
        q_ref[i], k_ref[i], v_ref[i] = q, k, v
        soft = lane(x, x.shape[1] - LANES) + bias
        rate = jax.nn.sigmoid(lane(x, x.shape[1] - LANES + 1))
        log_decay = own_a * (jnp.maximum(soft, 0.0) + jnp.log1p(jnp.exp(-jnp.abs(soft))))
        cum = lane(exact_sum(triangle, in_lanes(width, log_decay)), 0)
        begin = jnp.where(start < 0.0, jnp.exp(cum), 0.0)
        cols = in_lanes(width, cum, rate, begin, log_decay, soft)
        col_ref[i] = cols
        rows = cols.T
        fading, strict, last = fade(width, cols, rows, start)
        system = jnp.where(strict, rate * dot(k, k, NT) * fading, 0.0)
        attend = dot(q, k, NT) * fading
        prepared.append((q, k, v, rows, system, attend, begin, last))
    inverses = unit_inverses([part[4] for part in prepared], width)
    solved = []
    for i in range(group):
        q, k, v, rows = prepared[i][:4]
        inv_ref[i] = inverses[i]
        scaled = inverses[i] * rows[RATE : RATE + 1]
        inv_v = dot2(scaled, v, NN)
        inv_k = dot2(scaled * rows[BEGIN : BEGIN + 1], k, NN)
        invk_ref[i] = inv_k
        solved.append((inv_v, inv_k))
    state = carry[...]
    for i in range(group):
        q, k, _, _, _, attend, begin, last = prepared[i]
        inv_v, inv_k = solved[i]
        state_ref[i] = state
        new = inv_v - dot3(inv_k, state, NN)
        new_ref[i] = new
        high, low = split(state)
        core = begin * (dot(q, high, NN) + dot(q, low, NN)) + dot3(attend, new, NN)
        core_ref[i] = core
        squares = jnp.sum(core * core, axis=1, keepdims=True)
        square_ref[pl.ds(step * group + i, 1)] = in_lanes(width, squares).T[0:1]
        high, low = split(last * new)
        state = begin[width - 1 :] * state + (dot(k, high, TN) + dot(k, low, TN))
    carry[...] = state


def gate_kernel(place_ref, core_ref, mine_ref, theirs_ref, inv_ref, gain_ref, out_mine, out_theirs):
    count, width, _ = core_ref.shape
    half = width // 2
    flip = place_ref[count]

    def step(i, _):
        place = place_ref[i]
        inv = as_column(inv_ref[pl.ds(i, 1)])
        gate = whole_chunk(mine_ref, theirs_ref, place, flip)
        gated = core_ref[i] * inv * gain_ref[0:1] * (gate * jax.nn.sigmoid(gate))
        mine, theirs = halves_of(gated[:half], gated[half:], flip)
        out_mine[place] = mine.astype(bf16)
        out_theirs[place] = theirs.astype(bf16)
        return 0

    lax.fori_loop(0, count, step, 0, unroll=4)


def dots_kernel(
    place_ref, grad_mine, grad_theirs, core_ref, mine_ref, theirs_ref, inv_ref, gain_ref, out_ref
):
    count, width, _ = core_ref.shape
    flip = place_ref[count]

    def step(i, _):
        place = place_ref[i]
        inv = as_column(inv_ref[pl.ds(i, 1)])
        gate = whole_chunk(mine_ref, theirs_ref, place, flip)
        grad = whole_chunk(grad_mine, grad_theirs, place, flip)
        e = grad * (gate * jax.nn.sigmoid(gate)) * gain_ref[0:1]
        dots = jnp.sum(e * core_ref[i] * inv, axis=1, keepdims=True)
        out_ref[pl.ds(i, 1)] = in_lanes(width, dots).T[0:1]
        return 0

    lax.fori_loop(0, count, step, 0, unroll=4)


def backward_kernel(group, key_width, value_width, place_ref, *refs):
    placed, refs = refs[: 4 * group], refs[4 * group :]
    mine_refs, theirs_refs = placed[:group], placed[group : 2 * group]
    grad_mine, grad_theirs = placed[2 * group : 3 * group], placed[3 * group :]
    start_ref, taps_ref, head_ref, gain_ref, inv_core_ref, dots_ref = refs[:6]
    core_ref, z_ref, q_ref, k_ref, v_ref, col_ref, inv_ref, invk_ref, state_ref, new_ref = refs[6:16]
    out_mine, out_theirs, sum_ref, thin_ref, carry, ext = refs[16:]
    step = pl.program_id(0)
    width = core_ref.shape[1]
    half = width // 2
    wide = z_ref.shape[2]
    chunks = place_ref.shape[0] - 1
    flip = place_ref[chunks]
    base_chunk = chunks - group * (step + 1)

    @pl.when(step == 0)
    def _():
        carry[...] = jnp.zeros_like(carry)
        ext[...] = jnp.zeros_like(ext)
        sum_ref[...] = jnp.zeros_like(sum_ref)

    for offset in range(3):
        ext[offset, group - 1, width : width + 8] = ext[offset, 0, 0:8]
    own_a = head_ref[0:1, 0:1]
    gain = gain_ref[0:1]
    token = lax.broadcasted_iota(jnp.int32, (width, 1), 0).astype(f32)
    rows_id, cols_id = square_iota(width)
    triangle = jnp.where(rows_id <= cols_id, 1.0, 0.0).astype(bf16)
    every = range(group)
    xs = [whole_chunk(mine_refs[i], theirs_refs[i], 0, flip) for i in every]
    qs, ks = [q_ref[i] for i in every], [k_ref[i] for i in every]
    cols = [col_ref[i] for i in every]
    starts = [start_ref[i][:, 0:1] for i in every]
    rates, begins = [lane(c, RATE) for c in cols], [lane(c, BEGIN) for c in cols]
    fades = [fade(width, cols[i], cols[i].T, starts[i]) for i in every]
    query_key = [dot(qs[i], ks[i], NT) for i in every]
    grads, grad_gates = [], []
    for i in every:
        gate = xs[i][:, wide : wide + LANES]
        grad_gated = whole_chunk(grad_mine[i], grad_theirs[i], 0, flip)
        inv = as_column(inv_core_ref[pl.ds(base_chunk + i, 1)])
        dots = as_column(dots_ref[pl.ds(base_chunk + i, 1)])
        normed = core_ref[i] * inv
        sig = jax.nn.sigmoid(gate)
        scaled = grad_gated * (gate * sig)
        sum_ref[4:5, :LANES] += jnp.sum(scaled * normed, axis=0, keepdims=True)
        grads.append(inv * (scaled * gain - normed * (dots * (1.0 / value_width))))
        grad_gates.append(grad_gated * normed * gain * sig * (1.0 + gate * (1.0 - sig)))
    att_grads = [dot3(query_key[i] * fades[i][0], grads[i], TN) for i in every]
    bases = []
    for i in every:
        high, low = split(begins[i] * grads[i])
        bases.append((dot(qs[i], high, TN) + dot(qs[i], low, TN)) - dot3(invk_ref[i], att_grads[i], TN))
    pull = carry[...]
    pulls, grad_news = [None] * group, [None] * group
    for i in reversed(every):
        high, low = split(pull)
        back = fades[i][2] * (dot(ks[i], high, NN) + dot(ks[i], low, NN))
        pulls[i], grad_news[i] = pull, att_grads[i] + back
        pull = begins[i][width - 1 :] * pull + bases[i] - dot3(invk_ref[i], back, TN)
    carry[...] = pull
    grad_rhs = [dot3(inv_ref[i], grad_news[i], TN) for i in every]
    grad_atts = [dot3(grads[i], new_ref[i], NT) for i in every]
    lower_fades = [jnp.where(fades[i][1], dot(ks[i], ks[i], NT) * fades[i][0], 0.0) for i in every]
    key_states, query_states = [], []
    for i in every:
        high, low = split(state_ref[i])
        key_states.append(dot(ks[i], high, NN) + dot(ks[i], low, NN))
        query_states.append(dot(qs[i], high, NN) + dot(qs[i], low, NN))
    pull_ks = [dot3(new_ref[i], pulls[i], NT) for i in every]
    systems = [jnp.where(fades[i][1], -dot3(grad_rhs[i], new_ref[i], NT), 0.0) for i in every]
    grad_vs = [rates[i] * grad_rhs[i] for i in every]
    grad_qs, grad_ks = [], []
    for i in every:
        q, k, begin, last = qs[i], ks[i], begins[i], fades[i][2]
        qh, ql = split(fades[i][0] * grad_atts[i])
        kh, kl = split(fades[i][0] * rates[i] * systems[i])
        grad_qs.append(begin * dot3(grads[i], state_ref[i], NT) + (dot(qh, k, NN) + dot(ql, k, NN)))
        grad_ks.append(
            (dot(qh, q, TN) + dot(ql, q, TN))
            + (dot(kh, k, NN) + dot(kl, k, NN))
            + (dot(kh, k, TN) + dot(kl, k, TN))
            - begin * dot3(grad_vs[i], state_ref[i], NT)
            + last * pull_ks[i]
        )
    thins = []
    for i in every:
        rate, begin, last = rates[i], begins[i], fades[i][2]
        inside = v_ref[i].astype(f32) - begin * key_states[i]
        grad_rate = jnp.sum(systems[i] * lower_fades[i], axis=1, keepdims=True) + jnp.sum(
            grad_rhs[i] * inside, axis=1, keepdims=True
        )
        grad_begin = jnp.sum(
            grads[i] * query_states[i] - grad_vs[i] * key_states[i], axis=1, keepdims=True
        )
        grad_last = jnp.sum(
            jnp.sum(pulls[i] * state_ref[i], axis=1, keepdims=True), axis=0, keepdims=True
        )
        last_part = last * jnp.sum(pull_ks[i] * ks[i].astype(f32), axis=1, keepdims=True)
        faded = grad_atts[i] * query_key[i] * fades[i][0] + rate * systems[i] * lower_fades[i]
        grad_cum = (
            jnp.sum(faded, axis=1, keepdims=True)
            - as_column(jnp.sum(faded, axis=0, keepdims=True))
            - last_part
            + grad_begin * begin
        )
        at_end = jnp.sum(last_part, axis=0, keepdims=True) + grad_last * begin[width - 1 :]
        grad_cum = grad_cum + jnp.where(token == width - 1, at_end, 0.0)
        grad_log = lane(exact_sum(triangle, in_lanes(width, grad_cum)), 0)
        log_decay, soft = lane(cols[i], LOG), lane(cols[i], SOFT)
        grad_decay = grad_log * own_a * jax.nn.sigmoid(soft)
        thin = in_lanes(width, grad_decay, grad_rate * rate * (1.0 - rate))
        thin_ref[pl.ds(base_chunk + i, 1)] = thin.T[None, 0:8]
        sum_ref[5:6, :LANES] += jnp.sum(
            in_lanes(width, grad_log * log_decay, grad_decay), axis=0, keepdims=True
        )
        thins.append(thin)
    for i in reversed(every):
        z = z_ref[i]
        sig = jax.nn.sigmoid(z)
        conv = z * sig
        cq, ck = conv[:, :key_width], conv[:, key_width : 2 * key_width]
        iq = lax.rsqrt(jnp.sum(cq * cq, axis=1, keepdims=True) + 1e-6)
        ik = lax.rsqrt(jnp.sum(ck * ck, axis=1, keepdims=True) + 1e-6)
        dq = jnp.sum(grad_qs[i] * cq, axis=1, keepdims=True)
        dk = jnp.sum(grad_ks[i] * ck, axis=1, keepdims=True)
        scale = key_width ** (-0.5)
        grad_cq = (scale * iq) * (grad_qs[i] - (iq * iq * dq) * cq)
        grad_ck = ik * (grad_ks[i] - (ik * ik * dk) * ck)
        grad_z = jnp.concatenate([grad_cq, grad_ck, grad_vs[i]], axis=1)
        grad_z = grad_z * sig * (1.0 + z * (1.0 - sig))
        pre = xs[i][:, :wide].astype(bf16).astype(f32)
        grad_pre = taps_ref[0:1] * grad_z
        sum_ref[0:1] += jnp.sum(pre * grad_z, axis=0, keepdims=True)
        for offset in range(1, 4):
            valid = jnp.where(token - offset >= starts[i], 1.0, 0.0)
            part = grad_z * valid
            ext[offset - 1, i, 0:width] = part
            if i > 0:
                ext[offset - 1, i - 1, width : width + 8] = part[0:8]
            moved = ext[offset - 1, i, offset : offset + width]
            grad_pre = grad_pre + taps_ref[offset : offset + 1] * moved
            sum_ref[offset : offset + 1] += jnp.sum(pre * moved, axis=0, keepdims=True)
        out = jnp.concatenate([grad_pre, grad_gates[i], thins[i]], axis=1)
        place = place_ref[base_chunk + i]
        mine, theirs = halves_of(out[:half], out[half:], flip)
        out_mine[place] = mine.astype(bf16)
        out_theirs[place] = theirs.astype(bf16)


def stepped(group, array, order):
    tail = array.shape[1:]
    zeros = (0,) * len(tail)
    return pl.BlockSpec((group,) + tail, lambda i, place: (order(i),) + zeros)


def resident(array):
    zeros = (0,) * len(array.shape)
    return pl.BlockSpec(array.shape, lambda i, place: zeros)


def placed_blocks(group, array, order):
    def spec(c):
        shape = (1,) + array.shape[1:]
        return pl.BlockSpec(shape, lambda i, place: (place[group * order(i) + c], 0, 0))

    return [spec(c) for c in range(group)]


def chunk_group(chunks, most):
    return most if chunks % most == 0 else 1


def shape_of(*dims, dtype=f32):
    return jax.ShapeDtypeStruct(dims, dtype)


def cost(microseconds):
    return pl.CostEstimate(flops=0, bytes_accessed=int(microseconds * 3.6e6), transcendentals=0)


def params():
    return pltpu.CompilerParams(vmem_limit_bytes=VMEM_LIMIT)


def recurrence_forward(place, proj, start, taps, head, key_width):
    mine, theirs = proj
    chunks, width, wide = mine.shape[0], 2 * mine.shape[1], taps.shape[1]
    value = wide - 2 * key_width
    group = chunk_group(chunks, 8)
    outs = [
        shape_of(chunks, width, value),
        shape_of(chunks, width),
        shape_of(chunks, width, wide),
        shape_of(chunks, width, key_width, dtype=bf16),
        shape_of(chunks, width, key_width, dtype=bf16),
        shape_of(chunks, width, value, dtype=bf16),
        shape_of(chunks, width, LANES),
        shape_of(chunks, width, width),
        shape_of(chunks, width, key_width),
        shape_of(chunks, key_width, value),
        shape_of(chunks, width, value),
    ]
    order = lambda i: i
    out_specs = [stepped(group, a, order) for a in outs]
    out_specs[1] = resident(outs[1])
    return pl.pallas_call(
        functools.partial(forward_kernel, group, key_width),
        grid_spec=pltpu.PrefetchScalarGridSpec(
            num_scalar_prefetch=1,
            grid=(chunks // group,),
            in_specs=placed_blocks(group, mine, order)
            + placed_blocks(group, theirs, order)
            + [stepped(group, start, order), resident(taps), resident(head)],
            out_specs=out_specs,
            scratch_shapes=[
                pltpu.VMEM((key_width, value), f32),
                pltpu.VMEM((group, width + 8, wide), f32),
            ],
        ),
        out_shape=outs,
        compiler_params=params(),
        cost_estimate=cost(28.0 * chunks / 16),
        name="delta_forward",
    )(place, *([mine] * group), *([theirs] * group), start, taps, head)


def gate_spec(proj, wide):
    shape = proj.shape[:2] + (LANES,)
    return pl.BlockSpec(shape, lambda i, place: (0, 0, wide // LANES))


def gate_forward(place, core, proj, inv, gain, wide):
    mine, theirs = proj
    out = shape_of(*mine.shape[:2], LANES, dtype=bf16)
    return pl.pallas_call(
        gate_kernel,
        grid_spec=pltpu.PrefetchScalarGridSpec(
            num_scalar_prefetch=1,
            grid=(1,),
            in_specs=[
                resident(core),
                gate_spec(mine, wide),
                gate_spec(theirs, wide),
                resident(inv),
                resident(gain),
            ],
            out_specs=[resident(out), resident(out)],
        ),
        out_shape=[out, out],
        compiler_params=params(),
        cost_estimate=cost(4.0),
        name="gate_forward",
    )(place, core, mine, theirs, inv, gain)


def gate_dots(place, grad, core, proj, inv, gain, wide):
    mine, theirs = proj
    out = shape_of(*core.shape[:2])
    return pl.pallas_call(
        dots_kernel,
        grid_spec=pltpu.PrefetchScalarGridSpec(
            num_scalar_prefetch=1,
            grid=(1,),
            in_specs=[
                resident(grad[0]),
                resident(grad[1]),
                resident(core),
                gate_spec(mine, wide),
                gate_spec(theirs, wide),
                resident(inv),
                resident(gain),
            ],
            out_specs=resident(out),
        ),
        out_shape=out,
        compiler_params=params(),
        cost_estimate=cost(6.0),
        name="gate_dots",
    )(place, grad[0], grad[1], core, mine, theirs, inv, gain)


def recurrence_backward(place, proj, grad, start, taps, head, gain, inv, dots, kept, sizes):
    key_width, value_width = sizes
    chunks, wide = proj[0].shape[0], taps.shape[1]
    width = 2 * proj[0].shape[1]
    value = wide - 2 * key_width
    group = chunk_group(chunks, 2)
    steps = chunks // group
    order = lambda i: steps - 1 - i
    outs = [
        shape_of(*proj[0].shape, dtype=bf16),
        shape_of(*proj[1].shape, dtype=bf16),
        shape_of(8, wide),
        shape_of(chunks, 8, width),
    ]
    return pl.pallas_call(
        functools.partial(backward_kernel, group, key_width, value_width),
        grid_spec=pltpu.PrefetchScalarGridSpec(
            num_scalar_prefetch=1,
            grid=(steps,),
            in_specs=[
                spec for part in (*proj, *grad) for spec in placed_blocks(group, part, order)
            ]
            + [stepped(group, start, order)]
            + [resident(a) for a in (taps, head, gain, inv, dots)]
            + [stepped(group, a, order) for a in kept],
            out_specs=[resident(a) for a in outs],
            scratch_shapes=[
                pltpu.VMEM((key_width, value), f32),
                pltpu.VMEM((3, group, width + 8, wide), f32),
            ],
        ),
        out_shape=outs,
        compiler_params=params(),
        cost_estimate=cost(36.0 * chunks / 16),
        name="delta_backward",
    )(
        place,
        *[part for part in (*proj, *grad) for _ in range(group)],
        start,
        taps,
        head,
        gain,
        inv,
        dots,
        *kept,
    )


def weight_kernel(hidden_mine, hidden_theirs, grad_mine, grad_theirs, weight_ref, pair_ref, rest_ref, sum_ref):
    total = dot(hidden_mine[...], grad_mine[...], TN) + dot(hidden_theirs[...], grad_theirs[...], TN)
    summed = jnp.sum(total * weight_ref[...].astype(f32), axis=1, keepdims=True)
    sum_ref[...] = jnp.broadcast_to(summed, sum_ref.shape)
    low = total.astype(bf16)
    size, tiles = pair_ref.shape[2], pair_ref.shape[0]
    for block in range(pair_ref.shape[1]):
        rows = low[block * size : (block + 1) * size]
        for tile in range(tiles):
            pair_ref[tile, block] = rows[:, tile * LANES : (tile + 1) * LANES]
        for tile in range(rest_ref.shape[1] // size):
            at = (tiles + tile) * LANES
            rest_ref[block, tile * size : (tile + 1) * size] = rows[:, at : at + LANES]


def weight_gradient(hidden, grad, weight, count, tiles, rest):
    tokens, columns = grad[0].shape
    model = weight.shape[0]
    size = model // count
    step = 4 if count % 4 == 0 else 1
    part = pl.BlockSpec((tokens, step * size), lambda i: (0, i))
    whole = pl.BlockSpec((tokens, columns), lambda i: (0, 0))
    return pl.pallas_call(
        weight_kernel,
        grid=(count // step,),
        in_specs=[part, part, whole, whole, pl.BlockSpec((step * size, columns), lambda i: (i, 0))],
        out_specs=[
            pl.BlockSpec((tiles, step, size, LANES), lambda i: (0, i, 0, 0)),
            pl.BlockSpec((step, rest * size, LANES), lambda i: (i, 0, 0)),
            pl.BlockSpec((step * size, LANES), lambda i: (i, 0)),
        ],
        out_shape=[
            shape_of(tiles, count, size, LANES, dtype=bf16),
            shape_of(count, rest * size, LANES, dtype=bf16),
            shape_of(model, LANES),
        ],
        compiler_params=params(),
        cost_estimate=cost(14.0),
        name="weight_gradient",
    )(*hidden, *grad, weight)


def unpack_kernel(heads, back_ref, query_ref, key_ref, value_ref, gate_ref, out_ref):
    size = query_ref.shape[0]
    for device in range(back_ref.shape[0]):
        tiles = [back_ref[device, at : at + size].astype(f32) for at in range(0, 4 * size, size)]
        head, member = device // 4, device % 4
        pair_ref = query_ref if member < 2 else key_ref
        at = (2 * head + member % 2) * LANES
        pair_ref[:, at : at + LANES] = tiles[0]
        at = device * LANES
        value_ref[:, at : at + LANES] = tiles[1]
        gate_ref[:, at : at + LANES] = tiles[2]
        out_ref[at : at + LANES] = tiles[3]


def unpack_mixer(back, heads, shapes):
    return pl.pallas_call(
        functools.partial(unpack_kernel, heads),
        out_shape=[shape_of(*shape) for shape in shapes],
        compiler_params=params(),
        cost_estimate=cost(4.0),
        name="unpack_mixer",
    )(back)


def norm_back(grad, values, inv, gain):
    normed = values * inv
    e = grad * gain
    return inv * (e - normed * jnp.mean(e * normed, axis=-1, keepdims=True))


def on_device(
    stream_in,
    doc_start,
    first_gain,
    w_query,
    w_key,
    w_value,
    w_outgate,
    w_decay,
    w_rate,
    conv_query,
    conv_key,
    conv_value,
    a_log,
    dt_bias,
    out_gain,
    w_out,
    second_gain,
    w_gate,
    w_up,
    w_down,
    cotangent,
):
    count, pair = lax.axis_size("seq"), lax.axis_size("head")
    me, core_id = lax.axis_index("seq"), lax.axis_index("head")
    tok_rows, model = stream_in.shape
    heads = a_log.shape[0]
    members = count // heads
    head_id, member = me // members, me % members
    key_width = w_query.shape[1] // heads
    value_width = w_value.shape[1] // heads
    slice_width = value_width // members
    tokens = tok_rows * count
    rows = tok_rows // pair
    ff_slice = w_gate.shape[1] // count
    ff_full = ff_slice // LANES * LANES
    ff_wide = ff_full + LANES // 2
    ff_pack = 2 * ff_wide
    d_rows = w_query.shape[0]
    wide = 2 * key_width + LANES
    aligned = near(count) and key_width == 2 * LANES and slice_width == LANES and members == 4

    def own_rows(array):
        return lax.dynamic_slice_in_dim(array, core_id * rows, rows, 0)

    def pick(array, start, width, axis):
        return lax.dynamic_slice_in_dim(array, start, width, axis)

    place = block_places()

    stream = own_rows(stream_in).astype(f32)
    inv_one = lax.rsqrt(jnp.mean(stream * stream, axis=-1, keepdims=True) + 1e-6)
    normed_one = (stream * inv_one * first_gain).astype(bf16)
    cot_rows = own_rows(cotangent)
    own_starts = own_rows(doc_start)
    coarse = own_starts // 128
    extra = jnp.concatenate(
        [
            w_decay.reshape(rows, -1),
            w_rate.reshape(rows, -1),
            coarse.astype(bf16)[:, None],
            (own_starts - 128 * coarse).astype(bf16)[:, None],
        ],
        axis=1,
    )
    extended = jnp.concatenate([normed_one, widened(extra, LANES, 1)], axis=1)

    def gate_with_up(gate, up):
        parts = [gate[..., :ff_full], up[..., :ff_full], gate[..., ff_full:], up[..., ff_full:]]
        return jnp.concatenate(parts, axis=-1)

    def gate_and_up(both):
        split, last = both[..., : 2 * ff_full], both[..., 2 * ff_full :]
        gate = jnp.concatenate([split[..., :ff_full], last[..., : LANES // 2]], axis=-1)
        up = jnp.concatenate([split[..., ff_full:], last[..., LANES // 2 :]], axis=-1)
        return gate, up

    packed = gate_with_up(
        widened(w_gate.reshape(d_rows, count, ff_slice), ff_wide, 2),
        widened(w_up.reshape(d_rows, count, ff_slice), ff_wide, 2),
    )
    packed = jnp.swapaxes(packed.reshape(d_rows, count, -1, LANES), 0, 1)
    packed = jnp.concatenate(
        [
            jnp.swapaxes(packed, 1, 2).reshape(count, ff_pack // LANES * d_rows, LANES),
            widened(w_out.reshape(count, slice_width, -1), LANES, 2),
            widened(w_down.reshape(count, ff_slice, -1), LANES, 2),
        ],
        axis=1,
    )
    v_blocks = w_value.reshape(d_rows, count, slice_width)
    o_blocks = w_outgate.reshape(d_rows, count, slice_width)
    if aligned:
        qk = jnp.concatenate(
            [w_query.reshape(d_rows, heads, 2, LANES), w_key.reshape(d_rows, heads, 2, LANES)],
            axis=2,
        ).reshape(d_rows, count, LANES)
        qk = jnp.concatenate([qk, v_blocks, o_blocks], axis=2)
        own, packed, qk = after((gather_z(extended), packed, qk))
        sides = gather_xy(own)
        cot_own = gather_z(after(cot_rows, own[1]), PAIR)
        mixed = to_slices(qk)
        s_parts = list(exchanged(to_all(mixed[:, :LANES]))) + [mixed[:, LANES:]]
    else:
        groups = [[j * members + m for m in range(members)] for j in range(heads)]

        def whole_head(weight):
            part = to_slices(weight.reshape(d_rows, count, -1))
            return lax.all_gather(part, "seq", axis=1, tiled=True, axis_index_groups=groups)

        sides = gather_xy(gather_z(extended))
        cot_own = gather_z(cot_rows, PAIR)
        s_parts = [
            whole_head(w_query),
            whole_head(w_key),
            widened(to_slices(v_blocks), LANES, 1),
            widened(to_slices(o_blocks), LANES, 1),
        ]

    def own_taps(taps):
        return pick(taps, head_id * key_width, key_width, 1)

    taps_v = widened(pick(conv_value, me * slice_width, slice_width, 1), LANES, 1)
    taps = jnp.concatenate([own_taps(conv_query), own_taps(conv_key), taps_v], axis=1)
    taps = widened(taps, 8, 0)
    head = jnp.concatenate([-jnp.exp(pick(a_log, head_id, 1, 0)), pick(dt_bias, head_id, 1, 0)])
    head = jnp.broadcast_to(widened(head, LANES, 0)[None], (8, LANES))
    own_gain = widened(pick(out_gain, member * slice_width, slice_width, 0), LANES, 0)
    own_gain = jnp.broadcast_to(own_gain[None], (8, LANES))

    gathered = gather_end(gather_corner(sides))
    extra = [part[:, :, model:] for part in gathered]
    own_extra = extra[0] if near(count) else jnp.where(core_id == 0, extra[0], extra[1])
    own_extra = jnp.take(own_extra, place[:count], axis=0)
    thin = d_rows * heads // rows
    s_decay = own_extra[:, :, :thin].reshape(model, heads)
    s_rate = own_extra[:, :, thin : 2 * thin].reshape(model, heads)
    marks = [part[:, :, 2 * thin : 2 * thin + 2].astype(f32) for part in extra]
    marks = stream_order(marks, place)
    starts = marks[..., 0] * 128.0 + marks[..., 1]
    starts = starts - (jnp.arange(count, dtype=jnp.int32) * tok_rows).astype(f32)[:, None]
    start_cols = jnp.broadcast_to(starts[:, :, None], (count, tok_rows, 8))
    s_thin = jnp.concatenate([pick(s_decay, head_id, 1, 1), pick(s_rate, head_id, 1, 1)], axis=1)
    s_mixer = jnp.concatenate(s_parts + [widened(s_thin, LANES, 1)], axis=1)
    s_mixer, cot_own = after((s_mixer, cot_own))
    s_longer = widened(s_mixer, model + LANES, 0)

    def blocks(parts):
        return tuple(part.reshape(-1, rows, part.shape[-1]) for part in parts)

    def flat(parts):
        return tuple(part.reshape(-1, part.shape[-1]) for part in parts)

    longer_one = flat(gathered)
    proj = blocks([mm(part, s_longer) for part in longer_one])
    cot_sides = gather_xy(after(cot_own, s_mixer))
    packed = all_to_all(after(packed, s_mixer))
    core, square, *kept = recurrence_forward(place, proj, start_cols, taps, head, key_width)
    core, cot_sides, packed = after((core, cot_sides, packed))
    cot_parts = gather_corner(cot_sides)
    s_out = jnp.swapaxes(packed[:, ff_pack // LANES * d_rows :], 0, 1).reshape(-1, count * LANES)
    if LANES > w_out.shape[1]:
        s_out = jnp.swapaxes(
            packed[:, ff_pack // LANES * d_rows :, : w_out.shape[1]], 0, 1
        ).reshape(-1, model)
    s_down = widened(s_out[slice_width:], ff_wide, 0)
    s_out = widened(s_out[:slice_width], LANES, 0)
    s_ffn = from_tiles(packed[:, : ff_pack // LANES * d_rows], d_rows).reshape(model, -1)
    ffn_parts, down_parts = neighbour_slices(s_ffn, 1, ff_pack // LANES), neighbour_slices(s_down, 0, 1)

    inv_core = lax.rsqrt(sum_members(square, members) / value_width + 1e-5)
    gated = gate_forward(place, core, proj, inv_core, own_gain, wide)
    gated, ffn_parts[0] = after((gated, ffn_parts[0]))
    cot_parts = after(cot_parts, gated)
    partial, _ = scatter_begin(gated, s_out, NN)
    partial, ffn_parts[1:2] = after((partial, ffn_parts[1:2]))
    partial, _ = scatter_corner(partial)
    cot_all = gather_end(cot_parts)
    partial, ffn_parts[2:] = after((partial, ffn_parts[2:]))
    partial, _ = scatter_xy(partial)
    partial, down_parts = after((partial, down_parts))
    s_ffn, s_down = with_slices(s_ffn, ffn_parts, 1), with_slices(s_down, down_parts, 0)
    middle = stream + scatter_z(partial, rows)[0]
    inv_two = lax.rsqrt(jnp.mean(middle * middle, axis=-1, keepdims=True) + 1e-6)
    two_own = gather_z((middle * inv_two * second_gain).astype(bf16), PAIR)
    grad_inner = [mm_nt(part, s_down) for part in flat(cot_all)]
    two_own = after(two_own, grad_inner)
    hidden_two = flat(gather_end(gather_corner(gather_xy(two_own))))

    def feed_forward(hidden, grad):
        both = mm(hidden, s_ffn)
        inner, grads = [], []
        for at in range(0, both.shape[1], ff_pack):
            gate_pre, up_pre = gate_and_up(both[:, at : at + ff_pack])
            own = grad[:, at // 2 : at // 2 + ff_wide]
            sig = jax.nn.sigmoid(gate_pre)
            silu_pre = gate_pre * sig
            inner.append((silu_pre * up_pre).astype(bf16))
            grad_gate_pre = own * up_pre * sig * (1.0 + gate_pre * (1.0 - sig))
            grads.append(gate_with_up(grad_gate_pre.astype(bf16), (own * silu_pre).astype(bf16)))
        return jnp.concatenate(inner, axis=1), jnp.concatenate(grads, axis=1)

    inner, grad_gate_up = zip(*[feed_forward(*pair) for pair in zip(hidden_two, grad_inner)])
    partial, sent = scatter_begin(blocks(grad_gate_up), s_ffn, NT)
    late_two, late_inner, late_gate_up = after((hidden_two, inner, grad_gate_up), sent)
    g_ffn = sum(mm_tn(*pair) for pair in zip(late_two, late_gate_up))
    g_down = sum(mm_tn(*pair) for pair in zip(late_inner, flat(cot_all)))
    g_ffn, ffn_parts = neighbour_parts(g_ffn, 1, ff_pack // LANES)
    g_down, down_parts = neighbour_parts(g_down, 0, 1)
    partial, _ = scatter_corner(partial)
    if ffn_parts:
        partial, ffn_parts[0] = after((partial, ffn_parts[0]))
    partial, _ = scatter_xy(partial)
    if ffn_parts:
        partial, ffn_parts[1] = after((partial, ffn_parts[1]))
    grad_two, _ = scatter_z(partial, rows, PAIR)

    grad_back = norm_back(grad_two, middle, inv_two, second_gain)
    grad_middle = cot_rows.astype(f32) + grad_back
    mixer_own = gather_z(grad_middle.astype(bf16))
    late_inner = after(inner, grad_middle)
    ffn_out, _ = scatter_begin(blocks(late_inner), s_down, NN)
    mixer_sides = gather_xy(after(mixer_own, ffn_out))
    mixer_sides, ffn_parts[2:] = after((mixer_sides, ffn_parts[2:]))
    mixer_parts = gather_corner(mixer_sides)
    g_ffn = add_parts(g_ffn, ffn_parts, 1)
    mixer_parts, down_parts = after((mixer_parts, down_parts))
    g_down = add_parts(g_down, down_parts, 0)
    grad_second = jnp.sum(g_ffn * s_ffn[:, :ff_pack].astype(f32), axis=1) / second_gain
    down_tiles = jnp.swapaxes(
        g_down[:ff_slice].astype(bf16).reshape(ff_slice, count, -1), 0, 1
    )
    g_ffn = jnp.concatenate(
        [as_tiles(g_ffn.astype(bf16), count), widened(down_tiles, LANES, 2)], axis=1
    )
    g_ffn, mixer_parts, grad_second = after((g_ffn, mixer_parts, grad_second))
    grad_mixer = gather_end(mixer_parts)
    g_ffn = all_to_all(g_ffn)
    ffn_out, _ = scatter_corner(after(ffn_out, grad_mixer[0]))
    grad_mixer = flat(grad_mixer)
    grad_gated = blocks([mm_nt(part, s_out) for part in grad_mixer])
    dots = sum_members(gate_dots(place, grad_gated, core, proj, inv_core, own_gain, wide), members)
    g_out = sum(mm_tn(*pair) for pair in zip(flat(gated), grad_mixer))
    dots, ffn_out, g_out = lax.optimization_barrier((dots, ffn_out, g_out))
    ffn_out, _ = scatter_xy(ffn_out)
    *grad_proj, sums, thin_rows = recurrence_backward(
        place,
        proj,
        grad_gated,
        start_cols,
        taps,
        head,
        own_gain,
        inv_core,
        dots,
        [core] + kept,
        (key_width, value_width),
    )
    g_pairs, g_rest, g_sums = weight_gradient(
        longer_one, flat(grad_proj), s_mixer, count, 2 * key_width // LANES, 2
    )
    partial, _ = scatter_begin(after(grad_proj, g_pairs), s_mixer, NT)
    partial, sent = scatter_corner(partial)
    ffn_out, _ = scatter_z(after(ffn_out, sent), rows, PAIR)
    partial, sent_xy = scatter_xy(partial)
    grad_one, sent_z = scatter_z(partial, rows)
    g_ffn, sums, thin_rows, grad_second = after((g_ffn, sums, thin_rows, grad_second), sent_z)
    ffn_out = after(ffn_out, sent_z)
    output = both_halves((middle + ffn_out).astype(bf16))
    ff_rows = ff_pack // LANES * d_rows
    gw_down = g_ffn[:, ff_rows:, : w_down.shape[1]].reshape(w_down.shape).astype(f32)

    def joined(blocks):
        return jnp.swapaxes(blocks, 0, 1).reshape(d_rows, -1).astype(f32)

    gw_gate, gw_up = gate_and_up(from_tiles(g_ffn[:, :ff_rows], d_rows))
    gw_gate, gw_up = joined(gw_gate[..., :ff_slice]), joined(gw_up[..., :ff_slice])

    grad_input = both_halves(grad_middle + norm_back(grad_one, stream, inv_one, first_gain))

    grad_first = after(g_sums, sent_z)[:, 0] / first_gain
    if aligned:
        own = jnp.sum(exchanged(g_pairs.reshape(4, model, LANES)).astype(f32), axis=0)
        out_tiles = jnp.swapaxes(g_out.astype(bf16).reshape(LANES, count, -1), 0, 1)
        own = own.astype(bf16).reshape(count, d_rows, LANES)
        back = all_to_all(jnp.concatenate([own, g_rest, out_tiles], axis=1))
        shapes = [part.shape for part in (w_query, w_key, w_value, w_outgate, w_out)]
        gw_query, gw_key, gw_value, gw_outgate, gw_out = unpack_mixer(back, heads, shapes)
    else:

        def in_columns(tiles):
            return jnp.concatenate([tile.reshape(model, LANES) for tile in tiles], axis=1)

        def summed_slices(part):
            part = lax.psum_scatter(
                part, "seq", scatter_dimension=1, tiled=True, axis_index_groups=groups
            )
            return joined(from_slices(part, d_rows))

        out_tiles = g_out[:slice_width].astype(bf16).reshape(slice_width, count, -1)
        gw_out = all_to_all(jnp.swapaxes(out_tiles, 0, 1)).reshape(w_out.shape).astype(f32)
        half = key_width // LANES
        gw_query = summed_slices(in_columns(g_pairs[:half]))
        gw_key = summed_slices(in_columns(g_pairs[half:]))
        rest = from_tiles(g_rest, d_rows).reshape(model, 2 * LANES)
        gw_value = joined(from_slices(rest[:, :slice_width], d_rows))
        gw_outgate = joined(from_slices(rest[:, LANES : LANES + slice_width], d_rows))

    def put(part, start, width, axis):
        shape = list(part.shape)
        shape[axis] = width
        return lax.dynamic_update_slice_in_dim(jnp.zeros(shape, f32), part, start, axis)

    g_taps = sums[: conv_query.shape[0]]

    pieces = [
        put(g_taps[:, :key_width], head_id * key_width, conv_query.shape[1], 1),
        put(g_taps[:, key_width : 2 * key_width], head_id * key_width, conv_key.shape[1], 1),
        put(
            g_taps[:, 2 * key_width : 2 * key_width + slice_width],
            me * slice_width,
            conv_value.shape[1],
            1,
        ),
        put(sums[5, 0:1], head_id, heads, 0),
        put(sums[5, 1:2], head_id, heads, 0),
        put(thin_rows[None, :, :2], head_id, heads, 0),
    ]
    shared = [
        put(sums[4, :slice_width], member * slice_width, value_width, 0),
        grad_second,
        grad_first,
    ]

    def packed(parts):
        flat = jnp.concatenate([part.reshape(-1) for part in parts])
        return widened(flat, -(-flat.shape[0] // 1024) * 1024, 0).reshape(-1, LANES)

    def unpacked(flat, parts):
        flat, at, out = flat.reshape(-1), 0, []
        for part in parts:
            out.append(flat[at : at + part.size].reshape(part.shape))
            at += part.size
        return out

    merged = [packed(pieces), packed(shared)]
    summed = sum_stream(jnp.concatenate(merged, axis=0))
    cut = merged[0].shape[0]
    small = unpacked(summed[:cut], pieces)
    total = unpacked(summed[cut:] + other_core(summed[cut:]), shared)

    own_cols = blocks([pick(after(part, sent_z), me * d_rows, d_rows, 1) for part in longer_one])
    own_cols = stream_order(own_cols, place).astype(f32)
    thin_grads = jnp.einsum(
        "ctd,hcgt->gdh", own_cols, small[5], precision=lax.Precision.HIGHEST
    )
    return (
        output,
        grad_input,
        total[2],
        gw_query,
        gw_key,
        gw_value,
        gw_outgate,
        thin_grads[0],
        thin_grads[1],
        small[0],
        small[1],
        small[2],
        small[3],
        small[4],
        total[0],
        gw_out,
        total[1],
        gw_gate,
        gw_up,
        gw_down,
    )


def solution(mesh):
    in_specs = (
        P("seq", None),
        P("seq"),
        P(),
        P("seq", "head"),
        P("seq", "head"),
        P("seq", "head"),
        P("seq", "head"),
        P("seq", "head"),
        P("seq", "head"),
        P(None, "head"),
        P(None, "head"),
        P(None, "head"),
        P("head"),
        P("head"),
        P(),
        P("head", "seq"),
        P(),
        P("seq", "head"),
        P("seq", "head"),
        P("head", "seq"),
        P("seq", None),
    )
    out_specs = (
        P("seq", None),
        P("seq", None),
        P(),
        P("seq", "head"),
        P("seq", "head"),
        P("seq", "head"),
        P("seq", "head"),
        P("seq", "head"),
        P("seq", "head"),
        P(None, "head"),
        P(None, "head"),
        P(None, "head"),
        P("head"),
        P("head"),
        P(),
        P("head", "seq"),
        P(),
        P("seq", "head"),
        P("seq", "head"),
        P("head", "seq"),
    )
    return jax.shard_map(
        on_device, mesh=mesh, in_specs=in_specs, out_specs=out_specs, check_vma=False
    )
```

time: 1420 us -> 804 us (0.57)
  waiting for transfers between devices: 729 us -> 276 us
  blocking collectives: 213 us -> 0 us
  starting transfers between devices: 76.2 us -> 148 us
  Pallas kernels: 66.6 us -> 92.7 us
  matrix products: 97.9 us -> 79.2 us
    reduce_scatter x8 -> x0, waiting for transfers between devices: 334 us -> none  [the longest x4 283 us: scatter_tokens(): low = lax.psum_scatter(low, 'seq', scatter_dimension=0, tiled=False)]
    ppermute x0 -> x107, waiting for transfers between devices: none -> 261 us  [the longest x92 257 us: across(): return lax.ppermute(value, 'seq', [(i, i ^ offset) for i in range(count)])]
    all_gather x7 -> x0, waiting for transfers between devices: 186 us -> none  [the longest x4 186 us: gather_tokens(): return lax.all_gather(rows, ('seq', 'head'), axis=0, tiled=True)]
    all_gather x4 -> x0, blocking collectives: 123 us -> none  [the longest x1 44 us: on_device(): lax.all_gather(jnp.stack([grad_decay_raw, grad_rate_raw]), 'seq')]
    ppermute x0 -> x107, starting transfers between devices: none -> 122 us  [the longest x92 121 us: across(): return lax.ppermute(value, 'seq', [(i, i ^ offset) for i in range(count)])]
    all_to_all x14 -> x6, waiting for transfers between devices: 137 us -> 15.2 us  [the longest x2 15.2 us: exchanged(): lax.all_to_all(blocks, 'seq', split_axis=0, concat_axis=0, tiled=True, ax...]
    psum x1 -> x0, waiting for transfers between devices: 64.6 us -> none  [on_device(): lax.psum((placed(g_taps_q, head_id * key_width, conv_query.shape[1], 1),...]
    psum x3 -> x0, blocking collectives: 59.1 us -> none  [the longest x1 39.3 us: on_device(): lax.psum((grad_first, grad_second, placed(grad_out_gain, member * slice_w...]
  transfers between devices with their start and end apart: 32 -> 113, of which waited for: 20 -> 53; matrix products, arithmetic and copies ran while one was open for 9% -> 30% of each run, Pallas kernels for 0% -> 11%
where the time goes in v2:
time: 804 us; the launch traced here: 795 us
  waiting for transfers between devices  276 us (34%)
  starting transfers between devices  148 us (18%)
  local copies, waits for them, and re-layouts  134 us (17%)
  Pallas kernels  92.7 us (12%)
  matrix products  79.2 us (10%)
  other arithmetic  60.4 us (8%)
    ppermute x92, waiting for transfers between devices, across(): return lax.ppermute(value, 'seq', [(i, i ^ offset) for i in range(count)])  257 us
    ppermute x92, starting transfers between devices, across(): return lax.ppermute(value, 'seq', [(i, i ^ offset) for i in range(count)])  121 us
    unnamed x224, local copies, waits for them, and re-layouts  46.6 us
    pallas_call x1, Pallas kernels, recurrence_backward(): pl.pallas_call(functools.partial(backward_kernel, group, key_width, value...  35.6 us
    dot_general x16, matrix products, product(): lax.dot_general(part, right, (dims, ((), ())), preferred_element_type=f32)  34.3 us
    pallas_call x1, Pallas kernels, recurrence_forward(): pl.pallas_call(functools.partial(forward_kernel, group, key_width), grid_...  28 us
    dot_general x4, matrix products, mm(): return jnp.dot(left, right, preferred_element_type=f32)  21.7 us
  transfers between devices with their start and end apart: 113, of which 53 were waited for; matrix products, arithmetic and copies ran while one was open for 30% of the time, Pallas kernels for 11%

profile of v2, /device:TPU:0, one launch (start us, length us, event | category | flops | bytes accessed | tf_op | source)
XLA Modules:
  0.0 794.9 jit_solution(9565714780637791755)
XLA Ops:
  6.6 3.0 collective-permute-start.4
  11.1 3.6 collective-permute-start.2
  30.1 7.9 collective-permute-done.1
  38.0 3.9 all-to-all-start
  53.3 2.8 collective-permute-start.10
  56.1 27.7 %collective-permute-done.12 = bf16[1,64,2048]{2,1,0:T(8,128)(2,1)S(1)} collective-permute-done((bf16[1,64,2048]{2,1,0:T(8,128)(2,1)S(1)}, bf16[1,64,2048]{2,1,0:T(8,128)(2,1)S(1)}, u32[]{:S(2)}, u32[]{:S(2)}) %collective-permute-start.12) | collective-permute-done | bytes 262176 | tf_op jit(solution)/shard_map/ppermute | solution.py:34
  89.4 3.8 collective-permute-done.7
  104.4 3.6 all-to-all-start.1
  116.3 15.2 %all-to-all-done.1 = bf16[4,2048,128]{2,1,0:T(8,128)(2,1)S(1)} async-done(((bf16[4,2048,128]{2,1,0:T(8,128)(2,1)}), bf16[4,2048,128]{2,1,0:T(8,128)(2,1)S(1)}, u32[]{:S(2)}, u32[]{:S(2)}) %all-to-all-start.1) | async-done | bytes 2097184 | tf_op jit(solution)/shard_map/all_to_all | solution.py:60
  137.4 5.7 all-to-all-start.2
  154.9 8.9 %fusion.2.refs_0_.refs_1_.refs_2_.refs_3_.refs_4_.refs_5_.refs_6_.refs_7_.mine_ref = f32[16,64,896]{2,1,0:T(8,128)} fusion(bf16[16,64,2176]{2,1,0:T(8,128)(2,1)} %constant_dynamic-update-slice_fusion.3, bf16[2048,896]{1,0:T(8,128)(2,1)} %fusion.32.weight_ref), kind=kOutput, calls=%fused_computation.11 | convolution fusion | flops 3992977408 | bytes 11796480 | tf_op jit(solution)/shard_map/dot_general | solution.py:17
  166.3 9.0 %fusion.refs_8_.refs_9_.refs_10_.refs_11_.refs_12_.refs_13_.refs_14_.refs_15_.theirs_ref.refs_2_.refs_3_ = f32[16,64,896]{2,1,0:T(8,128)} fusion(bf16[16,64,2176]{2,1,0:T(8,128)(2,1)} %collective-permute-done.13, bf16[2048,896]{1,0:T(8,128)(2,1)} %fusion.32.weight_ref), kind=kOutput, calls=%fused_computation.9 | convolution fusion | flops 3992977408 | bytes 11796480 | tf_op jit(solution)/shard_map/dot_general | solution.py:17
  179.7 28.0 %delta_forward.1 = (f32[16,128,128]{2,1,0:T(8,128)}, f32[16,128]{1,0:T(8,128)}, f32[16,128,640]{2,1,0:T(8,128)}, bf16[16,128,256]{2,1,0:T(8,128)(2,1)}, bf16[16,...) custom-call(s32[17]{0:T(128)} %pad_add_fusion.place_ref, ...), custom_call_target="tpu_custom_call" | custom-call | bytes 100800000 | tf_op jit(solution)/shard_map/delta_forward/pallas_call | solution.py:680
  225.6 4.5 gate_forward.1
  230.5 2.8 collective-permute-done.20
  243.6 17.3 %collective-permute-done.23 = bf16[2048,128]{0,1:T(8,128)(2,1)S(1)} collective-permute-done((bf16[2048,128]{0,1:T(8,128)(2,1)}, bf16[2048,128]{0,1:T(8,128)(2,1)S(1)}, u32[]{:S(2)}, u32[]{:S(2)}) %collective-permute-start.23) | collective-permute-done | bytes 524320 | tf_op jit(solution)/shard_map/ppermute | solution.py:34
  271.6 2.9 collective-permute-done.27
  281.4 2.9 collective-permute-done.33
  284.3 6.4 collective-permute-done.32
  291.4 7.9 collective-permute-done.30
  305.4 4.9 collective-permute-done.36
  310.3 5.6 collective-permute-done.34
  315.9 8.8 %collective-permute-done.35 = bf16[64,2048]{1,0:T(8,128)(2,1)S(1)} collective-permute-done((bf16[64,2048]{1,0:T(8,128)(2,1)S(1)}, bf16[64,2048]{1,0:T(8,128)(2,1)S(1)}, u32[]{:S(2)}, u32[]{:S(2)}) %collective-permute-start.35) | collective-permute-done | bytes 262176 | tf_op jit(solution)/shard_map/ppermute | solution.py:34
  328.1 3.4 collective-permute-done.39
  332.9 5.8 collective-permute-done.37
  341.5 10.4 %collective-permute-done.44 = bf16[1,64,2048]{2,1,0:T(8,128)(2,1)S(1)} collective-permute-done((bf16[1,64,2048]{2,1,0:T(8,128)(2,1)S(1)}, bf16[1,64,2048]{2,1,0:T(8,128)(2,1)S(1)}, u32[]{:S(2)}, u32[]{:S(2)}) %collective-permute-start.44) | collective-permute-done | bytes 262176 | tf_op jit(solution)/shard_map/ppermute | solution.py:34
  353.3 4.9 collective-permute-done.45
  380.4 7.3 collective-permute-done.53
  392.5 8.3 %collective-permute-done.58 = bf16[2048,128]{0,1:T(8,128)(2,1)S(1)} collective-permute-done((bf16[2048,128]{0,1:T(8,128)(2,1)S(1)}, bf16[2048,128]{0,1:T(8,128)(2,1)S(1)}, u32[]{:S(2)}, u32[]{:S(2)}) %collective-permute-start.58) | collective-permute-done | bytes 524320 | tf_op jit(solution)/shard_map/ppermute | solution.py:34
  403.8 11.7 %collective-permute-done.59 = bf16[64,2048]{1,0:T(8,128)(2,1)S(1)} collective-permute-done((bf16[64,2048]{1,0:T(8,128)(2,1)S(1)}, bf16[64,2048]{1,0:T(8,128)(2,1)S(1)}, u32[]{:S(2)}, u32[]{:S(2)}) %collective-permute-start.59) | collective-permute-done | bytes 262176 | tf_op jit(solution)/shard_map/ppermute | solution.py:34
  421.1 5.3 collective-permute-done.64
  427.2 3.7 collective-permute-done.62
  430.9 11.7 %collective-permute-done.61 = bf16[1,64,2048]{2,1,0:T(8,128)(2,1)S(1)} collective-permute-done((bf16[1,64,2048]{2,1,0:T(8,128)(2,1)S(1)}, bf16[1,64,2048]{2,1,0:T(8,128)(2,1)S(1)}, u32[]{:S(2)}, u32[]{:S(2)}) %collective-permute-start.61) | collective-permute-done | bytes 262176 | tf_op jit(solution)/shard_map/ppermute | solution.py:34
  456.1 16.7 %collective-permute-done.69 = bf16[1,64,2048]{2,1,0:T(8,128)(2,1)S(1)} collective-permute-done((bf16[1,64,2048]{2,1,0:T(8,128)(2,1)S(1)}, bf16[1,64,2048]{2,1,0:T(8,128)(2,1)S(1)}, u32[]{:S(2)}, u32[]{:S(2)}) %collective-permute-start.69) | collective-permute-done | bytes 262176 | tf_op jit(solution)/shard_map/ppermute | solution.py:34
  483.1 2.7 collective-permute-done.72
  500.4 4.2 fusion.140.grad_mine.refs_4_.refs_5_
  506.0 4.2 fusion.141.grad_theirs.refs_6_.refs_7_
  510.2 6.8 gate_dots.1
  520.5 2.9 convolution_bitcast_fusion
  523.5 3.8 fusion.6
  529.4 2.8 collective-permute-done.81
  536.3 35.6 %delta_backward.1 = (bf16[16,64,896]{2,1,0:T(8,128)(2,1)}, bf16[16,64,896]{2,1,0:T(8,128)(2,1)}, f32[8,640]{1,0:T(8,128)}, f32[16,8,128]{2,1,0:T(8,128)}) custom-call(s32[17]{0:T(128)} %pad_add_fusion.place_ref, f32[16,64,896]{2,1,0:T(8,128)} %fusion.2.refs_0_.refs_1_.refs_2_.refs_3_.refs_4_.refs_5_.refs_6_.refs_7_.mine_ref, ...), custom_call_target="tpu_custom_call" | custom-call | bytes 129600000 | tf_op jit(solution)/shard_map/delta_backward/pallas_call | solution.py:770
  572.0 14.0 %weight_gradient.1 = (bf16[4,16,128,128]{3,2,1,0:T(8,128)(2,1)}, bf16[16,256,128]{2,1,0:T(8,128)(2,1)}, f32[2048,128]{1,0:T(8,128)}) custom-call(bf16[1024,2176]{1,0:T(8,128)(2,1)} %bitcast.42.hidden_mine, bf16[1024,2176]{1,0:T(8,128)(2,1)} %bitcast.43.hidden_theirs, bf16[1024,896]{1,0:T(8,128)(2,1)} %bitcast.238, bf16[1024,896]{1,0:T(8,128)(2,1)} %bitcast.239, ...), custom_call_target="tpu_custom_call" | custom-call | bytes 50400000 | tf_op jit(solution)/shard_map/weight_gradient/pallas_call | solution.py:826
  587.0 5.8 convolution_convert_fusion
  594.6 3.6 all-to-all-start.4
  598.2 6.2 convolution_convert_fusion.1
  607.9 6.3 collective-permute-done.83
  614.1 15.2 %collective-permute-done.82 = bf16[64,2048]{1,0:T(8,128)(2,1)S(1)} collective-permute-done((bf16[64,2048]{1,0:T(8,128)(2,1)S(1)}, bf16[64,2048]{1,0:T(8,128)(2,1)S(1)}, u32[]{:S(2)}, u32[]{:S(2)}) %collective-permute-start.82) | collective-permute-done | bytes 262176 | tf_op jit(solution)/shard_map/ppermute | solution.py:34
  631.2 5.7 all-to-all-start.3
  636.9 5.4 fusion.99
  647.2 5.1 convert_add_fusion.1
  652.3 2.9 collective-permute-done.96
  655.2 4.1 collective-permute-done.91
  660.5 11.5 %collective-permute-start.97 = (bf16[128,2048]{1,0:T(8,128)(2,1)}, bf16[128,2048]{1,0:T(8,128)(2,1)}, u32[]{:S(2)}, u32[]{:S(2)}) collective-permute-start(bf16[128,2048]{1,0:T(8,128)(2,1)} %get-tuple-element.554), channel_id=1, source_target_pairs={{0,4},{2,6},{4,0},{6,2},{8,12},{10,14},{12,8},{14,10},{16,20},{18,... | collective-permute-start | bytes 1572872 | tf_op jit(solution)/shard_map/ppermute | solution.py:34
  684.8 9.5 %collective-permute-done.89 = bf16[128,1024]{1,0:T(8,128)(2,1)} collective-permute-done((bf16[128,1024]{1,0:T(8,128)(2,1)}, bf16[128,1024]{1,0:T(8,128)(2,1)}, u32[]{:S(2)}, u32[]{:S(2)}) %collective-permute-start.89) | collective-permute-done | bytes 262176 | tf_op jit(solution)/shard_map/ppermute | solution.py:34
  701.3 4.1 collective-permute-start.99
  708.8 4.1 collective-permute-start.100
  713.0 3.7 all-to-all-start.5
  718.7 2.7 slice.811
  754.4 2.9 copy.219
  757.3 3.0 copy.218
  770.3 3.2 collective-permute-done.104
  776.8 5.7 collective-permute-done.105
  791.0 3.8 unpack_mixer.1
  (638 shorter events, 323.4 us)
Async XLA Ops:
  6.6 23.4 %collective-permute-start.4 = (bf16[1,64,2176]{2,1,0:T(8,128)(2,1)S(1)}, bf16[1,64,2176]{2,1,0:T(8,128)(2,1)}, u32[]{:S(2)}, u32[]{:S(2)}) collective-permute-start(bf16[1,64,2176]{2,1,0:T(8,128)(2,1)S(1)} %maximum_bitcast_fusion.2), channel_id=1, source_target_pairs={{0,4},{2,6},{4,0},{6,2},{8,12},{10,14},{12,8},{14,10},{16,20},{18,... | collective-permute-start | bytes 835592 | tf_op jit(solution)/shard_map/ppermute | solution.py:34
  9.7 20.4 %collective-permute-start.3 = (bf16[1,64,2176]{2,1,0:T(8,128)(2,1)S(1)}, bf16[1,64,2176]{2,1,0:T(8,128)(2,1)}, u32[]{:S(2)}, u32[]{:S(2)}) collective-permute-start(bf16[1,64,2176]{2,1,0:T(8,128)(2,1)S(1)} %maximum_bitcast_fusion.2), channel_id=1, source_target_pairs={{0,2},{2,0},{4,6},{6,4},{8,10},{10,8},{12,14},{14,12},{16,18},{18,... | collective-permute-start | bytes 835592 | tf_op jit(solution)/shard_map/ppermute | solution.py:34
  11.1 18.9 %collective-permute-start.2 = (bf16[1,64,2176]{2,1,0:T(8,128)(2,1)S(1)}, bf16[1,64,2176]{2,1,0:T(8,128)(2,1)}, u32[]{:S(2)}, u32[]{:S(2)}) collective-permute-start(bf16[1,64,2176]{2,1,0:T(8,128)(2,1)S(1)} %maximum_bitcast_fusion.2), channel_id=1, source_target_pairs={{0,24},{2,26},{4,28},{6,30},{8,16},{10,18},{12,20},{14,22},{16,8},... | collective-permute-start | bytes 835592 | tf_op jit(solution)/shard_map/ppermute | solution.py:34
  14.7 23.3 %collective-permute-start.1 = (bf16[1,64,2176]{2,1,0:T(8,128)(2,1)S(1)}, bf16[1,64,2176]{2,1,0:T(8,128)(2,1)}, u32[]{:S(2)}, u32[]{:S(2)}) collective-permute-start(bf16[1,64,2176]{2,1,0:T(8,128)(2,1)S(1)} %maximum_bitcast_fusion.2), channel_id=1, source_target_pairs={{0,16},{2,18},{4,20},{6,22},{8,24},{10,26},{12,28},{14,30},{16,0},... | collective-permute-start | bytes 835592 | tf_op jit(solution)/shard_map/ppermute | solution.py:34
  14.7 23.3 %collective-permute-start = (bf16[1,64,2176]{2,1,0:T(8,128)(2,1)S(1)}, bf16[1,64,2176]{2,1,0:T(8,128)(2,1)}, u32[]{:S(2)}, u32[]{:S(2)}) collective-permute-start(bf16[1,64,2176]{2,1,0:T(8,128)(2,1)S(1)} %maximum_bitcast_fusion.2), channel_id=1, source_target_pairs={{0,8},{2,10},{4,12},{6,14},{8,0},{10,2},{12,4},{14,6},{16,24},{18,... | collective-permute-start | bytes 835592 | tf_op jit(solution)/shard_map/ppermute | solution.py:34
  38.0 64.6 %all-to-all-start = ((bf16[128,16,384]{2,0,1:T(8,128)(2,1)}), bf16[128,16,384]{2,0,1:T(8,128)(2,1)S(1)}, u32[]{:S(2)}, u32[]{:S(2)}) async-start(bf16[128,16,384]{2,0,1:T(8,128)(2,1)} %pad_maximum_fusion.4), calls=%async_computation | async-start | bytes 3145728 | tf_op jit(solution)/shard_map/all_to_all | solution.py:246
  48.0 45.1 %collective-permute-start.6 = (bf16[3,64,2176]{2,1,0:T(8,128)(2,1)}, bf16[3,64,2176]{2,1,0:T(8,128)(2,1)}, u32[]{:S(2)}, u32[]{:S(2)}) collective-permute-start(bf16[3,64,2176]{2,1,0:T(8,128)(2,1)} %get-tuple-element.644), channel_id=1, source_target_pairs={{0,4},{2,6},{4,0},{6,2},{8,12},{10,14},{12,8},{14,10},{16,20},{18,... | collective-permute-start | bytes 2506760 | tf_op jit(solution)/shard_map/ppermute | solution.py:34
  49.9 43.2 %collective-permute-start.5 = (bf16[3,64,2176]{2,1,0:T(8,128)(2,1)}, bf16[3,64,2176]{2,1,0:T(8,128)(2,1)S(1)}, u32[]{:S(2)}, u32[]{:S(2)}) collective-permute-start(bf16[3,64,2176]{2,1,0:T(8,128)(2,1)} %get-tuple-element.644), channel_id=1, source_target_pairs={{0,2},{2,0},{4,6},{6,4},{8,10},{10,8},{12,14},{14,12},{16,18},{18,... | collective-permute-start | bytes 2506760 | tf_op jit(solution)/shard_map/ppermute | solution.py:34
  52.4 31.4 %collective-permute-start.12 = (bf16[1,64,2048]{2,1,0:T(8,128)(2,1)S(1)}, bf16[1,64,2048]{2,1,0:T(8,128)(2,1)S(1)}, u32[]{:S(2)}, u32[]{:S(2)}) collective-permute-start(bf16[1,64,2048]{2,1,0:T(8,128)(2,1)S(1)} %bitcast.272), channel_id=1, source_target_pairs={{0,4},{2,6},{4,0},{6,2},{8,12},{10,14},{12,8},{14,10},{16,20},{18,... | collective-permute-start | bytes 786440 | tf_op jit(solution)/shard_map/ppermute | solution.py:34
  53.1 35.6 %collective-permute-start.11 = (bf16[1,64,2048]{2,1,0:T(8,128)(2,1)S(1)}, bf16[1,64,2048]{2,1,0:T(8,128)(2,1)S(1)}, u32[]{:S(2)}, u32[]{:S(2)}) collective-permute-start(bf16[1,64,2048]{2,1,0:T(8,128)(2,1)S(1)} %bitcast.273), channel_id=1, source_target_pairs={{0,2},{2,0},{4,6},{6,4},{8,10},{10,8},{12,14},{14,12},{16,18},{18,... | collective-permute-start | bytes 786440 | tf_op jit(solution)/shard_map/ppermute | solution.py:34
  53.3 36.1 %collective-permute-start.10 = (bf16[1,64,2048]{2,1,0:T(8,128)(2,1)S(1)}, bf16[1,64,2048]{2,1,0:T(8,128)(2,1)S(1)}, u32[]{:S(2)}, u32[]{:S(2)}) collective-permute-start(bf16[1,64,2048]{2,1,0:T(8,128)(2,1)S(1)} %bitcast.274), channel_id=1, source_target_pairs={{0,16},{2,18},{4,20},{6,22},{8,24},{10,26},{12,28},{14,30},{16,0},... | collective-permute-start | bytes 786440 | tf_op jit(solution)/shard_map/ppermute | solution.py:34
  94.9 13.1 %collective-permute-start.8 = (bf16[1,64,2176]{2,1,0:T(8,128)(2,1)}, bf16[1,64,2176]{2,1,0:T(8,128)(2,1)}, u32[]{:S(2)}, u32[]{:S(2)}) collective-permute-start(bf16[1,64,2176]{2,1,0:T(8,128)(2,1)} %slice.650), channel_id=1, source_target_pairs={{0,2},{2,0},{4,6},{6,4},{8,10},{10,8},{12,14},{14,12},{16,18},{18,... | collective-permute-start | bytes 835592 | tf_op jit(solution)/shard_map/ppermute | solution.py:34
  96.4 13.4 %collective-permute-start.9 = (bf16[2,64,2176]{2,1,0:T(8,128)(2,1)S(1)}, bf16[2,64,2176]{2,1,0:T(8,128)(2,1)}, u32[]{:S(2)}, u32[]{:S(2)}) collective-permute-start(bf16[2,64,2176]{2,1,0:T(8,128)(2,1)S(1)} %slice.651), channel_id=1, source_target_pairs={{0,4},{2,6},{4,0},{6,2},{8,12},{10,14},{12,8},{14,10},{16,20},{18,... | collective-permute-start | bytes 1671176 | tf_op jit(solution)/shard_map/ppermute | solution.py:34
  104.4 27.1 %all-to-all-start.1 = ((bf16[4,2048,128]{2,1,0:T(8,128)(2,1)}), bf16[4,2048,128]{2,1,0:T(8,128)(2,1)S(1)}, u32[]{:S(2)}, u32[]{:S(2)}) async-start(bf16[4,2048,128]{2,1,0:T(8,128)(2,1)} %broadcast_in_dim.90), calls=%async_computation.1 | async-start | bytes 4194304 | tf_op jit(solution)/shard_map/all_to_all | solution.py:60
  112.6 51.2 %collective-permute-start.13 = (bf16[16,64,2176]{2,1,0:T(8,128)(2,1)}, bf16[16,64,2176]{2,1,0:T(8,128)(2,1)}, u32[]{:S(2)}, u32[]{:S(2)}) collective-permute-start(bf16[16,64,2176]{2,1,0:T(8,128)(2,1)} %constant_dynamic-update-slice_fusion.3), channel_id=1, source_target_pairs={{0,1},{1,0},{2,3},{3,2},{4,5},{5,4},{6,7},{7,6},{8,9},{9,8},{10,11... | collective-permute-start | bytes 13369352 | tf_op jit(solution)/shard_map/ppermute | solution.py:38
  137.4 78.5 %all-to-all-start.2 = ((bf16[16,688,128]{2,1,0:T(8,128)(2,1)}), bf16[16,688,128]{2,1,0:T(8,128)(2,1)S(1)}, u32[]{:S(2)}, u32[]{:S(2)}) async-start(bf16[16,688,128]{2,1,0:T(8,128)(2,1)} %pad_maximum_fusion), calls=%async_computation.2 | async-start | bytes 5636096 | tf_op jit(solution)/shard_map/all_to_all | solution.py:206
  150.9 61.2 %collective-permute-start.15 = (bf16[1,64,2048]{2,1,0:T(8,128)(2,1)}, bf16[1,64,2048]{2,1,0:T(8,128)(2,1)}, u32[]{:S(2)}, u32[]{:S(2)}) collective-permute-start(bf16[1,64,2048]{2,1,0:T(8,128)(2,1)} %copy-done.58), channel_id=1, source_target_pairs={{0,4},{2,6},{4,0},{6,2},{8,12},{10,14},{12,8},{14,10},{16,20},{18,... | collective-permute-start | bytes 786440 | tf_op jit(solution)/shard_map/ppermute | solution.py:34
  152.9 59.2 %collective-permute-start.14 = (bf16[1,64,2048]{2,1,0:T(8,128)(2,1)}, bf16[1,64,2048]{2,1,0:T(8,128)(2,1)}, u32[]{:S(2)}, u32[]{:S(2)}) collective-permute-start(bf16[1,64,2048]{2,1,0:T(8,128)(2,1)} %copy-done.58), channel_id=1, source_target_pairs={{0,2},{2,0},{4,6},{6,4},{8,10},{10,8},{12,14},{14,12},{16,18},{18,... | collective-permute-start | bytes 786440 | tf_op jit(solution)/shard_map/ppermute | solution.py:34
  154.3 56.4 %collective-permute-start.16 = (bf16[1,64,2048]{2,1,0:T(8,128)(2,1)}, bf16[1,64,2048]{2,1,0:T(8,128)(2,1)}, u32[]{:S(2)}, u32[]{:S(2)}) collective-permute-start(bf16[1,64,2048]{2,1,0:T(8,128)(2,1)} %copy-done.54), channel_id=1, source_target_pairs={{0,2},{2,0},{4,6},{6,4},{8,10},{10,8},{12,14},{14,12},{16,18},{18,... | collective-permute-start | bytes 786440 | tf_op jit(solution)/shard_map/ppermute | solution.py:34
  218.3 18.9 %collective-permute-start.40 = (bf16[1,64,2048]{2,1,0:T(8,128)(2,1)}, bf16[1,64,2048]{2,1,0:T(8,128)(2,1)}, u32[]{:S(2)}, u32[]{:S(2)}) collective-permute-start(bf16[1,64,2048]{2,1,0:T(8,128)(2,1)} %collective-permute-done.14), channel_id=1, source_target_pairs={{0,4},{2,6},{4,0},{6,2},{8,12},{10,14},{12,8},{14,10},{16,20},{18,... | collective-permute-start | bytes 786440 | tf_op jit(solution)/shard_map/ppermute | solution.py:34
  235.0 31.1 %collective-permute-start.28 = (bf16[2048,128]{0,1:T(8,128)(2,1)}, bf16[2048,128]{0,1:T(8,128)(2,1)S(1)}, u32[]{:S(2)}, u32[]{:S(2)}) collective-permute-start(bf16[2048,128]{0,1:T(8,128)(2,1)} %get-tuple-element.611), channel_id=1, source_target_pairs={{0,8},{2,10},{4,12},{6,14},{8,0},{10,2},{12,4},{14,6},{16,24},{18,... | collective-permute-start | bytes 1572872 | tf_op jit(solution)/shard_map/ppermute | solution.py:34
  236.5 24.3 %collective-permute-start.23 = (bf16[2048,128]{0,1:T(8,128)(2,1)}, bf16[2048,128]{0,1:T(8,128)(2,1)S(1)}, u32[]{:S(2)}, u32[]{:S(2)}) collective-permute-start(bf16[2048,128]{0,1:T(8,128)(2,1)} %get-tuple-element.612), channel_id=1, source_target_pairs={{0,8},{2,10},{4,12},{6,14},{8,0},{10,2},{12,4},{14,6},{16,24},{18,... | collective-permute-start | bytes 1572872 | tf_op jit(solution)/shard_map/ppermute | solution.py:34
  266.1 18.1 %collective-permute-start.33 = (bf16[192,2048]{1,0:T(8,128)(2,1)S(1)}, bf16[192,2048]{1,0:T(8,128)(2,1)S(1)}, u32[]{:S(2)}, u32[]{:S(2)}) collective-permute-start(bf16[192,2048]{1,0:T(8,128)(2,1)S(1)} %pad.154), channel_id=1, source_target_pairs={{0,8},{2,10},{4,12},{6,14},{8,0},{10,2},{12,4},{14,6},{16,24},{18,... | collective-permute-start | bytes 2359304 | tf_op jit(solution)/shard_map/ppermute | solution.py:34
  275.7 14.9 %collective-permute-start.32 = (bf16[128,2048]{1,0:T(8,128)(2,1)S(1)}, bf16[128,2048]{1,0:T(8,128)(2,1)S(1)}, u32[]{:S(2)}, u32[]{:S(2)}) collective-permute-start(bf16[128,2048]{1,0:T(8,128)(2,1)S(1)} %add_convert_fusion.1), channel_id=1, source_target_pairs={{0,4},{2,6},{4,0},{6,2},{8,12},{10,14},{12,8},{14,10},{16,20},{18,... | collective-permute-start | bytes 1572872 | tf_op jit(solution)/shard_map/ppermute | solution.py:34
  276.5 14.9 %collective-permute-start.31 = (bf16[128,2048]{1,0:T(8,128)(2,1)S(1)}, bf16[128,2048]{1,0:T(8,128)(2,1)S(1)}, u32[]{:S(2)}, u32[]{:S(2)}) collective-permute-start(bf16[128,2048]{1,0:T(8,128)(2,1)S(1)} %add_convert_fusion.2), channel_id=1, source_target_pairs={{0,2},{2,0},{4,6},{6,4},{8,10},{10,8},{12,14},{14,12},{16,18},{18,... | collective-permute-start | bytes 1572872 | tf_op jit(solution)/shard_map/ppermute | solution.py:34
  277.0 22.3 %collective-permute-start.30 = (bf16[128,2048]{1,0:T(8,128)(2,1)S(1)}, bf16[128,2048]{1,0:T(8,128)(2,1)S(1)}, u32[]{:S(2)}, u32[]{:S(2)}) collective-permute-start(bf16[128,2048]{1,0:T(8,128)(2,1)S(1)} %add_convert_fusion.3), channel_id=1, source_target_pairs={{0,4},{2,6},{4,0},{6,2},{8,12},{10,14},{12,8},{14,10},{16,20},{18,... | collective-permute-start | bytes 1572872 | tf_op jit(solution)/shard_map/ppermute | solution.py:34
  278.8 21.1 %collective-permute-start.29 = (bf16[128,2048]{1,0:T(8,128)(2,1)S(1)}, bf16[128,2048]{1,0:T(8,128)(2,1)S(1)}, u32[]{:S(2)}, u32[]{:S(2)}) collective-permute-start(bf16[128,2048]{1,0:T(8,128)(2,1)S(1)} %add_convert_fusion.4), channel_id=1, source_target_pairs={{0,2},{2,0},{4,6},{6,4},{8,10},{10,8},{12,14},{14,12},{16,18},{18,... | collective-permute-start | bytes 1572872 | tf_op jit(solution)/shard_map/ppermute | solution.py:34
  284.3 42.8 %collective-permute-start.41 = (bf16[8,64,2048]{2,1,0:T(8,128)(2,1)S(1)}, bf16[8,64,2048]{2,1,0:T(8,128)(2,1)S(1)}, u32[]{:S(2)}, u32[]{:S(2)}) collective-permute-start(bf16[8,64,2048]{2,1,0:T(8,128)(2,1)S(1)} %constant_dynamic-update-slice_fusion.14), channel_id=1, source_target_pairs={{0,1},{1,0},{2,3},{3,2},{4,5},{5,4},{6,7},{7,6},{8,9},{9,8},{10,11... | collective-permute-start | bytes 6291464 | tf_op jit(solution)/shard_map/ppermute | solution.py:38
  301.9 14.0 %collective-permute-start.34 = (bf16[64,2048]{1,0:T(8,128)(2,1)S(1)}, bf16[64,2048]{1,0:T(8,128)(2,1)S(1)}, u32[]{:S(2)}, u32[]{:S(2)}) collective-permute-start(bf16[64,2048]{1,0:T(8,128)(2,1)S(1)} %get-tuple-element.638), channel_id=1, source_target_pairs={{0,24},{2,26},{4,28},{6,30},{8,16},{10,18},{12,20},{14,22},{16,8},... | collective-permute-start | bytes 786440 | tf_op jit(solution)/shard_map/ppermute | solution.py:34
  304.3 20.4 %collective-permute-start.35 = (bf16[64,2048]{1,0:T(8,128)(2,1)S(1)}, bf16[64,2048]{1,0:T(8,128)(2,1)S(1)}, u32[]{:S(2)}, u32[]{:S(2)}) collective-permute-start(bf16[64,2048]{1,0:T(8,128)(2,1)S(1)} %get-tuple-element.639), channel_id=1, source_target_pairs={{0,16},{2,18},{4,20},{6,22},{8,24},{10,26},{12,28},{14,30},{16,0},... | collective-permute-start | bytes 786440 | tf_op jit(solution)/shard_map/ppermute | solution.py:34
  338.7 13.2 %collective-permute-start.43 = (bf16[1,64,2048]{2,1,0:T(8,128)(2,1)S(1)}, bf16[1,64,2048]{2,1,0:T(8,128)(2,1)S(1)}, u32[]{:S(2)}, u32[]{:S(2)}) collective-permute-start(bf16[1,64,2048]{2,1,0:T(8,128)(2,1)S(1)} %collective-permute-done.37), channel_id=1, source_target_pairs={{0,4},{2,6},{4,0},{6,2},{8,12},{10,14},{12,8},{14,10},{16,20},{18,... | collective-permute-start | bytes 786440 | tf_op jit(solution)/shard_map/ppermute | solution.py:34
  373.7 14.0 %collective-permute-start.53 = (bf16[2048,128]{0,1:T(8,128)(2,1)S(1)}, bf16[2048,128]{0,1:T(8,128)(2,1)S(1)}, u32[]{:S(2)}, u32[]{:S(2)}) collective-permute-start(bf16[2048,128]{0,1:T(8,128)(2,1)S(1)} %get-tuple-element.566), channel_id=1, source_target_pairs={{0,8},{2,10},{4,12},{6,14},{8,0},{10,2},{12,4},{14,6},{16,24},{18,... | collective-permute-start | bytes 1572872 | tf_op jit(solution)/shard_map/ppermute | solution.py:34
  417.6 25.1 %collective-permute-start.66 = (bf16[256,2048]{1,0:T(8,128)(2,1)S(1)}, bf16[256,2048]{1,0:T(8,128)(2,1)S(1)}, u32[]{:S(2)}, u32[]{:S(2)}) collective-permute-start(bf16[256,2048]{1,0:T(8,128)(2,1)S(1)} %convolution_convert_fusion.4), channel_id=1, source_target_pairs={{0,1},{1,0},{2,3},{3,2},{4,5},{5,4},{6,7},{7,6},{8,9},{9,8},{10,11... | collective-permute-start | bytes 3145736 | tf_op jit(solution)/shard_map/ppermute | solution.py:38
  421.1 21.6 %collective-permute-start.61 = (bf16[1,64,2048]{2,1,0:T(8,128)(2,1)S(1)}, bf16[1,64,2048]{2,1,0:T(8,128)(2,1)S(1)}, u32[]{:S(2)}, u32[]{:S(2)}) collective-permute-start(bf16[1,64,2048]{2,1,0:T(8,128)(2,1)S(1)} %get-tuple-element.394), channel_id=1, source_target_pairs={{0,16},{2,18},{4,20},{6,22},{8,24},{10,26},{12,28},{14,30},{16,0},... | collective-permute-start | bytes 786440 | tf_op jit(solution)/shard_map/ppermute | solution.py:34
  426.4 16.3 %collective-permute-start.60 = (bf16[1,64,2048]{2,1,0:T(8,128)(2,1)S(1)}, bf16[1,64,2048]{2,1,0:T(8,128)(2,1)S(1)}, u32[]{:S(2)}, u32[]{:S(2)}) collective-permute-start(bf16[1,64,2048]{2,1,0:T(8,128)(2,1)S(1)} %get-tuple-element.394), channel_id=1, source_target_pairs={{0,8},{2,10},{4,12},{6,14},{8,0},{10,2},{12,4},{14,6},{16,24},{18,... | collective-permute-start | bytes 786440 | tf_op jit(solution)/shard_map/ppermute | solution.py:34
  427.2 18.2 %collective-permute-start.65 = (bf16[256,2048]{1,0:T(8,128)(2,1)S(1)}, bf16[256,2048]{1,0:T(8,128)(2,1)S(1)}, u32[]{:S(2)}, u32[]{:S(2)}) collective-permute-start(bf16[256,2048]{1,0:T(8,128)(2,1)S(1)} %convolution_convert_fusion.5), channel_id=1, source_target_pairs={{0,1},{1,0},{2,3},{3,2},{4,5},{5,4},{6,7},{7,6},{8,9},{9,8},{10,11... | collective-permute-start | bytes 3145736 | tf_op jit(solution)/shard_map/ppermute | solution.py:38
  447.6 25.2 %collective-permute-start.68 = (bf16[3,64,2048]{2,1,0:T(8,128)(2,1)S(1)}, bf16[3,64,2048]{2,1,0:T(8,128)(2,1)S(1)}, u32[]{:S(2)}, u32[]{:S(2)}) collective-permute-start(bf16[3,64,2048]{2,1,0:T(8,128)(2,1)S(1)} %constant_dynamic-update-slice_fusion.50), channel_id=1, source_target_pairs={{0,4},{2,6},{4,0},{6,2},{8,12},{10,14},{12,8},{14,10},{16,20},{18,... | collective-permute-start | bytes 2359304 | tf_op jit(solution)/shard_map/ppermute | solution.py:34
  449.0 23.8 %collective-permute-start.67 = (bf16[3,64,2048]{2,1,0:T(8,128)(2,1)S(1)}, bf16[3,64,2048]{2,1,0:T(8,128)(2,1)S(1)}, u32[]{:S(2)}, u32[]{:S(2)}) collective-permute-start(bf16[3,64,2048]{2,1,0:T(8,128)(2,1)S(1)} %constant_dynamic-update-slice_fusion.50), channel_id=1, source_target_pairs={{0,2},{2,0},{4,6},{6,4},{8,10},{10,8},{12,14},{14,12},{16,18},{18,... | collective-permute-start | bytes 2359304 | tf_op jit(solution)/shard_map/ppermute | solution.py:34
  450.5 22.3 %collective-permute-start.70 = (bf16[2048,128]{0,1:T(8,128)(2,1)S(1)}, bf16[2048,128]{0,1:T(8,128)(2,1)S(1)}, u32[]{:S(2)}, u32[]{:S(2)}) collective-permute-start(bf16[2048,128]{0,1:T(8,128)(2,1)S(1)} %get-tuple-element.564), channel_id=1, source_target_pairs={{0,8},{2,10},{4,12},{6,14},{8,0},{10,2},{12,4},{14,6},{16,24},{18,... | collective-permute-start | bytes 1572872 | tf_op jit(solution)/shard_map/ppermute | solution.py:34
  450.6 22.2 %collective-permute-start.69 = (bf16[1,64,2048]{2,1,0:T(8,128)(2,1)S(1)}, bf16[1,64,2048]{2,1,0:T(8,128)(2,1)S(1)}, u32[]{:S(2)}, u32[]{:S(2)}) collective-permute-start(bf16[1,64,2048]{2,1,0:T(8,128)(2,1)S(1)} %collective-permute-done.64), channel_id=1, source_target_pairs={{0,2},{2,0},{4,6},{6,4},{8,10},{10,8},{12,14},{14,12},{16,18},{18,... | collective-permute-start | bytes 786440 | tf_op jit(solution)/shard_map/ppermute | solution.py:34
  454.1 28.4 %collective-permute-start.73 = (bf16[192,2048]{1,0:T(8,128)(2,1)}, bf16[192,2048]{1,0:T(8,128)(2,1)}, u32[]{:S(2)}, u32[]{:S(2)}) collective-permute-start(bf16[192,2048]{1,0:T(8,128)(2,1)} %slice.1091), channel_id=1, source_target_pairs={{0,8},{2,10},{4,12},{6,14},{8,0},{10,2},{12,4},{14,6},{16,24},{18,... | collective-permute-start | bytes 2359304 | tf_op jit(solution)/shard_map/ppermute | solution.py:34
  499.1 30.3 %collective-permute-start.79 = (bf16[64,1024]{1,0:T(8,128)(2,1)S(1)}, bf16[64,1024]{1,0:T(8,128)(2,1)S(1)}, u32[]{:S(2)}, u32[]{:S(2)}) collective-permute-start(bf16[64,1024]{1,0:T(8,128)(2,1)S(1)} %get-tuple-element.652), channel_id=1, source_target_pairs={{0,4},{2,6},{4,0},{6,2},{8,12},{10,14},{12,8},{14,10},{16,20},{18,... | collective-permute-start | bytes 393224 | tf_op jit(solution)/shard_map/ppermute | solution.py:34
  499.9 29.5 %collective-permute-start.78 = (bf16[64,1024]{1,0:T(8,128)(2,1)S(1)}, bf16[64,1024]{1,0:T(8,128)(2,1)S(1)}, u32[]{:S(2)}, u32[]{:S(2)}) collective-permute-start(bf16[64,1024]{1,0:T(8,128)(2,1)S(1)} %get-tuple-element.653), channel_id=1, source_target_pairs={{0,2},{2,0},{4,6},{6,4},{8,10},{10,8},{12,14},{14,12},{16,18},{18,... | collective-permute-start | bytes 393224 | tf_op jit(solution)/shard_map/ppermute | solution.py:34
  533.7 71.0 %collective-permute-start.85 = (bf16[64,2048]{1,0:T(8,128)(2,1)}, bf16[64,2048]{1,0:T(8,128)(2,1)}, u32[]{:S(2)}, u32[]{:S(2)}) collective-permute-start(bf16[64,2048]{1,0:T(8,128)(2,1)} %add_convert_fusion.7), channel_id=1, source_target_pairs={{0,4},{2,6},{4,0},{6,2},{8,12},{10,14},{12,8},{14,10},{16,20},{18,... | collective-permute-start | bytes 786440 | tf_op jit(solution)/shard_map/ppermute | solution.py:34
  535.8 72.1 %collective-permute-start.84 = (bf16[64,2048]{1,0:T(8,128)(2,1)}, bf16[64,2048]{1,0:T(8,128)(2,1)}, u32[]{:S(2)}, u32[]{:S(2)}) collective-permute-start(bf16[64,2048]{1,0:T(8,128)(2,1)} %add_convert_fusion.8), channel_id=1, source_target_pairs={{0,2},{2,0},{4,6},{6,4},{8,10},{10,8},{12,14},{14,12},{16,18},{18,... | collective-permute-start | bytes 786440 | tf_op jit(solution)/shard_map/ppermute | solution.py:34
  592.8 44.1 %collective-permute-start.88 = (bf16[512,2048]{1,0:T(8,128)(2,1)}, bf16[512,2048]{1,0:T(8,128)(2,1)}, u32[]{:S(2)}, u32[]{:S(2)}) collective-permute-start(bf16[512,2048]{1,0:T(8,128)(2,1)} %convolution_convert_fusion), channel_id=1, source_target_pairs={{0,1},{1,0},{2,3},{3,2},{4,5},{5,4},{6,7},{7,6},{8,9},{9,8},{10,11... | collective-permute-start | bytes 6291464 | tf_op jit(solution)/shard_map/ppermute | solution.py:38
  593.6 20.5 %collective-permute-start.83 = (bf16[64,2048]{1,0:T(8,128)(2,1)}, bf16[64,2048]{1,0:T(8,128)(2,1)S(1)}, u32[]{:S(2)}, u32[]{:S(2)}) collective-permute-start(bf16[64,2048]{1,0:T(8,128)(2,1)} %add_convert_fusion.9), channel_id=1, source_target_pairs={{0,4},{2,6},{4,0},{6,2},{8,12},{10,14},{12,8},{14,10},{16,20},{18,... | collective-permute-start | bytes 786440 | tf_op jit(solution)/shard_map/ppermute | solution.py:34
  594.6 36.7 %all-to-all-start.4 = ((bf16[4,2048,128]{2,1,0:T(8,128)(2,1)}), bf16[4,2048,128]{2,1,0:T(8,128)(2,1)S(1)}, u32[]{:S(2)}, u32[]{:S(2)}) async-start(bf16[4,2048,128]{2,1,0:T(8,128)(2,1)} %bitcast.261), calls=%async_computation.4 | async-start | bytes 4194304 | tf_op jit(solution)/shard_map/all_to_all | solution.py:60
  604.4 42.8 %collective-permute-start.87 = (bf16[512,2048]{1,0:T(8,128)(2,1)}, bf16[512,2048]{1,0:T(8,128)(2,1)}, u32[]{:S(2)}, u32[]{:S(2)}) collective-permute-start(bf16[512,2048]{1,0:T(8,128)(2,1)} %convolution_convert_fusion.1), channel_id=1, source_target_pairs={{0,1},{1,0},{2,3},{3,2},{4,5},{5,4},{6,7},{7,6},{8,9},{9,8},{10,11... | collective-permute-start | bytes 6291464 | tf_op jit(solution)/shard_map/ppermute | solution.py:38
  604.7 24.6 %collective-permute-start.82 = (bf16[64,2048]{1,0:T(8,128)(2,1)S(1)}, bf16[64,2048]{1,0:T(8,128)(2,1)S(1)}, u32[]{:S(2)}, u32[]{:S(2)}) collective-permute-start(bf16[64,2048]{1,0:T(8,128)(2,1)S(1)} %add_convert_fusion.10), channel_id=1, source_target_pairs={{0,2},{2,0},{4,6},{6,4},{8,10},{10,8},{12,14},{14,12},{16,18},{18,... | collective-permute-start | bytes 786440 | tf_op jit(solution)/shard_map/ppermute | solution.py:34
  631.2 48.2 %collective-permute-start.86 = (bf16[64,2048]{1,0:T(8,128)(2,1)}, bf16[64,2048]{1,0:T(8,128)(2,1)}, u32[]{:S(2)}, u32[]{:S(2)}) collective-permute-start(bf16[64,2048]{1,0:T(8,128)(2,1)} %add_convert_fusion.6), channel_id=1, source_target_pairs={{0,16},{2,18},{4,20},{6,22},{8,24},{10,26},{12,28},{14,30},{16,0},... | collective-permute-start | bytes 786440 | tf_op jit(solution)/shard_map/ppermute | solution.py:34
  631.2 81.8 %all-to-all-start.3 = ((bf16[16,560,128]{2,1,0:T(8,128)(2,1)}), bf16[16,560,128]{2,1,0:T(8,128)(2,1)}, u32[]{:S(2)}, u32[]{:S(2)}) async-start(bf16[16,560,128]{2,1,0:T(8,128)(2,1)} %pad_maximum_fusion.1), calls=%async_computation.3 | async-start | bytes 4587520 | tf_op jit(solution)/shard_map/all_to_all | solution.py:206
  643.2 28.8 %collective-permute-start.94 = (bf16[128,1024]{1,0:T(8,128)(2,1)S(1)}, bf16[128,1024]{1,0:T(8,128)(2,1)S(1)}, u32[]{:S(2)}, u32[]{:S(2)}) collective-permute-start(bf16[128,1024]{1,0:T(8,128)(2,1)S(1)} %get-tuple-element.567), channel_id=1, source_target_pairs={{0,4},{2,6},{4,0},{6,2},{8,12},{10,14},{12,8},{14,10},{16,20},{18,... | collective-permute-start | bytes 786440 | tf_op jit(solution)/shard_map/ppermute | solution.py:34
  660.5 33.8 %collective-permute-start.97 = (bf16[128,2048]{1,0:T(8,128)(2,1)}, bf16[128,2048]{1,0:T(8,128)(2,1)}, u32[]{:S(2)}, u32[]{:S(2)}) collective-permute-start(bf16[128,2048]{1,0:T(8,128)(2,1)} %get-tuple-element.554), channel_id=1, source_target_pairs={{0,4},{2,6},{4,0},{6,2},{8,12},{10,14},{12,8},{14,10},{16,20},{18,... | collective-permute-start | bytes 1572872 | tf_op jit(solution)/shard_map/ppermute | solution.py:34
  672.8 21.4 %collective-permute-start.95 = (bf16[128,2048]{1,0:T(8,128)(2,1)}, bf16[128,2048]{1,0:T(8,128)(2,1)}, u32[]{:S(2)}, u32[]{:S(2)}) collective-permute-start(bf16[128,2048]{1,0:T(8,128)(2,1)} %fusion.11), channel_id=1, source_target_pairs={{0,2},{2,0},{4,6},{6,4},{8,10},{10,8},{12,14},{14,12},{16,18},{18,... | collective-permute-start | bytes 1572872 | tf_op jit(solution)/shard_map/ppermute | solution.py:34
  679.4 14.9 %collective-permute-start.89 = (bf16[128,1024]{1,0:T(8,128)(2,1)}, bf16[128,1024]{1,0:T(8,128)(2,1)}, u32[]{:S(2)}, u32[]{:S(2)}) collective-permute-start(bf16[128,1024]{1,0:T(8,128)(2,1)} %get-tuple-element.570), channel_id=1, source_target_pairs={{0,4},{2,6},{4,0},{6,2},{8,12},{10,14},{12,8},{14,10},{16,20},{18,... | collective-permute-start | bytes 786440 | tf_op jit(solution)/shard_map/ppermute | solution.py:34
  682.7 22.6 %collective-permute-start.92 = (bf16[128,2048]{1,0:T(8,128)(2,1)}, bf16[128,2048]{1,0:T(8,128)(2,1)S(1)}, u32[]{:S(2)}, u32[]{:S(2)}) collective-permute-start(bf16[128,2048]{1,0:T(8,128)(2,1)} %get-tuple-element.555), channel_id=1, source_target_pairs={{0,4},{2,6},{4,0},{6,2},{8,12},{10,14},{12,8},{14,10},{16,20},{18,... | collective-permute-start | bytes 1572872 | tf_op jit(solution)/shard_map/ppermute | solution.py:34
  700.0 62.8 %collective-permute-start.98 = (bf16[64,2048]{1,0:T(8,128)(2,1)}, bf16[64,2048]{1,0:T(8,128)(2,1)}, u32[]{:S(2)}, u32[]{:S(2)}) collective-permute-start(bf16[64,2048]{1,0:T(8,128)(2,1)} %get-tuple-element.634), channel_id=1, source_target_pairs={{0,24},{2,26},{4,28},{6,30},{8,16},{10,18},{12,20},{14,22},{16,8},... | collective-permute-start | bytes 786440 | tf_op jit(solution)/shard_map/ppermute | solution.py:34
  701.3 61.5 %collective-permute-start.99 = (bf16[64,2048]{1,0:T(8,128)(2,1)}, bf16[64,2048]{1,0:T(8,128)(2,1)}, u32[]{:S(2)}, u32[]{:S(2)}) collective-permute-start(bf16[64,2048]{1,0:T(8,128)(2,1)} %get-tuple-element.635), channel_id=1, source_target_pairs={{0,16},{2,18},{4,20},{6,22},{8,24},{10,26},{12,28},{14,30},{16,0},... | collective-permute-start | bytes 786440 | tf_op jit(solution)/shard_map/ppermute | solution.py:34
  708.8 53.9 %collective-permute-start.100 = (bf16[64,2048]{1,0:T(8,128)(2,1)}, bf16[64,2048]{1,0:T(8,128)(2,1)}, u32[]{:S(2)}, u32[]{:S(2)}) collective-permute-start(bf16[64,2048]{1,0:T(8,128)(2,1)} %slice.1092), channel_id=1, source_target_pairs={{0,8},{2,10},{4,12},{6,14},{8,0},{10,2},{12,4},{14,6},{16,24},{18,... | collective-permute-start | bytes 786440 | tf_op jit(solution)/shard_map/ppermute | solution.py:34
  713.0 76.6 %all-to-all-start.5 = ((bf16[16,512,128]{2,1,0:T(8,128)(2,1)}), bf16[16,512,128]{2,1,0:T(8,128)(2,1)S(1)}, u32[]{:S(2)}, u32[]{:S(2)}) async-start(bf16[16,512,128]{2,1,0:T(8,128)(2,1)} %pad_maximum_fusion.2), calls=%async_computation.5 | async-start | bytes 4194304 | tf_op jit(solution)/shard_map/all_to_all | solution.py:206
  746.0 14.3 %collective-permute-start.102 = (f32[304,128]{1,0:T(8,128)}, f32[304,128]{1,0:T(8,128)}, u32[]{:S(2)}, u32[]{:S(2)}) collective-permute-start(f32[304,128]{1,0:T(8,128)} %pad_maximum_fusion.22), channel_id=1, source_target_pairs={{0,2},{2,0},{4,6},{6,4},{8,10},{10,8},{12,14},{14,12},{16,18},{18,... | collective-permute-start | bytes 466952 | tf_op jit(solution)/shard_map/ppermute | solution.py:34
  747.8 21.6 %collective-permute-start.93 = (bf16[64,2048]{1,0:T(8,128)(2,1)}, bf16[64,2048]{1,0:T(8,128)(2,1)}, u32[]{:S(2)}, u32[]{:S(2)}) collective-permute-start(bf16[64,2048]{1,0:T(8,128)(2,1)} %add_convert_fusion.5), channel_id=1, source_target_pairs={{0,1},{1,0},{2,3},{3,2},{4,5},{5,4},{6,7},{7,6},{8,9},{9,8},{10,11... | collective-permute-start | bytes 786440 | tf_op jit(solution)/shard_map/ppermute | solution.py:38
  766.8 20.6 %collective-permute-start.101 = (f32[64,2048]{1,0:T(8,128)}, f32[64,2048]{1,0:T(8,128)S(1)}, u32[]{:S(2)}, u32[]{:S(2)}) collective-permute-start(f32[64,2048]{1,0:T(8,128)} %fusion.29), channel_id=1, source_target_pairs={{0,1},{1,0},{2,3},{3,2},{4,5},{5,4},{6,7},{7,6},{8,9},{9,8},{10,11... | collective-permute-start | bytes 1572872 | tf_op jit(solution)/shard_map/ppermute | solution.py:38
  (128 other events, 1367.9 us)

commit v3 on v2

--- a/solution.py
+++ b/solution.py
@@ -53,17 +53,6 @@
     apart = blocks ^ lax.axis_index("seq")
     flip = lax.axis_index("head").astype(jnp.int32)
     return jnp.concatenate([(apart % 4) * 4 + apart // 4, flip[None]])
-
-
-def exchanged(blocks):
-    groups = [[4 * z + j for j in range(4)] for z in range(4)]
-    return lax.all_to_all(
-        blocks, "seq", split_axis=0, concat_axis=0, tiled=True, axis_index_groups=groups
-    )
-
-
-def to_all(value):
-    return jnp.broadcast_to(value[None], (4,) + value.shape)
 
 
 def gather_z(rows, zs=ALL):
@@ -208,7 +197,7 @@
 
 def in_order(parts, place):
     count = parts[0].shape[0]
-    return tuple(jnp.take(part, place[:count], axis=0) for part in parts)
+    return tuple(jnp.take(part, place[:count], axis=0, mode="clip") for part in parts)
 
 
 def stream_order(parts, place):
@@ -233,13 +222,16 @@
     return value + across(value, 1) + across(value, 2) + across(value, 3)
 
 
-def sum_stream(value):
-    count = lax.axis_size("seq")
-    if not near(count):
+def sum_plane(value):
+    if not near(lax.axis_size("seq")):
         return lax.psum(value, "seq")
-    for offset in (1, 2, 4, 8):
-        value = value + across(value, offset)
-    return value
+    return value + across(value, 1) + across(value, 2) + across(value, 3)
+
+
+def sum_column(value):
+    if not near(lax.axis_size("seq")):
+        return value
+    return value + across(value, 4) + across(value, 8) + across(value, 12)
 
 
 def to_slices(blocks):
@@ -325,7 +317,7 @@
     return lane(jnp.broadcast_to(row, (LANES, LANES)).T, 0)
 
 
-CUM, RATE, BEGIN, LOG, SOFT = 0, 1, 2, 3, 4
+CUM, RATE, BEGIN, LOG, SOFT, START = 0, 1, 2, 3, 4, 5
 
 
 def chunk_masks(width, first):
@@ -357,10 +349,11 @@
     return grad * s * (1.0 + z * (1.0 - s))
 
 
-def forward_kernel(group, key_width, place_ref, *refs):
+def forward_kernel(group, key_width, mark_lane, place_ref, *refs):
     mine_refs, theirs_refs, refs = refs[:group], refs[group : 2 * group], refs[2 * group :]
-    (start_ref, taps_ref, head_ref, core_ref, square_ref, z_ref, q_ref, k_ref, v_ref, col_ref) = refs[:10]
-    inv_ref, invk_ref, state_ref, new_ref, carry, ext = refs[10:]
+    mine_extra, theirs_extra, refs = refs[:group], refs[group : 2 * group], refs[2 * group :]
+    (taps_ref, head_ref, core_ref, square_ref, z_ref, q_ref, k_ref, v_ref, col_ref) = refs[:9]
+    inv_ref, invk_ref, state_ref, new_ref, carry, ext = refs[9:]
     step = pl.program_id(0)
     width = core_ref.shape[1]
     wide = z_ref.shape[2]
@@ -383,7 +376,9 @@
         ext[i, 8 : 8 + width] = pre
         if i + 1 < group:
             ext[i + 1, 0:8] = pre[width - 8 :]
-        start = start_ref[i][:, 0:1]
+        marks = whole_chunk(mine_extra[i], theirs_extra[i], 0, flip).astype(f32)
+        first = ((step * group + i) * width).astype(f32)
+        start = lane(marks, mark_lane) * 128.0 + lane(marks, mark_lane + 1) - first
         z = taps_ref[0:1] * pre
         for offset in range(1, 4):
             valid = jnp.where(token - offset >= start, 1.0, 0.0)
@@ -400,7 +395,7 @@
         log_decay = own_a * (jnp.maximum(soft, 0.0) + jnp.log1p(jnp.exp(-jnp.abs(soft))))
         cum = lane(exact_sum(triangle, in_lanes(width, log_decay)), 0)
         begin = jnp.where(start < 0.0, jnp.exp(cum), 0.0)
-        cols = in_lanes(width, cum, rate, begin, log_decay, soft)
+        cols = in_lanes(width, cum, rate, begin, log_decay, soft, start)
         col_ref[i] = cols
         rows = cols.T
         fading, strict, last = fade(width, cols, rows, start)
@@ -471,26 +466,30 @@
     lax.fori_loop(0, count, step, 0, unroll=4)
 
 
-def backward_kernel(group, key_width, value_width, place_ref, *refs):
+def backward_kernel(group, low, key_width, value_width, place_ref, *refs):
     placed, refs = refs[: 4 * group], refs[4 * group :]
     mine_refs, theirs_refs = placed[:group], placed[group : 2 * group]
     grad_mine, grad_theirs = placed[2 * group : 3 * group], placed[3 * group :]
-    start_ref, taps_ref, head_ref, gain_ref, inv_core_ref, dots_ref = refs[:6]
-    core_ref, z_ref, q_ref, k_ref, v_ref, col_ref, inv_ref, invk_ref, state_ref, new_ref = refs[6:16]
-    out_mine, out_theirs, sum_ref, thin_ref, carry, ext = refs[16:]
+    taps_ref, head_ref, gain_ref, inv_core_ref, dots_ref = refs[:5]
+    core_ref, z_ref, q_ref, k_ref, v_ref, col_ref, inv_ref, invk_ref, state_ref, new_ref = refs[5:15]
+    pull_in, edge_in, sum_in, pair_ref, rest_ref, thin_ref, pull_ref, edge_ref, sum_ref = refs[15:24]
+    carry, ext = refs[24:]
     step = pl.program_id(0)
     width = core_ref.shape[1]
     half = width // 2
     wide = z_ref.shape[2]
-    chunks = place_ref.shape[0] - 1
-    flip = place_ref[chunks]
-    base_chunk = chunks - group * (step + 1)
+    chunks = place_ref.shape[0] - 3
+    flip, apart = place_ref[chunks], place_ref[chunks + 2]
+    steps = pl.num_programs(0)
+    base_chunk = low + group * (steps - 1 - step)
+    here = group * (steps - 1 - step)
 
     @pl.when(step == 0)
     def _():
-        carry[...] = jnp.zeros_like(carry)
-        ext[...] = jnp.zeros_like(ext)
-        sum_ref[...] = jnp.zeros_like(sum_ref)
+        carry[...] = pull_in[...]
+        sum_ref[...] = sum_in[...]
+        for offset in range(3):
+            ext[offset, 0, 0:8] = edge_in[offset]
 
     for offset in range(3):
         ext[offset, group - 1, width : width + 8] = ext[offset, 0, 0:8]
@@ -503,7 +502,7 @@
     xs = [whole_chunk(mine_refs[i], theirs_refs[i], 0, flip) for i in every]
     qs, ks = [q_ref[i] for i in every], [k_ref[i] for i in every]
     cols = [col_ref[i] for i in every]
-    starts = [start_ref[i][:, 0:1] for i in every]
+    starts = [lane(c, START) for c in cols]
     rates, begins = [lane(c, RATE) for c in cols], [lane(c, BEGIN) for c in cols]
     fades = [fade(width, cols[i], cols[i].T, starts[i]) for i in every]
     query_key = [dot(qs[i], ks[i], NT) for i in every]
@@ -532,6 +531,7 @@
         pulls[i], grad_news[i] = pull, att_grads[i] + back
         pull = begins[i][width - 1 :] * pull + bases[i] - dot3(invk_ref[i], back, TN)
     carry[...] = pull
+    pull_ref[...] = pull
     grad_rhs = [dot3(inv_ref[i], grad_news[i], TN) for i in every]
     grad_atts = [dot3(grads[i], new_ref[i], NT) for i in every]
     lower_fades = [jnp.where(fades[i][1], dot(ks[i], ks[i], NT) * fades[i][0], 0.0) for i in every]
@@ -583,7 +583,7 @@
         log_decay, soft = lane(cols[i], LOG), lane(cols[i], SOFT)
         grad_decay = grad_log * own_a * jax.nn.sigmoid(soft)
         thin = in_lanes(width, grad_decay, grad_rate * rate * (1.0 - rate))
-        thin_ref[pl.ds(base_chunk + i, 1)] = thin.T[None, 0:8]
+        thin_ref[pl.ds(here + i, 1)] = thin.T[None, 0:8]
         sum_ref[5:6, :LANES] += jnp.sum(
             in_lanes(width, grad_log * log_decay, grad_decay), axis=0, keepdims=True
         )
@@ -614,11 +614,53 @@
             moved = ext[offset - 1, i, offset : offset + width]
             grad_pre = grad_pre + taps_ref[offset : offset + 1] * moved
             sum_ref[offset : offset + 1] += jnp.sum(pre * moved, axis=0, keepdims=True)
-        out = jnp.concatenate([grad_pre, grad_gates[i], thins[i]], axis=1)
-        place = place_ref[base_chunk + i]
-        mine, theirs = halves_of(out[:half], out[half:], flip)
-        out_mine[place] = mine.astype(bf16)
-        out_theirs[place] = theirs.astype(bf16)
+        grad_pre = grad_pre.astype(bf16)
+        for tile in range(pair_ref.shape[0]):
+            pair_ref[tile ^ apart, i] = grad_pre[:, tile * LANES : (tile + 1) * LANES]
+        rest = [grad_pre[:, 2 * key_width :], grad_gates[i].astype(bf16), thins[i].astype(bf16)]
+        rest_ref[i] = jnp.concatenate(rest, axis=1)
+    for offset in range(3):
+        edge_ref[offset] = ext[offset, 0, 0:8]
+
+
+def collect_kernel(halves, place_ref, *refs):
+    refs, (out_mine, out_theirs) = list(refs[:-2]), refs[-2:]
+    blocks, rows = out_mine.shape[:2]
+    flip = place_ref[blocks]
+    size = blocks // len(halves)
+    for half, columns in enumerate(halves):
+        parts = [[refs.pop(0) for _ in range(count)] for count in columns]
+        for i in range(size):
+            place = place_ref[half * size + i]
+            at = 0
+            for tiles in parts:
+                total = tiles[0][i]
+                if len(tiles) > 1:
+                    total = sum((tile[i].astype(f32) for tile in tiles[1:]), total.astype(f32))
+                mine, theirs = halves_of(total[:rows], total[rows:], flip)
+                out_mine[place, :, at : at + total.shape[1]] = mine.astype(bf16)
+                out_theirs[place, :, at : at + total.shape[1]] = theirs.astype(bf16)
+                at += total.shape[1]
+
+
+def collect(place, halves, rows):
+    arrays = [array for half in halves for parts in half for array in parts]
+    columns = sum(parts[0].shape[2] for parts in halves[0])
+    blocks = sum(half[0][0].shape[0] for half in halves)
+    out = shape_of(blocks, rows, columns, dtype=bf16)
+    return pl.pallas_call(
+        functools.partial(collect_kernel, [[len(parts) for parts in half] for half in halves]),
+        grid_spec=pltpu.PrefetchScalarGridSpec(
+            num_scalar_prefetch=1,
+            grid=(1,),
+            in_specs=[resident(array) for array in arrays],
+            out_specs=[resident(out), resident(out)],
+        ),
+        out_shape=[out, out],
+        compiler_params=params(),
+        cost_estimate=cost(4.0),
+        name="collect",
+    )(place, *arrays)
 
 
 def stepped(group, array, order):
@@ -632,10 +674,10 @@
     return pl.BlockSpec(array.shape, lambda i, place: zeros)
 
 
-def placed_blocks(group, array, order):
+def placed_blocks(group, array, order, lanes=None):
     def spec(c):
-        shape = (1,) + array.shape[1:]
-        return pl.BlockSpec(shape, lambda i, place: (place[group * order(i) + c], 0, 0))
+        shape = (1, array.shape[1], array.shape[2] if lanes is None else LANES)
+        return pl.BlockSpec(shape, lambda i, place: (place[group * order(i) + c], 0, lanes or 0))
 
     return [spec(c) for c in range(group)]
 
@@ -656,8 +698,9 @@
     return pltpu.CompilerParams(vmem_limit_bytes=VMEM_LIMIT)
 
 
-def recurrence_forward(place, proj, start, taps, head, key_width):
+def recurrence_forward(place, proj, gathered, taps, head, key_width, mark_lane):
     mine, theirs = proj
+    extra = gathered[0].shape[2] // LANES - 1
     chunks, width, wide = mine.shape[0], 2 * mine.shape[1], taps.shape[1]
     value = wide - 2 * key_width
     group = chunk_group(chunks, 8)
@@ -678,13 +721,15 @@
     out_specs = [stepped(group, a, order) for a in outs]
     out_specs[1] = resident(outs[1])
     return pl.pallas_call(
-        functools.partial(forward_kernel, group, key_width),
+        functools.partial(forward_kernel, group, key_width, mark_lane),
         grid_spec=pltpu.PrefetchScalarGridSpec(
             num_scalar_prefetch=1,
             grid=(chunks // group,),
             in_specs=placed_blocks(group, mine, order)
             + placed_blocks(group, theirs, order)
-            + [stepped(group, start, order), resident(taps), resident(head)],
+            + placed_blocks(group, gathered[0], order, extra)
+            + placed_blocks(group, gathered[1], order, extra)
+            + [resident(taps), resident(head)],
             out_specs=out_specs,
             scratch_shapes=[
                 pltpu.VMEM((key_width, value), f32),
@@ -695,7 +740,12 @@
         compiler_params=params(),
         cost_estimate=cost(28.0 * chunks / 16),
         name="delta_forward",
-    )(place, *([mine] * group), *([theirs] * group), start, taps, head)
+    )(
+        place,
+        *[part for part in (mine, theirs, *gathered) for _ in range(group)],
+        taps,
+        head,
+    )
 
 
 def gate_spec(proj, wide):
@@ -753,32 +803,38 @@
     )(place, grad[0], grad[1], core, mine, theirs, inv, gain)
 
 
-def recurrence_backward(place, proj, grad, start, taps, head, gain, inv, dots, kept, sizes):
+def recurrence_backward(place, proj, grad, taps, head, gain, inv, dots, kept, sizes, state, part):
     key_width, value_width = sizes
     chunks, wide = proj[0].shape[0], taps.shape[1]
     width = 2 * proj[0].shape[1]
     value = wide - 2 * key_width
-    group = chunk_group(chunks, 2)
-    steps = chunks // group
-    order = lambda i: steps - 1 - i
+    half = chunks // 2
+    group = chunk_group(half, 2)
+    steps = half // group
+    low = half * part
+    order = lambda i: low // group + steps - 1 - i
+    local = lambda i: steps - 1 - i
+    if state is None:
+        state = [jnp.zeros((key_width, value), f32), jnp.zeros((3, 8, wide), f32), jnp.zeros((8, wide), f32)]
+    tiles = 2 * key_width // LANES
     outs = [
-        shape_of(*proj[0].shape, dtype=bf16),
-        shape_of(*proj[1].shape, dtype=bf16),
-        shape_of(8, wide),
-        shape_of(chunks, 8, width),
-    ]
-    return pl.pallas_call(
-        functools.partial(backward_kernel, group, key_width, value_width),
+        shape_of(tiles, half, width, LANES, dtype=bf16),
+        shape_of(half, width, 3 * LANES, dtype=bf16),
+        shape_of(half, 8, width),
+    ] + [shape_of(*part.shape) for part in state]
+    pair_spec = pl.BlockSpec((tiles, group, width, LANES), lambda i, place: (0, local(i), 0, 0))
+    *results, pull, edge, sums = pl.pallas_call(
+        functools.partial(backward_kernel, group, low, key_width, value_width),
         grid_spec=pltpu.PrefetchScalarGridSpec(
             num_scalar_prefetch=1,
             grid=(steps,),
             in_specs=[
                 spec for part in (*proj, *grad) for spec in placed_blocks(group, part, order)
             ]
-            + [stepped(group, start, order)]
             + [resident(a) for a in (taps, head, gain, inv, dots)]
-            + [stepped(group, a, order) for a in kept],
-            out_specs=[resident(a) for a in outs],
+            + [stepped(group, a, order) for a in kept]
+            + [resident(a) for a in state],
+            out_specs=[pair_spec, stepped(group, outs[1], local)] + [resident(a) for a in outs[2:]],
             scratch_shapes=[
                 pltpu.VMEM((key_width, value), f32),
                 pltpu.VMEM((3, group, width + 8, wide), f32),
@@ -786,41 +842,94 @@
         ),
         out_shape=outs,
         compiler_params=params(),
-        cost_estimate=cost(36.0 * chunks / 16),
+        cost_estimate=cost(18.0 * chunks / 16),
         name="delta_backward",
     )(
         place,
         *[part for part in (*proj, *grad) for _ in range(group)],
-        start,
         taps,
         head,
         gain,
         inv,
         dots,
         *kept,
+        *state,
     )
-
-
-def weight_kernel(hidden_mine, hidden_theirs, grad_mine, grad_theirs, weight_ref, pair_ref, rest_ref, sum_ref):
+    return results, [pull, edge, sums]
+
+
+def assemble_kernel(heads, parts, place_ref, *refs):
+    part_refs, (rest_ref, extra_ref, out_ref, own_ref) = refs[:parts], refs[parts:]
+    blocks, rows = extra_ref.shape[:2]
+    head, apart = place_ref[blocks + 1], place_ref[blocks + 2]
+    size = out_ref.shape[0] // blocks
+    for part in range(parts):
+        wide = part_refs[part].shape[1]
+        at = pl.multiple_of((part ^ apart) * wide, LANES)
+        out_ref[:, pl.ds(at, wide)] = part_refs[part][...]
+    at = sum(ref.shape[1] for ref in part_refs)
+    out_ref[:, at : at + rest_ref.shape[1]] = rest_ref[...]
+    at += rest_ref.shape[1]
+    own = part_refs[0].shape[1]
+    own_ref[:, :own] = part_refs[0][...]
+    own_ref[:, own : own + rest_ref.shape[1]] = rest_ref[...]
+    own += rest_ref.shape[1]
+    row, col = square_iota(LANES)
+    fold = -(-size // rows)
+    for block in range(blocks):
+        x = extra_ref[place_ref[block]]
+        for piece in range(fold):
+            base = 2 * heads * piece + head
+            pick = ((row == base) & (col == 0)) | ((row == base + heads) & (col == 1))
+            thin = dot(x, jnp.where(pick, 1.0, 0.0).astype(bf16), NN).astype(bf16)
+            first = block * size + piece * rows
+            thin = thin[: min(rows, size)]
+            out_ref[first : first + min(rows, size), at : at + LANES] = thin
+            own_ref[first : first + min(rows, size), own : own + LANES] = thin
+
+
+def assemble(place, parts, rest, extra, heads):
+    model = rest.shape[0]
+    columns = sum(part.shape[1] for part in parts) + rest.shape[1] + LANES
+    own = parts[0].shape[1] + rest.shape[1] + LANES
+    lanes = extra.shape[2] // LANES - 1
+    return pl.pallas_call(
+        functools.partial(assemble_kernel, heads, len(parts)),
+        grid_spec=pltpu.PrefetchScalarGridSpec(
+            num_scalar_prefetch=1,
+            grid=(1,),
+            in_specs=[resident(part) for part in (*parts, rest)]
+            + [pl.BlockSpec(extra.shape[:2] + (LANES,), lambda i, place: (0, 0, lanes))],
+            out_specs=[
+                pl.BlockSpec((model, columns), lambda i, place: (0, 0)),
+                pl.BlockSpec((model, own), lambda i, place: (0, 0)),
+            ],
+        ),
+        out_shape=[shape_of(model, columns, dtype=bf16), shape_of(model, own, dtype=bf16)],
+        compiler_params=params(),
+        cost_estimate=cost(5.0),
+        name="assemble",
+    )(place, *parts, rest, extra)
+
+
+def weight_kernel(hidden_mine, hidden_theirs, grad_mine, grad_theirs, weight_ref, out_ref, sum_ref):
     total = dot(hidden_mine[...], grad_mine[...], TN) + dot(hidden_theirs[...], grad_theirs[...], TN)
     summed = jnp.sum(total * weight_ref[...].astype(f32), axis=1, keepdims=True)
     sum_ref[...] = jnp.broadcast_to(summed, sum_ref.shape)
     low = total.astype(bf16)
-    size, tiles = pair_ref.shape[2], pair_ref.shape[0]
-    for block in range(pair_ref.shape[1]):
+    size = out_ref.shape[2]
+    for block in range(out_ref.shape[0]):
         rows = low[block * size : (block + 1) * size]
-        for tile in range(tiles):
-            pair_ref[tile, block] = rows[:, tile * LANES : (tile + 1) * LANES]
-        for tile in range(rest_ref.shape[1] // size):
-            at = (tiles + tile) * LANES
-            rest_ref[block, tile * size : (tile + 1) * size] = rows[:, at : at + LANES]
-
-
-def weight_gradient(hidden, grad, weight, count, tiles, rest):
+        for tile in range(out_ref.shape[1]):
+            out_ref[block, tile] = rows[:, tile * LANES : (tile + 1) * LANES]
+
+
+def weight_gradient(hidden, grad, weight, count):
     tokens, columns = grad[0].shape
     model = weight.shape[0]
     size = model // count
     step = 4 if count % 4 == 0 else 1
+    tiles = columns // LANES - 1
     part = pl.BlockSpec((tokens, step * size), lambda i: (0, i))
     whole = pl.BlockSpec((tokens, columns), lambda i: (0, 0))
     return pl.pallas_call(
@@ -828,43 +937,65 @@
         grid=(count // step,),
         in_specs=[part, part, whole, whole, pl.BlockSpec((step * size, columns), lambda i: (i, 0))],
         out_specs=[
-            pl.BlockSpec((tiles, step, size, LANES), lambda i: (0, i, 0, 0)),
-            pl.BlockSpec((step, rest * size, LANES), lambda i: (i, 0, 0)),
+            pl.BlockSpec((step, tiles, size, LANES), lambda i: (i, 0, 0, 0)),
             pl.BlockSpec((step * size, LANES), lambda i: (i, 0)),
         ],
-        out_shape=[
-            shape_of(tiles, count, size, LANES, dtype=bf16),
-            shape_of(count, rest * size, LANES, dtype=bf16),
-            shape_of(model, LANES),
-        ],
+        out_shape=[shape_of(count, tiles, size, LANES, dtype=bf16), shape_of(model, LANES)],
         compiler_params=params(),
-        cost_estimate=cost(14.0),
+        cost_estimate=cost(2.0 * tiles),
         name="weight_gradient",
     )(*hidden, *grad, weight)
 
 
-def unpack_kernel(heads, back_ref, query_ref, key_ref, value_ref, gate_ref, out_ref):
-    size = query_ref.shape[0]
-    for device in range(back_ref.shape[0]):
-        tiles = [back_ref[device, at : at + size].astype(f32) for at in range(0, 4 * size, size)]
+def unpack_kernel(tiles_ref, query_ref, key_ref, value_ref, gate_ref):
+    for device in range(tiles_ref.shape[0]):
         head, member = device // 4, device % 4
-        pair_ref = query_ref if member < 2 else key_ref
+        out_ref = query_ref if member < 2 else key_ref
         at = (2 * head + member % 2) * LANES
-        pair_ref[:, at : at + LANES] = tiles[0]
+        out_ref[:, at : at + LANES] = tiles_ref[device, 0].astype(f32)
         at = device * LANES
-        value_ref[:, at : at + LANES] = tiles[1]
-        gate_ref[:, at : at + LANES] = tiles[2]
-        out_ref[at : at + LANES] = tiles[3]
-
-
-def unpack_mixer(back, heads, shapes):
+        value_ref[:, at : at + LANES] = tiles_ref[device, 1].astype(f32)
+        gate_ref[:, at : at + LANES] = tiles_ref[device, 2].astype(f32)
+
+
+def unpack_mixer(tiles, shapes):
     return pl.pallas_call(
-        functools.partial(unpack_kernel, heads),
+        unpack_kernel,
         out_shape=[shape_of(*shape) for shape in shapes],
         compiler_params=params(),
         cost_estimate=cost(4.0),
         name="unpack_mixer",
-    )(back)
+    )(tiles)
+
+
+def unpack_ffn_kernel(ff_slice, tiles_ref, gate_ref, up_ref, down_ref, out_ref):
+    size = gate_ref.shape[0]
+    whole = ff_slice // LANES * LANES
+    last = ff_slice - whole
+    gates, ups = [], []
+    for device in range(tiles_ref.shape[0]):
+        full = [tiles_ref[device, at : at + size].astype(f32) for at in range(0, 2 * whole // LANES * size, size)]
+        end = 2 * whole // LANES * size
+        both = tiles_ref[device, end : end + size].astype(f32)
+        gates += full[: len(full) // 2] + [both[:, :last]]
+        ups += full[len(full) // 2 :] + [both[:, LANES // 2 : LANES // 2 + last]]
+        end += size
+        at = device * ff_slice
+        down_ref[at : at + ff_slice] = tiles_ref[device, end : end + ff_slice].astype(f32)
+        end += ff_slice
+        out_ref[device * LANES : (device + 1) * LANES] = tiles_ref[device, end : end + LANES].astype(f32)
+    gate_ref[...] = jnp.concatenate(gates, axis=1)
+    up_ref[...] = jnp.concatenate(ups, axis=1)
+
+
+def unpack_ffn(tiles, ff_slice, shapes):
+    return pl.pallas_call(
+        functools.partial(unpack_ffn_kernel, ff_slice),
+        out_shape=[shape_of(*shape) for shape in shapes],
+        compiler_params=params(),
+        cost_estimate=cost(6.0),
+        name="unpack_ffn",
+    )(tiles)
 
 
 def norm_back(grad, values, inv, gain):
@@ -929,13 +1060,12 @@
     cot_rows = own_rows(cotangent)
     own_starts = own_rows(doc_start)
     coarse = own_starts // 128
+    fold = -(-d_rows // rows)
+    thin_weights = widened(jnp.concatenate([w_decay, w_rate], axis=1), fold * rows, 0)
+    mark_lane = 2 * heads * fold
     extra = jnp.concatenate(
-        [
-            w_decay.reshape(rows, -1),
-            w_rate.reshape(rows, -1),
-            coarse.astype(bf16)[:, None],
-            (own_starts - 128 * coarse).astype(bf16)[:, None],
-        ],
+        [thin_weights[at * rows : (at + 1) * rows] for at in range(fold)]
+        + [coarse.astype(bf16)[:, None], (own_starts - 128 * coarse).astype(bf16)[:, None]],
         axis=1,
     )
     extended = jnp.concatenate([normed_one, widened(extra, LANES, 1)], axis=1)
@@ -963,6 +1093,17 @@
         ],
         axis=1,
     )
+    def own_taps(taps):
+        return pick(taps, head_id * key_width, key_width, 1)
+
+    taps_v = widened(pick(conv_value, me * slice_width, slice_width, 1), LANES, 1)
+    taps = jnp.concatenate([own_taps(conv_query), own_taps(conv_key), taps_v], axis=1)
+    taps = widened(taps, 8, 0)
+    head = jnp.concatenate([-jnp.exp(pick(a_log, head_id, 1, 0)), pick(dt_bias, head_id, 1, 0)])
+    head = jnp.broadcast_to(widened(head, LANES, 0)[None], (8, LANES))
+    own_gain = widened(pick(out_gain, member * slice_width, slice_width, 0), LANES, 0)
+    own_gain = jnp.broadcast_to(own_gain[None], (8, LANES))
+
     v_blocks = w_value.reshape(d_rows, count, slice_width)
     o_blocks = w_outgate.reshape(d_rows, count, slice_width)
     if aligned:
@@ -970,12 +1111,15 @@
             [w_query.reshape(d_rows, heads, 2, LANES), w_key.reshape(d_rows, heads, 2, LANES)],
             axis=2,
         ).reshape(d_rows, count, LANES)
-        qk = jnp.concatenate([qk, v_blocks, o_blocks], axis=2)
-        own, packed, qk = after((gather_z(extended), packed, qk))
-        sides = gather_xy(own)
+        rest = jnp.concatenate([v_blocks, o_blocks], axis=2)
+        own, packed, qk, rest, taps, head, own_gain = after(
+            (gather_z(extended), packed, qk, rest, taps, head, own_gain)
+        )
+        sides, qk = after((gather_xy(own), to_slices(qk)))
         cot_own = gather_z(after(cot_rows, own[1]), PAIR)
-        mixed = to_slices(qk)
-        s_parts = list(exchanged(to_all(mixed[:, :LANES]))) + [mixed[:, LANES:]]
+        s_parts = [qk] + [across(qk, offset) for offset in (1, 2, 3)]
+        sides, s_parts, rest = after((sides, s_parts, rest))
+        s_rest = to_slices(rest)
     else:
         groups = [[j * members + m for m in range(members)] for j in range(heads)]
 
@@ -985,40 +1129,18 @@
 
         sides = gather_xy(gather_z(extended))
         cot_own = gather_z(cot_rows, PAIR)
-        s_parts = [
-            whole_head(w_query),
-            whole_head(w_key),
-            widened(to_slices(v_blocks), LANES, 1),
-            widened(to_slices(o_blocks), LANES, 1),
-        ]
-
-    def own_taps(taps):
-        return pick(taps, head_id * key_width, key_width, 1)
-
-    taps_v = widened(pick(conv_value, me * slice_width, slice_width, 1), LANES, 1)
-    taps = jnp.concatenate([own_taps(conv_query), own_taps(conv_key), taps_v], axis=1)
-    taps = widened(taps, 8, 0)
-    head = jnp.concatenate([-jnp.exp(pick(a_log, head_id, 1, 0)), pick(dt_bias, head_id, 1, 0)])
-    head = jnp.broadcast_to(widened(head, LANES, 0)[None], (8, LANES))
-    own_gain = widened(pick(out_gain, member * slice_width, slice_width, 0), LANES, 0)
-    own_gain = jnp.broadcast_to(own_gain[None], (8, LANES))
+        s_parts = [whole_head(w_query), whole_head(w_key)]
+        s_rest = [widened(to_slices(part), LANES, 1) for part in (v_blocks, o_blocks)]
+        s_rest = jnp.concatenate(s_rest, axis=1)
 
     gathered = gather_end(gather_corner(sides))
-    extra = [part[:, :, model:] for part in gathered]
-    own_extra = extra[0] if near(count) else jnp.where(core_id == 0, extra[0], extra[1])
-    own_extra = jnp.take(own_extra, place[:count], axis=0)
-    thin = d_rows * heads // rows
-    s_decay = own_extra[:, :, :thin].reshape(model, heads)
-    s_rate = own_extra[:, :, thin : 2 * thin].reshape(model, heads)
-    marks = [part[:, :, 2 * thin : 2 * thin + 2].astype(f32) for part in extra]
-    marks = stream_order(marks, place)
-    starts = marks[..., 0] * 128.0 + marks[..., 1]
-    starts = starts - (jnp.arange(count, dtype=jnp.int32) * tok_rows).astype(f32)[:, None]
-    start_cols = jnp.broadcast_to(starts[:, :, None], (count, tok_rows, 8))
-    s_thin = jnp.concatenate([pick(s_decay, head_id, 1, 1), pick(s_rate, head_id, 1, 1)], axis=1)
-    s_mixer = jnp.concatenate(s_parts + [widened(s_thin, LANES, 1)], axis=1)
-    s_mixer, cot_own = after((s_mixer, cot_own))
-    s_longer = widened(s_mixer, model + LANES, 0)
+    own_extra = gathered[0]
+    if not near(count):
+        own_extra = jnp.where(core_id == 0, gathered[0], gathered[1])
+    ids = jnp.stack([head_id, member if aligned else 0 * member]).astype(jnp.int32)
+    place_ids = jnp.concatenate([place, ids])
+    s_mixer, s_own = assemble(place_ids, s_parts, s_rest, own_extra, heads)
+    s_own = s_own if aligned else s_mixer
 
     def blocks(parts):
         return tuple(part.reshape(-1, rows, part.shape[-1]) for part in parts)
@@ -1027,12 +1149,13 @@
         return tuple(part.reshape(-1, part.shape[-1]) for part in parts)
 
     longer_one = flat(gathered)
-    proj = blocks([mm(part, s_longer) for part in longer_one])
-    cot_sides = gather_xy(after(cot_own, s_mixer))
-    packed = all_to_all(after(packed, s_mixer))
-    core, square, *kept = recurrence_forward(place, proj, start_cols, taps, head, key_width)
-    core, cot_sides, packed = after((core, cot_sides, packed))
-    cot_parts = gather_corner(cot_sides)
+    proj = blocks([mm(part[:, :model], s_mixer) for part in longer_one])
+    packed = all_to_all(after(packed, s_rest))
+    core, square, *kept = recurrence_forward(
+        place, proj, gathered, taps, head, key_width, mark_lane
+    )
+    core, cot_own, packed = after((core, cot_own, packed))
+    cot_sides = gather_xy(cot_own)
     s_out = jnp.swapaxes(packed[:, ff_pack // LANES * d_rows :], 0, 1).reshape(-1, count * LANES)
     if LANES > w_out.shape[1]:
         s_out = jnp.swapaxes(
@@ -1046,18 +1169,18 @@
     inv_core = lax.rsqrt(sum_members(square, members) / value_width + 1e-5)
     gated = gate_forward(place, core, proj, inv_core, own_gain, wide)
     gated, ffn_parts[0] = after((gated, ffn_parts[0]))
-    cot_parts = after(cot_parts, gated)
-    partial, _ = scatter_begin(gated, s_out, NN)
+    partial, sent = scatter_begin(gated, s_out, NN)
     partial, ffn_parts[1:2] = after((partial, ffn_parts[1:2]))
+    cot_parts = gather_corner(after(cot_sides, sent))
     partial, _ = scatter_corner(partial)
     cot_all = gather_end(cot_parts)
     partial, ffn_parts[2:] = after((partial, ffn_parts[2:]))
     partial, _ = scatter_xy(partial)
     partial, down_parts = after((partial, down_parts))
-    s_ffn, s_down = with_slices(s_ffn, ffn_parts, 1), with_slices(s_down, down_parts, 0)
     middle = stream + scatter_z(partial, rows)[0]
     inv_two = lax.rsqrt(jnp.mean(middle * middle, axis=-1, keepdims=True) + 1e-6)
     two_own = gather_z((middle * inv_two * second_gain).astype(bf16), PAIR)
+    s_ffn, s_down = with_slices(s_ffn, ffn_parts, 1), with_slices(s_down, down_parts, 0)
     grad_inner = [mm_nt(part, s_down) for part in flat(cot_all)]
     two_own = after(two_own, grad_inner)
     hidden_two = flat(gather_end(gather_corner(gather_xy(two_own))))
@@ -1105,81 +1228,57 @@
     down_tiles = jnp.swapaxes(
         g_down[:ff_slice].astype(bf16).reshape(ff_slice, count, -1), 0, 1
     )
-    g_ffn = jnp.concatenate(
-        [as_tiles(g_ffn.astype(bf16), count), widened(down_tiles, LANES, 2)], axis=1
-    )
-    g_ffn, mixer_parts, grad_second = after((g_ffn, mixer_parts, grad_second))
+    ffn_tiles = [as_tiles(g_ffn.astype(bf16), count), widened(down_tiles, LANES, 2)]
+    ffn_tiles, mixer_parts, grad_second = after((ffn_tiles, mixer_parts, grad_second))
     grad_mixer = gather_end(mixer_parts)
-    g_ffn = all_to_all(g_ffn)
     ffn_out, _ = scatter_corner(after(ffn_out, grad_mixer[0]))
     grad_mixer = flat(grad_mixer)
     grad_gated = blocks([mm_nt(part, s_out) for part in grad_mixer])
+    grad_gated, ffn_out = after((grad_gated, ffn_out))
     dots = sum_members(gate_dots(place, grad_gated, core, proj, inv_core, own_gain, wide), members)
     g_out = sum(mm_tn(*pair) for pair in zip(flat(gated), grad_mixer))
-    dots, ffn_out, g_out = lax.optimization_barrier((dots, ffn_out, g_out))
+    out_tiles = jnp.swapaxes(g_out.astype(bf16)[:slice_width].reshape(slice_width, count, -1), 0, 1)
+    g_ffn = jnp.concatenate(ffn_tiles + [widened(out_tiles, LANES, 2)], axis=1)
+    dots, ffn_out, g_ffn = lax.optimization_barrier((dots, ffn_out, g_ffn))
+    g_ffn = all_to_all(g_ffn)
     ffn_out, _ = scatter_xy(ffn_out)
-    *grad_proj, sums, thin_rows = recurrence_backward(
-        place,
-        proj,
-        grad_gated,
-        start_cols,
-        taps,
-        head,
-        own_gain,
-        inv_core,
-        dots,
-        [core] + kept,
-        (key_width, value_width),
-    )
-    g_pairs, g_rest, g_sums = weight_gradient(
-        longer_one, flat(grad_proj), s_mixer, count, 2 * key_width // LANES, 2
-    )
-    partial, _ = scatter_begin(after(grad_proj, g_pairs), s_mixer, NT)
+    pairs = 2 * key_width // LANES
+    state, halves, thin_rows = None, [None, None], [None, None]
+    for part in (1, 0):
+        (pair, rest, thin_rows[part]), state = recurrence_backward(
+            place_ids,
+            proj,
+            grad_gated,
+            taps,
+            head,
+            own_gain,
+            inv_core,
+            dots,
+            [core] + kept,
+            (key_width, value_width),
+            state,
+            part,
+        )
+        if part == 0:
+            pair, halves[1], ffn_out = after((pair, halves[1], ffn_out))
+        if aligned:
+            tiles = [[pair[0]] + [across(pair[offset], offset) for offset in (1, 2, 3)]]
+        else:
+            tiles = [[pair[tile]] for tile in range(pairs)]
+        halves[part] = tiles + [[rest]]
+    sums = state[2]
+    thin_rows = jnp.concatenate(thin_rows, axis=0)
+    grad_proj = collect(place, halves, rows)
+    grad_proj, g_ffn = after((grad_proj, g_ffn))
+    partial, sent_core = scatter_begin(grad_proj, s_own, NT)
     partial, sent = scatter_corner(partial)
-    ffn_out, _ = scatter_z(after(ffn_out, sent), rows, PAIR)
+    grad_proj = after(flat(grad_proj), sent, sent_core)
+    g_tiles, g_sums = weight_gradient(longer_one, grad_proj, s_own, count)
     partial, sent_xy = scatter_xy(partial)
-    grad_one, sent_z = scatter_z(partial, rows)
-    g_ffn, sums, thin_rows, grad_second = after((g_ffn, sums, thin_rows, grad_second), sent_z)
-    ffn_out = after(ffn_out, sent_z)
-    output = both_halves((middle + ffn_out).astype(bf16))
-    ff_rows = ff_pack // LANES * d_rows
-    gw_down = g_ffn[:, ff_rows:, : w_down.shape[1]].reshape(w_down.shape).astype(f32)
-
-    def joined(blocks):
-        return jnp.swapaxes(blocks, 0, 1).reshape(d_rows, -1).astype(f32)
-
-    gw_gate, gw_up = gate_and_up(from_tiles(g_ffn[:, :ff_rows], d_rows))
-    gw_gate, gw_up = joined(gw_gate[..., :ff_slice]), joined(gw_up[..., :ff_slice])
-
-    grad_input = both_halves(grad_middle + norm_back(grad_one, stream, inv_one, first_gain))
-
-    grad_first = after(g_sums, sent_z)[:, 0] / first_gain
+    ffn_out, _ = scatter_z(after(ffn_out, sent_xy), rows, PAIR)
     if aligned:
-        own = jnp.sum(exchanged(g_pairs.reshape(4, model, LANES)).astype(f32), axis=0)
-        out_tiles = jnp.swapaxes(g_out.astype(bf16).reshape(LANES, count, -1), 0, 1)
-        own = own.astype(bf16).reshape(count, d_rows, LANES)
-        back = all_to_all(jnp.concatenate([own, g_rest, out_tiles], axis=1))
-        shapes = [part.shape for part in (w_query, w_key, w_value, w_outgate, w_out)]
-        gw_query, gw_key, gw_value, gw_outgate, gw_out = unpack_mixer(back, heads, shapes)
-    else:
-
-        def in_columns(tiles):
-            return jnp.concatenate([tile.reshape(model, LANES) for tile in tiles], axis=1)
-
-        def summed_slices(part):
-            part = lax.psum_scatter(
-                part, "seq", scatter_dimension=1, tiled=True, axis_index_groups=groups
-            )
-            return joined(from_slices(part, d_rows))
-
-        out_tiles = g_out[:slice_width].astype(bf16).reshape(slice_width, count, -1)
-        gw_out = all_to_all(jnp.swapaxes(out_tiles, 0, 1)).reshape(w_out.shape).astype(f32)
-        half = key_width // LANES
-        gw_query = summed_slices(in_columns(g_pairs[:half]))
-        gw_key = summed_slices(in_columns(g_pairs[half:]))
-        rest = from_tiles(g_rest, d_rows).reshape(model, 2 * LANES)
-        gw_value = joined(from_slices(rest[:, :slice_width], d_rows))
-        gw_outgate = joined(from_slices(rest[:, LANES : LANES + slice_width], d_rows))
+        g_tiles = all_to_all(g_tiles)
+    grad_first = g_sums[:, 0] / first_gain
 
     def put(part, start, width, axis):
         shape = list(part.shape)
@@ -1187,7 +1286,6 @@
         return lax.dynamic_update_slice_in_dim(jnp.zeros(shape, f32), part, start, axis)
 
     g_taps = sums[: conv_query.shape[0]]
-
     pieces = [
         put(g_taps[:, :key_width], head_id * key_width, conv_query.shape[1], 1),
         put(g_taps[:, key_width : 2 * key_width], head_id * key_width, conv_key.shape[1], 1),
@@ -1207,7 +1305,7 @@
         grad_first,
     ]
 
-    def packed(parts):
+    def packed_up(parts):
         flat = jnp.concatenate([part.reshape(-1) for part in parts])
         return widened(flat, -(-flat.shape[0] // 1024) * 1024, 0).reshape(-1, LANES)
 
@@ -1218,11 +1316,55 @@
             at += part.size
         return out
 
-    merged = [packed(pieces), packed(shared)]
-    summed = sum_stream(jnp.concatenate(merged, axis=0))
+    merged = [packed_up(pieces), packed_up(shared)]
+    summed = sum_plane(jnp.concatenate(merged, axis=0))
+    grad_one, sent_z = scatter_z(partial, rows)
+    summed = sum_column(summed)
+    grad_one, summed = after((grad_one, summed))
     cut = merged[0].shape[0]
     small = unpacked(summed[:cut], pieces)
     total = unpacked(summed[cut:] + other_core(summed[cut:]), shared)
+    g_ffn, ffn_out = after((g_ffn, ffn_out), sent_z)
+    output = both_halves((middle + ffn_out).astype(bf16))
+    ff_rows = ff_pack // LANES * d_rows
+    down_end = ff_rows + ff_slice
+    if aligned:
+        shapes = [part.shape for part in (w_gate, w_up, w_down, w_out)]
+        gw_gate, gw_up, gw_down, gw_out = unpack_ffn(g_ffn, ff_slice, shapes)
+    else:
+        gw_down = g_ffn[:, ff_rows:down_end, : w_down.shape[1]].reshape(w_down.shape).astype(f32)
+        gw_out = g_ffn[:, down_end:, : w_out.shape[1]].reshape(w_out.shape).astype(f32)
+
+    def joined(blocks):
+        return jnp.swapaxes(blocks, 0, 1).reshape(d_rows, -1).astype(f32)
+
+    if not aligned:
+        gw_gate, gw_up = gate_and_up(from_tiles(g_ffn[:, :ff_rows], d_rows))
+        gw_gate, gw_up = joined(gw_gate[..., :ff_slice]), joined(gw_up[..., :ff_slice])
+
+    grad_input = both_halves(grad_middle + norm_back(grad_one, stream, inv_one, first_gain))
+
+    if aligned:
+        shapes = [part.shape for part in (w_query, w_key, w_value, w_outgate)]
+        gw_query, gw_key, gw_value, gw_outgate = unpack_mixer(g_tiles, shapes)
+    else:
+
+        def in_columns(start, end):
+            tiles = [g_tiles[:, tile].reshape(model, LANES) for tile in range(start, end)]
+            return jnp.concatenate(tiles, axis=1)
+
+        def summed_slices(part):
+            part = lax.psum_scatter(
+                part, "seq", scatter_dimension=1, tiled=True, axis_index_groups=groups
+            )
+            return joined(from_slices(part, d_rows))
+
+        half = key_width // LANES
+        gw_query = summed_slices(in_columns(0, half))
+        gw_key = summed_slices(in_columns(half, 2 * half))
+        rest = in_columns(2 * half, 2 * half + 2)
+        gw_value = joined(from_slices(rest[:, :slice_width], d_rows))
+        gw_outgate = joined(from_slices(rest[:, LANES : LANES + slice_width], d_rows))
 
     own_cols = blocks([pick(after(part, sent_z), me * d_rows, d_rows, 1) for part in longer_one])
     own_cols = stream_order(own_cols, place).astype(f32)

time: 804 us -> 767 us (0.954)
  local copies, waits for them, and re-layouts: 134 us -> 94.5 us
  other arithmetic: 60.4 us -> 34.4 us
  waiting for transfers between devices: 276 us -> 302 us
  Pallas kernels: 92.7 us -> 112 us
  matrix products: 79.2 us -> 67.7 us
    ppermute x92 -> x103, waiting for transfers between devices: 257 us -> 300 us  [across(): return lax.ppermute(value, 'seq', [(i, i ^ offset) for i in range(count)])]
    pallas_call x3 -> x7, Pallas kernels: 67.4 us -> 92.5 us  [the longest x2 41.5 us: recurrence_backward(): pl.pallas_call(functools.partial(backward_kernel, group, low, key_width,...]
    all_to_all x2 -> x0, waiting for transfers between devices: 15.2 us -> none  [exchanged(): lax.all_to_all(blocks, 'seq', split_axis=0, concat_axis=0, tiled=True, ax...]
    unnamed x224 -> x220, local copies, waits for them, and re-layouts: 46.6 us -> 33.1 us
    dot_general x16, matrix products: 34.3 us -> 23 us  [product(): lax.dot_general(part, right, (dims, ((), ())), preferred_element_type=f32)]
    slice x8 -> x2, local copies, waits for them, and re-layouts: 11.6 us -> 1.64 us  [the longest x1 1.56 us: on_device(): grad_first = g_sums[:, 0] / first_gain]
    ppermute x92 -> x103, starting transfers between devices: 121 us -> 115 us  [across(): return lax.ppermute(value, 'seq', [(i, i ^ offset) for i in range(count)])]
  transfers between devices with their start and end apart: 113 -> 123, of which waited for: 53 -> 49; matrix products, arithmetic and copies ran while one was open for 30% -> 21% of each run, Pallas kernels for 11% -> 14%
where the time goes in v3:
time: 767 us; the launch traced here: 760 us
  waiting for transfers between devices  302 us (39%)
  starting transfers between devices  146 us (19%)
  Pallas kernels  112 us (15%)
  local copies, waits for them, and re-layouts  94.5 us (12%)
  matrix products  67.7 us (9%)
  other arithmetic  34.4 us (4%)
    ppermute x103, waiting for transfers between devices, across(): return lax.ppermute(value, 'seq', [(i, i ^ offset) for i in range(count)])  300 us
    ppermute x103, starting transfers between devices, across(): return lax.ppermute(value, 'seq', [(i, i ^ offset) for i in range(count)])  115 us
    pallas_call x2, Pallas kernels, recurrence_backward(): pl.pallas_call(functools.partial(backward_kernel, group, low, key_width,...  41.5 us
    unnamed x220, local copies, waits for them, and re-layouts  33.1 us
    pallas_call x1, Pallas kernels, recurrence_forward(): pl.pallas_call(functools.partial(forward_kernel, group, key_width, mark_l...  32.6 us
    dot_general x16, matrix products, product(): lax.dot_general(part, right, (dims, ((), ())), preferred_element_type=f32)  23 us
    dot_general x4, matrix products, mm(): return jnp.dot(left, right, preferred_element_type=f32)  22.4 us
    all_to_all x3, starting transfers between devices, all_to_all(): lax.all_to_all(blocks, 'seq', split_axis=0, concat_axis=0, tiled=True)  19.9 us
  transfers between devices with their start and end apart: 123, of which 49 were waited for; matrix products, arithmetic and copies ran while one was open for 21% of the time, Pallas kernels for 14%

profile of v3, /device:TPU:0, one launch (start us, length us, event | category | flops | bytes accessed | tf_op | source)
XLA Modules:
  0.0 760.4 jit_solution(6147743394971357771)
XLA Ops:
  5.4 3.0 collective-permute-start.4
  9.9 3.6 collective-permute-start.2
  38.0 3.9 all-to-all-start
  48.8 26.1 %collective-permute-done.7 = bf16[1,64,2176]{2,1,0:T(8,128)(2,1)S(1)} collective-permute-done((bf16[1,64,2176]{2,1,0:T(8,128)(2,1)}, bf16[1,64,2176]{2,1,0:T(8,128)(2,1)S(1)}, u32[]{:S(2)}, u32[]{:S(2)}) %collective-permute-start.7) | collective-permute-done | bytes 278560 | tf_op jit(solution)/shard_map/ppermute | solution.py:34
  79.2 12.3 %collective-permute-done.10.refs_3_ = bf16[2048,128]{1,0:T(8,128)(2,1)S(1)} collective-permute-done((bf16[2048,128]{1,0:T(8,128)(2,1)S(1)}, bf16[2048,128]{1,0:T(8,128)(2,1)S(1)}, u32[]{:S(2)}, u32[]{:S(2)}) %collective-permute-start.10) | collective-permute-done | bytes 524320 | tf_op jit(solution)/shard_map/ppermute | solution.py:34
  91.4 8.9 %collective-permute-done.9.refs_2_ = bf16[2048,128]{1,0:T(8,128)(2,1)S(1)} collective-permute-done((bf16[2048,128]{1,0:T(8,128)(2,1)S(1)}, bf16[2048,128]{1,0:T(8,128)(2,1)S(1)}, u32[]{:S(2)}, u32[]{:S(2)}) %collective-permute-start.9) | collective-permute-done | bytes 524320 | tf_op jit(solution)/shard_map/ppermute | solution.py:34
  101.1 4.7 all-to-all-start.1
  119.2 12.4 %collective-permute-done.12 = bf16[2,64,2176]{2,1,0:T(8,128)(2,1)S(1)} collective-permute-done((bf16[2,64,2176]{2,1,0:T(8,128)(2,1)S(1)}, bf16[2,64,2176]{2,1,0:T(8,128)(2,1)S(1)}, u32[]{:S(2)}, u32[]{:S(2)}) %collective-permute-start.12) | collective-permute-done | bytes 557088 | tf_op jit(solution)/shard_map/ppermute | solution.py:34
  133.5 5.6 all-to-all-start.2
  147.2 5.9 assemble.1
  153.1 9.8 %fusion.2 = f32[1024,896]{1,0:T(8,128)} fusion(bf16[2048,896]{1,0:T(8,128)(2,1)} %get-tuple-element.325, bf16[1024,2176]{1,0:T(8,128)(2,1)} %bitcast.15.hidden_mine), kind=kOutput, calls=%fused_computation.4 | convolution fusion | flops 3758096384 | bytes 11534336 | tf_op jit(solution)/shard_map/dot_general | solution.py:17
  162.9 8.5 %fusion = f32[1024,896]{1,0:T(8,128)} fusion(bf16[2048,896]{1,0:T(8,128)(2,1)S(1)} %copy-done.78, bf16[1024,2176]{1,0:T(8,128)(2,1)} %bitcast.22.hidden_theirs), kind=kOutput, calls=%fused_computation.2 | convolution fusion | flops 3758096384 | bytes 11534336 | tf_op jit(solution)/shard_map/dot_general | solution.py:17
  171.4 32.6 %delta_forward.1 = (f32[16,128,128]{2,1,0:T(8,128)}, f32[16,128]{1,0:T(8,128)}, f32[16,128,640]{2,1,0:T(8,128)}, bf16[16,128,256]{2,1,0:T(8,128)(2,1)}, bf16[16,...) custom-call(s32[17]{0:T(128)} %pad_add_fusion.place_ref, ...), custom_call_target="tpu_custom_call" | custom-call | bytes 100800000 | tf_op jit(solution)/shard_map/delta_forward/pallas_call | solution.py:723
  207.6 7.1 collective-permute-done.14
  216.7 3.2 collective-permute-start.41
  228.2 4.3 gate_forward.1
  232.9 7.7 %collective-permute-done.20 = bf16[2048,128]{0,1:T(8,128)(2,1)S(1)} collective-permute-done((bf16[2048,128]{0,1:T(8,128)(2,1)S(1)}, bf16[2048,128]{0,1:T(8,128)(2,1)S(1)}, u32[]{:S(2)}, u32[]{:S(2)}) %collective-permute-start.20) | collective-permute-done | bytes 524320 | tf_op jit(solution)/shard_map/ppermute | solution.py:34
  250.3 16.9 %collective-permute-done.23 = bf16[2048,128]{0,1:T(8,128)(2,1)S(1)} collective-permute-done((bf16[2048,128]{0,1:T(8,128)(2,1)S(1)}, bf16[2048,128]{0,1:T(8,128)(2,1)S(1)}, u32[]{:S(2)}, u32[]{:S(2)}) %collective-permute-start.23) | collective-permute-done | bytes 524320 | tf_op jit(solution)/shard_map/ppermute | solution.py:34
  272.8 3.7 collective-permute-done.25
  276.8 4.0 collective-permute-done.27
  284.1 6.5 collective-permute-done.33
  291.0 4.8 collective-permute-done.32
  297.7 7.1 collective-permute-done.30
  311.3 3.5 collective-permute-done.36
  314.8 5.1 collective-permute-done.34
  319.9 10.4 %collective-permute-done.35 = bf16[64,2048]{1,0:T(8,128)(2,1)S(1)} collective-permute-done((bf16[64,2048]{1,0:T(8,128)(2,1)S(1)}, bf16[64,2048]{1,0:T(8,128)(2,1)S(1)}, u32[]{:S(2)}, u32[]{:S(2)}) %collective-permute-start.35) | collective-permute-done | bytes 262176 | tf_op jit(solution)/shard_map/ppermute | solution.py:34
  332.9 4.3 collective-permute-done.39
  338.0 6.2 collective-permute-done.37
  347.4 11.1 %collective-permute-done.47 = bf16[1,64,2048]{2,1,0:T(8,128)(2,1)S(1)} collective-permute-done((bf16[1,64,2048]{2,1,0:T(8,128)(2,1)S(1)}, bf16[1,64,2048]{2,1,0:T(8,128)(2,1)S(1)}, u32[]{:S(2)}, u32[]{:S(2)}) %collective-permute-start.47) | collective-permute-done | bytes 262176 | tf_op jit(solution)/shard_map/ppermute | solution.py:34
  359.9 5.3 collective-permute-done.48
  387.5 7.3 collective-permute-done.56
  399.7 8.3 %collective-permute-done.61 = bf16[2048,128]{0,1:T(8,128)(2,1)S(1)} collective-permute-done((bf16[2048,128]{0,1:T(8,128)(2,1)S(1)}, bf16[2048,128]{0,1:T(8,128)(2,1)S(1)}, u32[]{:S(2)}, u32[]{:S(2)}) %collective-permute-start.61) | collective-permute-done | bytes 524320 | tf_op jit(solution)/shard_map/ppermute | solution.py:34
  411.2 11.7 %collective-permute-done.62 = bf16[64,2048]{1,0:T(8,128)(2,1)S(1)} collective-permute-done((bf16[64,2048]{1,0:T(8,128)(2,1)S(1)}, bf16[64,2048]{1,0:T(8,128)(2,1)S(1)}, u32[]{:S(2)}, u32[]{:S(2)}) %collective-permute-start.62) | collective-permute-done | bytes 262176 | tf_op jit(solution)/shard_map/ppermute | solution.py:34
  428.3 5.5 collective-permute-done.67
  436.9 12.9 %collective-permute-done.64 = bf16[1,64,2048]{2,1,0:T(8,128)(2,1)S(1)} collective-permute-done((bf16[1,64,2048]{2,1,0:T(8,128)(2,1)S(1)}, bf16[1,64,2048]{2,1,0:T(8,128)(2,1)S(1)}, u32[]{:S(2)}, u32[]{:S(2)}) %collective-permute-start.64) | collective-permute-done | bytes 262176 | tf_op jit(solution)/shard_map/ppermute | solution.py:34
  463.7 16.6 %collective-permute-done.72 = bf16[1,64,2048]{2,1,0:T(8,128)(2,1)S(1)} collective-permute-done((bf16[1,64,2048]{2,1,0:T(8,128)(2,1)S(1)}, bf16[1,64,2048]{2,1,0:T(8,128)(2,1)S(1)}, u32[]{:S(2)}, u32[]{:S(2)}) %collective-permute-start.72) | collective-permute-done | bytes 262176 | tf_op jit(solution)/shard_map/ppermute | solution.py:34
  486.0 2.9 copy.159
  489.2 4.2 collective-permute-done.75
  509.8 4.2 fusion.119.grad_mine.refs_4_.refs_5_
  514.1 4.3 fusion.120.grad_theirs.refs_6_.refs_7_
  518.4 6.4 gate_dots.1
  528.4 2.9 convolution_bitcast_fusion
  531.3 3.0 fusion.5
  536.7 2.9 pad_maximum_fusion.1
  541.0 4.8 all-to-all-start.3
  553.1 20.8 %delta_backward.2 = (bf16[4,8,128,128]{3,2,1,0:T(8,128)(2,1)}, bf16[8,128,384]{2,1,0:T(8,128)(2,1)}, f32[8,8,128]{2,1,0:T(8,128)}, f32[256,128]{1,0:T(8,128)}, f32[3,8,640]{2,1,0:T(8,128)}, /*index=5*/f32[8,640]{1,0:T(8,128)}) custom-call(s32[19]{0:T(128)} %pad_add_fusion.1.place_ref, f32[16,64,896]{2,1,0:T(8,128)} %bitcast.238, f32[16,64,896]{2,1,0:T(8,128)} %bitcast.239, ...), custom_call_target="tpu_custom_call" | custom-call | bytes 64800000 | tf_op jit(solution)/shard_map/delta_backward/pallas_call | solution.py:826
  575.9 2.8 collective-permute-start.87
  579.4 20.7 %delta_backward.3 = (bf16[4,8,128,128]{3,2,1,0:T(8,128)(2,1)}, bf16[8,128,384]{2,1,0:T(8,128)(2,1)}, f32[8,8,128]{2,1,0:T(8,128)}, f32[256,128]{1,0:T(8,128)}, f32[3,8,640]{2,1,0:T(8,128)}, /*index=5*/f32[8,640]{1,0:T(8,128)}) custom-call(s32[19]{0:T(128)} %pad_add_fusion.1.place_ref, f32[16,64,896]{2,1,0:T(8,128)} %bitcast.240, f32[16,64,896]{2,1,0:T(8,128)} %bitcast.241, ...), custom_call_target="tpu_custom_call" | custom-call | bytes 64800000 | tf_op jit(solution)/shard_map/delta_backward/pallas_call | solution.py:826
  600.3 4.1 collective-permute-done.85.refs_6_
  610.7 6.1 collective-permute-done.94.refs_3_
  616.9 3.7 collective-permute-done.93.refs_2_
  621.4 4.5 collect.1
  638.4 9.2 %weight_gradient.1 = (bf16[16,3,128,128]{3,2,1,0:T(8,128)(2,1)}, f32[2048,128]{1,0:T(8,128)}) custom-call(bf16[1024,2176]{1,0:T(8,128)(2,1)} %bitcast.15.hidden_mine, bf16[1024,2176]{1,0:T(8,128)(2,1)} %bitcast.22.hidden_theirs, bf16[1024,512]{1,0:T(8,128)(2,1)} %bitcast.269, bf16[1024,512]{1,0:T(8,128)(2,1)} %bitcast.270, ...), custom_call_target="tpu_custom_call" | custom-call | bytes 21600000 | tf_op jit(solution)/shard_map/weight_gradient/pallas_call | solution.py:935
  653.4 9.5 %all-to-all-start.4 = ((bf16[16,3,128,128]{3,2,1,0:T(8,128)(2,1)}), bf16[16,3,128,128]{3,2,1,0:T(8,128)(2,1)}, u32[]{:S(2)}, u32[]{:S(2)}) async-start(bf16[16,3,128,128]{3,2,1,0:T(8,128)(2,1)} %get-tuple-element.546), calls=%async_computation.4 | async-start | bytes 3145728 | tf_op jit(solution)/shard_map/all_to_all | solution.py:195
  665.3 3.7 collective-permute-start.115
  670.3 2.9 fusion.115
  675.4 2.9 convert_add_fusion
  678.4 11.9 %collective-permute-done.105 = bf16[128,1024]{1,0:T(8,128)(2,1)S(1)} collective-permute-done((bf16[128,1024]{1,0:T(8,128)(2,1)S(1)}, bf16[128,1024]{1,0:T(8,128)(2,1)S(1)}, u32[]{:S(2)}, u32[]{:S(2)}) %collective-permute-start.105) | collective-permute-done | bytes 262176 | tf_op jit(solution)/shard_map/ppermute | solution.py:34
  695.7 4.7 collective-permute-done.103
  701.7 10.8 %collective-permute-done.114 = f32[304,128]{1,0:T(8,128)S(1)} collective-permute-done((f32[304,128]{1,0:T(8,128)S(1)}, f32[304,128]{1,0:T(8,128)S(1)}, u32[]{:S(2)}, u32[]{:S(2)}) %collective-permute-start.114) | collective-permute-done | bytes 155680 | tf_op jit(solution)/shard_map/ppermute | solution.py:34
  715.4 6.9 collective-permute-done.99
  730.0 3.2 unpack_mixer.1
  740.7 4.7 unpack_ffn.1
  745.5 5.4 collective-permute-done.108
  (631 shorter events, 271.0 us)
Async XLA Ops:
  5.4 29.0 %collective-permute-start.4 = (bf16[1,64,2176]{2,1,0:T(8,128)(2,1)S(1)}, bf16[1,64,2176]{2,1,0:T(8,128)(2,1)}, u32[]{:S(2)}, u32[]{:S(2)}) collective-permute-start(bf16[1,64,2176]{2,1,0:T(8,128)(2,1)S(1)} %fusion.56), channel_id=1, source_target_pairs={{0,4},{2,6},{4,0},{6,2},{8,12},{10,14},{12,8},{14,10},{16,20},{18,... | collective-permute-start | bytes 835592 | tf_op jit(solution)/shard_map/ppermute | solution.py:34
  8.4 26.0 %collective-permute-start.3 = (bf16[1,64,2176]{2,1,0:T(8,128)(2,1)S(1)}, bf16[1,64,2176]{2,1,0:T(8,128)(2,1)}, u32[]{:S(2)}, u32[]{:S(2)}) collective-permute-start(bf16[1,64,2176]{2,1,0:T(8,128)(2,1)S(1)} %fusion.56), channel_id=1, source_target_pairs={{0,2},{2,0},{4,6},{6,4},{8,10},{10,8},{12,14},{14,12},{16,18},{18,... | collective-permute-start | bytes 835592 | tf_op jit(solution)/shard_map/ppermute | solution.py:34
  9.9 24.5 %collective-permute-start.2 = (bf16[1,64,2176]{2,1,0:T(8,128)(2,1)S(1)}, bf16[1,64,2176]{2,1,0:T(8,128)(2,1)}, u32[]{:S(2)}, u32[]{:S(2)}) collective-permute-start(bf16[1,64,2176]{2,1,0:T(8,128)(2,1)S(1)} %fusion.56), channel_id=1, source_target_pairs={{0,24},{2,26},{4,28},{6,30},{8,16},{10,18},{12,20},{14,22},{16,8},... | collective-permute-start | bytes 835592 | tf_op jit(solution)/shard_map/ppermute | solution.py:34
  13.5 23.3 %collective-permute-start.1 = (bf16[1,64,2176]{2,1,0:T(8,128)(2,1)S(1)}, bf16[1,64,2176]{2,1,0:T(8,128)(2,1)}, u32[]{:S(2)}, u32[]{:S(2)}) collective-permute-start(bf16[1,64,2176]{2,1,0:T(8,128)(2,1)S(1)} %fusion.56), channel_id=1, source_target_pairs={{0,16},{2,18},{4,20},{6,22},{8,24},{10,26},{12,28},{14,30},{16,0},... | collective-permute-start | bytes 835592 | tf_op jit(solution)/shard_map/ppermute | solution.py:34
  13.5 23.3 %collective-permute-start = (bf16[1,64,2176]{2,1,0:T(8,128)(2,1)S(1)}, bf16[1,64,2176]{2,1,0:T(8,128)(2,1)}, u32[]{:S(2)}, u32[]{:S(2)}) collective-permute-start(bf16[1,64,2176]{2,1,0:T(8,128)(2,1)S(1)} %fusion.56), channel_id=1, source_target_pairs={{0,8},{2,10},{4,12},{6,14},{8,0},{10,2},{12,4},{14,6},{16,24},{18,... | collective-permute-start | bytes 835592 | tf_op jit(solution)/shard_map/ppermute | solution.py:34
  38.0 37.7 %all-to-all-start = ((bf16[128,16,128]{2,0,1:T(8,128)(2,1)}), bf16[128,16,128]{2,0,1:T(8,128)(2,1)S(1)}, u32[]{:S(2)}, u32[]{:S(2)}) async-start(bf16[128,16,128]{2,0,1:T(8,128)(2,1)} %bitcast.11), calls=%async_computation | async-start | bytes 1048576 | tf_op jit(solution)/shard_map/all_to_all | solution.py:238
  44.8 30.1 %collective-permute-start.6 = (bf16[3,64,2176]{2,1,0:T(8,128)(2,1)S(1)}, bf16[3,64,2176]{2,1,0:T(8,128)(2,1)S(1)}, u32[]{:S(2)}, u32[]{:S(2)}) collective-permute-start(bf16[3,64,2176]{2,1,0:T(8,128)(2,1)S(1)} %constant_dynamic-update-slice_fusion), channel_id=1, source_target_pairs={{0,4},{2,6},{4,0},{6,2},{8,12},{10,14},{12,8},{14,10},{16,20},{18,... | collective-permute-start | bytes 2506760 | tf_op jit(solution)/shard_map/ppermute | solution.py:34
  46.8 28.8 %collective-permute-start.5 = (bf16[3,64,2176]{2,1,0:T(8,128)(2,1)S(1)}, bf16[3,64,2176]{2,1,0:T(8,128)(2,1)S(1)}, u32[]{:S(2)}, u32[]{:S(2)}) collective-permute-start(bf16[3,64,2176]{2,1,0:T(8,128)(2,1)S(1)} %constant_dynamic-update-slice_fusion), channel_id=1, source_target_pairs={{0,2},{2,0},{4,6},{6,4},{8,10},{10,8},{12,14},{14,12},{16,18},{18,... | collective-permute-start | bytes 2506760 | tf_op jit(solution)/shard_map/ppermute | solution.py:34
  48.2 26.7 %collective-permute-start.7 = (bf16[1,64,2176]{2,1,0:T(8,128)(2,1)}, bf16[1,64,2176]{2,1,0:T(8,128)(2,1)S(1)}, u32[]{:S(2)}, u32[]{:S(2)}) collective-permute-start(bf16[1,64,2176]{2,1,0:T(8,128)(2,1)} %collective-permute-done.4), channel_id=1, source_target_pairs={{0,2},{2,0},{4,6},{6,4},{8,10},{10,8},{12,14},{14,12},{16,18},{18,... | collective-permute-start | bytes 835592 | tf_op jit(solution)/shard_map/ppermute | solution.py:34
  75.6 15.8 %collective-permute-start.10 = (bf16[2048,128]{1,0:T(8,128)(2,1)S(1)}, bf16[2048,128]{1,0:T(8,128)(2,1)S(1)}, u32[]{:S(2)}, u32[]{:S(2)}) collective-permute-start(bf16[2048,128]{1,0:T(8,128)(2,1)S(1)} %bitcast.283), channel_id=1, source_target_pairs={{0,6},{2,4},{4,2},{6,0},{8,14},{10,12},{12,10},{14,8},{16,22},{18,... | collective-permute-start | bytes 1572872 | tf_op jit(solution)/shard_map/ppermute | solution.py:34
  77.0 23.3 %collective-permute-start.9 = (bf16[2048,128]{1,0:T(8,128)(2,1)S(1)}, bf16[2048,128]{1,0:T(8,128)(2,1)S(1)}, u32[]{:S(2)}, u32[]{:S(2)}) collective-permute-start(bf16[2048,128]{1,0:T(8,128)(2,1)S(1)} %bitcast.284), channel_id=1, source_target_pairs={{0,4},{2,6},{4,0},{6,2},{8,12},{10,14},{12,8},{14,10},{16,20},{18,... | collective-permute-start | bytes 1572872 | tf_op jit(solution)/shard_map/ppermute | solution.py:34
  78.2 22.9 %collective-permute-start.8 = (bf16[2048,128]{1,0:T(8,128)(2,1)S(1)}, bf16[2048,128]{1,0:T(8,128)(2,1)}, u32[]{:S(2)}, u32[]{:S(2)}) collective-permute-start(bf16[2048,128]{1,0:T(8,128)(2,1)S(1)} %bitcast.285), channel_id=1, source_target_pairs={{0,2},{2,0},{4,6},{6,4},{8,10},{10,8},{12,14},{14,12},{16,18},{18,... | collective-permute-start | bytes 1572872 | tf_op jit(solution)/shard_map/ppermute | solution.py:34
  101.1 31.4 %all-to-all-start.1 = ((bf16[128,16,256]{2,0,1:T(8,128)(2,1)}), bf16[128,16,256]{2,0,1:T(8,128)(2,1)S(1)}, u32[]{:S(2)}, u32[]{:S(2)}) async-start(bf16[128,16,256]{2,0,1:T(8,128)(2,1)} %pad_maximum_fusion.5), calls=%async_computation.1 | async-start | bytes 2097152 | tf_op jit(solution)/shard_map/all_to_all | solution.py:238
  107.8 23.9 %collective-permute-start.12 = (bf16[2,64,2176]{2,1,0:T(8,128)(2,1)S(1)}, bf16[2,64,2176]{2,1,0:T(8,128)(2,1)S(1)}, u32[]{:S(2)}, u32[]{:S(2)}) collective-permute-start(bf16[2,64,2176]{2,1,0:T(8,128)(2,1)S(1)} %slice.629), channel_id=1, source_target_pairs={{0,4},{2,6},{4,0},{6,2},{8,12},{10,14},{12,8},{14,10},{16,20},{18,... | collective-permute-start | bytes 1671176 | tf_op jit(solution)/shard_map/ppermute | solution.py:34
  132.5 30.4 %collective-permute-start.13 = (bf16[16,64,2176]{2,1,0:T(8,128)(2,1)}, bf16[16,64,2176]{2,1,0:T(8,128)(2,1)}, u32[]{:S(2)}, u32[]{:S(2)}) collective-permute-start(bf16[16,64,2176]{2,1,0:T(8,128)(2,1)} %constant_dynamic-update-slice_fusion.3.refs_5_.refs_16_.refs_17_.refs_18_.refs_19_.refs_20_.refs_21_.refs_2, ...), channel_id=1, source_target_pairs={{0,1},{1,0},{2,3},{3,2},{4,5},{5,4},{6,7},{7,6},{8,9},{9,8},{10,11... | collective-permute-start | bytes 13369352 | tf_op jit(solution)/shard_map/ppermute | solution.py:38
  133.5 83.2 %all-to-all-start.2 = ((bf16[16,688,128]{2,1,0:T(8,128)(2,1)}), bf16[16,688,128]{2,1,0:T(8,128)(2,1)S(1)}, u32[]{:S(2)}, u32[]{:S(2)}) async-start(bf16[16,688,128]{2,1,0:T(8,128)(2,1)} %pad_maximum_fusion), calls=%async_computation.2 | async-start | bytes 5636096 | tf_op jit(solution)/shard_map/all_to_all | solution.py:195
  141.3 64.9 %collective-permute-start.16 = (bf16[1,64,2048]{2,1,0:T(8,128)(2,1)S(1)}, bf16[1,64,2048]{2,1,0:T(8,128)(2,1)}, u32[]{:S(2)}, u32[]{:S(2)}) collective-permute-start(bf16[1,64,2048]{2,1,0:T(8,128)(2,1)S(1)} %bitcast.290), channel_id=1, source_target_pairs={{0,4},{2,6},{4,0},{6,2},{8,12},{10,14},{12,8},{14,10},{16,20},{18,... | collective-permute-start | bytes 786440 | tf_op jit(solution)/shard_map/ppermute | solution.py:34
  143.3 64.2 %collective-permute-start.15 = (bf16[1,64,2048]{2,1,0:T(8,128)(2,1)S(1)}, bf16[1,64,2048]{2,1,0:T(8,128)(2,1)S(1)}, u32[]{:S(2)}, u32[]{:S(2)}) collective-permute-start(bf16[1,64,2048]{2,1,0:T(8,128)(2,1)S(1)} %bitcast.291), channel_id=1, source_target_pairs={{0,2},{2,0},{4,6},{6,4},{8,10},{10,8},{12,14},{14,12},{16,18},{18,... | collective-permute-start | bytes 786440 | tf_op jit(solution)/shard_map/ppermute | solution.py:34
  144.8 69.9 %collective-permute-start.14 = (bf16[1,64,2048]{2,1,0:T(8,128)(2,1)S(1)}, bf16[1,64,2048]{2,1,0:T(8,128)(2,1)S(1)}, u32[]{:S(2)}, u32[]{:S(2)}) collective-permute-start(bf16[1,64,2048]{2,1,0:T(8,128)(2,1)S(1)} %bitcast.292), channel_id=1, source_target_pairs={{0,16},{2,18},{4,20},{6,22},{8,24},{10,26},{12,28},{14,30},{16,0},... | collective-permute-start | bytes 786440 | tf_op jit(solution)/shard_map/ppermute | solution.py:34
  216.7 27.0 %collective-permute-start.41 = (bf16[1,64,2048]{2,1,0:T(8,128)(2,1)}, bf16[1,64,2048]{2,1,0:T(8,128)(2,1)}, u32[]{:S(2)}, u32[]{:S(2)}) collective-permute-start(bf16[1,64,2048]{2,1,0:T(8,128)(2,1)} %copy-done.56), channel_id=1, source_target_pairs={{0,4},{2,6},{4,0},{6,2},{8,12},{10,14},{12,8},{14,10},{16,20},{18,... | collective-permute-start | bytes 786440 | tf_op jit(solution)/shard_map/ppermute | solution.py:34
  220.0 23.8 %collective-permute-start.40 = (bf16[1,64,2048]{2,1,0:T(8,128)(2,1)}, bf16[1,64,2048]{2,1,0:T(8,128)(2,1)}, u32[]{:S(2)}, u32[]{:S(2)}) collective-permute-start(bf16[1,64,2048]{2,1,0:T(8,128)(2,1)} %copy-done.56), channel_id=1, source_target_pairs={{0,2},{2,0},{4,6},{6,4},{8,10},{10,8},{12,14},{14,12},{16,18},{18,... | collective-permute-start | bytes 786440 | tf_op jit(solution)/shard_map/ppermute | solution.py:34
  222.4 19.5 %collective-permute-start.42 = (bf16[1,64,2048]{2,1,0:T(8,128)(2,1)}, bf16[1,64,2048]{2,1,0:T(8,128)(2,1)}, u32[]{:S(2)}, u32[]{:S(2)}) collective-permute-start(bf16[1,64,2048]{2,1,0:T(8,128)(2,1)} %collective-permute-done.16), channel_id=1, source_target_pairs={{0,2},{2,0},{4,6},{6,4},{8,10},{10,8},{12,14},{14,12},{16,18},{18,... | collective-permute-start | bytes 786440 | tf_op jit(solution)/shard_map/ppermute | solution.py:34
  241.5 30.9 %collective-permute-start.28 = (bf16[2048,128]{0,1:T(8,128)(2,1)S(1)}, bf16[2048,128]{0,1:T(8,128)(2,1)S(1)}, u32[]{:S(2)}, u32[]{:S(2)}) collective-permute-start(bf16[2048,128]{0,1:T(8,128)(2,1)S(1)} %get-tuple-element.617), channel_id=1, source_target_pairs={{0,8},{2,10},{4,12},{6,14},{8,0},{10,2},{12,4},{14,6},{16,24},{18,... | collective-permute-start | bytes 1572872 | tf_op jit(solution)/shard_map/ppermute | solution.py:34
  242.0 25.2 %collective-permute-start.23 = (bf16[2048,128]{0,1:T(8,128)(2,1)S(1)}, bf16[2048,128]{0,1:T(8,128)(2,1)S(1)}, u32[]{:S(2)}, u32[]{:S(2)}) collective-permute-start(bf16[2048,128]{0,1:T(8,128)(2,1)S(1)} %get-tuple-element.618), channel_id=1, source_target_pairs={{0,8},{2,10},{4,12},{6,14},{8,0},{10,2},{12,4},{14,6},{16,24},{18,... | collective-permute-start | bytes 1572872 | tf_op jit(solution)/shard_map/ppermute | solution.py:34
  244.6 25.2 %collective-permute-start.43 = (bf16[1,64,2048]{2,1,0:T(8,128)(2,1)}, bf16[1,64,2048]{2,1,0:T(8,128)(2,1)S(1)}, u32[]{:S(2)}, u32[]{:S(2)}) collective-permute-start(bf16[1,64,2048]{2,1,0:T(8,128)(2,1)} %collective-permute-done.40), channel_id=1, source_target_pairs={{0,4},{2,6},{4,0},{6,2},{8,12},{10,14},{12,8},{14,10},{16,20},{18,... | collective-permute-start | bytes 786440 | tf_op jit(solution)/shard_map/ppermute | solution.py:34
  272.4 18.1 %collective-permute-start.33 = (bf16[192,2048]{1,0:T(8,128)(2,1)S(1)}, bf16[192,2048]{1,0:T(8,128)(2,1)S(1)}, u32[]{:S(2)}, u32[]{:S(2)}) collective-permute-start(bf16[192,2048]{1,0:T(8,128)(2,1)S(1)} %pad.144), channel_id=1, source_target_pairs={{0,8},{2,10},{4,12},{6,14},{8,0},{10,2},{12,4},{14,6},{16,24},{18,... | collective-permute-start | bytes 2359304 | tf_op jit(solution)/shard_map/ppermute | solution.py:34
  276.5 33.8 %collective-permute-start.44 = (bf16[8,64,2048]{2,1,0:T(8,128)(2,1)S(1)}, bf16[8,64,2048]{2,1,0:T(8,128)(2,1)S(1)}, u32[]{:S(2)}, u32[]{:S(2)}) collective-permute-start(bf16[8,64,2048]{2,1,0:T(8,128)(2,1)S(1)} %constant_dynamic-update-slice_fusion.12), channel_id=1, source_target_pairs={{0,1},{1,0},{2,3},{3,2},{4,5},{5,4},{6,7},{7,6},{8,9},{9,8},{10,11... | collective-permute-start | bytes 6291464 | tf_op jit(solution)/shard_map/ppermute | solution.py:38
  281.0 14.9 %collective-permute-start.32 = (bf16[128,2048]{1,0:T(8,128)(2,1)S(1)}, bf16[128,2048]{1,0:T(8,128)(2,1)S(1)}, u32[]{:S(2)}, u32[]{:S(2)}) collective-permute-start(bf16[128,2048]{1,0:T(8,128)(2,1)S(1)} %add_convert_fusion.1), channel_id=1, source_target_pairs={{0,4},{2,6},{4,0},{6,2},{8,12},{10,14},{12,8},{14,10},{16,20},{18,... | collective-permute-start | bytes 1572872 | tf_op jit(solution)/shard_map/ppermute | solution.py:34
  282.8 14.9 %collective-permute-start.31 = (bf16[128,2048]{1,0:T(8,128)(2,1)S(1)}, bf16[128,2048]{1,0:T(8,128)(2,1)S(1)}, u32[]{:S(2)}, u32[]{:S(2)}) collective-permute-start(bf16[128,2048]{1,0:T(8,128)(2,1)S(1)} %add_convert_fusion.2), channel_id=1, source_target_pairs={{0,2},{2,0},{4,6},{6,4},{8,10},{10,8},{12,14},{14,12},{16,18},{18,... | collective-permute-start | bytes 1572872 | tf_op jit(solution)/shard_map/ppermute | solution.py:34
  283.3 21.5 %collective-permute-start.30 = (bf16[128,2048]{1,0:T(8,128)(2,1)S(1)}, bf16[128,2048]{1,0:T(8,128)(2,1)S(1)}, u32[]{:S(2)}, u32[]{:S(2)}) collective-permute-start(bf16[128,2048]{1,0:T(8,128)(2,1)S(1)} %add_convert_fusion.3), channel_id=1, source_target_pairs={{0,4},{2,6},{4,0},{6,2},{8,12},{10,14},{12,8},{14,10},{16,20},{18,... | collective-permute-start | bytes 1572872 | tf_op jit(solution)/shard_map/ppermute | solution.py:34
  290.5 15.6 %collective-permute-start.29 = (bf16[128,2048]{1,0:T(8,128)(2,1)S(1)}, bf16[128,2048]{1,0:T(8,128)(2,1)S(1)}, u32[]{:S(2)}, u32[]{:S(2)}) collective-permute-start(bf16[128,2048]{1,0:T(8,128)(2,1)S(1)} %add_convert_fusion.4), channel_id=1, source_target_pairs={{0,2},{2,0},{4,6},{6,4},{8,10},{10,8},{12,14},{14,12},{16,18},{18,... | collective-permute-start | bytes 1572872 | tf_op jit(solution)/shard_map/ppermute | solution.py:34
  308.3 22.1 %collective-permute-start.35 = (bf16[64,2048]{1,0:T(8,128)(2,1)S(1)}, bf16[64,2048]{1,0:T(8,128)(2,1)S(1)}, u32[]{:S(2)}, u32[]{:S(2)}) collective-permute-start(bf16[64,2048]{1,0:T(8,128)(2,1)S(1)} %get-tuple-element.655), channel_id=1, source_target_pairs={{0,16},{2,18},{4,20},{6,22},{8,24},{10,26},{12,28},{14,30},{16,0},... | collective-permute-start | bytes 786440 | tf_op jit(solution)/shard_map/ppermute | solution.py:34
  425.0 24.9 %collective-permute-start.69 = (bf16[256,2048]{1,0:T(8,128)(2,1)S(1)}, bf16[256,2048]{1,0:T(8,128)(2,1)S(1)}, u32[]{:S(2)}, u32[]{:S(2)}) collective-permute-start(bf16[256,2048]{1,0:T(8,128)(2,1)S(1)} %convolution_convert_fusion.4), channel_id=1, source_target_pairs={{0,1},{1,0},{2,3},{3,2},{4,5},{5,4},{6,7},{7,6},{8,9},{9,8},{10,11... | collective-permute-start | bytes 3145736 | tf_op jit(solution)/shard_map/ppermute | solution.py:38
  428.3 21.6 %collective-permute-start.64 = (bf16[1,64,2048]{2,1,0:T(8,128)(2,1)S(1)}, bf16[1,64,2048]{2,1,0:T(8,128)(2,1)S(1)}, u32[]{:S(2)}, u32[]{:S(2)}) collective-permute-start(bf16[1,64,2048]{2,1,0:T(8,128)(2,1)S(1)} %get-tuple-element.453), channel_id=1, source_target_pairs={{0,16},{2,18},{4,20},{6,22},{8,24},{10,26},{12,28},{14,30},{16,0},... | collective-permute-start | bytes 786440 | tf_op jit(solution)/shard_map/ppermute | solution.py:34
  433.8 16.1 %collective-permute-start.63 = (bf16[1,64,2048]{2,1,0:T(8,128)(2,1)S(1)}, bf16[1,64,2048]{2,1,0:T(8,128)(2,1)S(1)}, u32[]{:S(2)}, u32[]{:S(2)}) collective-permute-start(bf16[1,64,2048]{2,1,0:T(8,128)(2,1)S(1)} %get-tuple-element.453), channel_id=1, source_target_pairs={{0,8},{2,10},{4,12},{6,14},{8,0},{10,2},{12,4},{14,6},{16,24},{18,... | collective-permute-start | bytes 786440 | tf_op jit(solution)/shard_map/ppermute | solution.py:34
  434.6 18.0 %collective-permute-start.68 = (bf16[256,2048]{1,0:T(8,128)(2,1)S(1)}, bf16[256,2048]{1,0:T(8,128)(2,1)S(1)}, u32[]{:S(2)}, u32[]{:S(2)}) collective-permute-start(bf16[256,2048]{1,0:T(8,128)(2,1)S(1)} %convolution_convert_fusion.5), channel_id=1, source_target_pairs={{0,1},{1,0},{2,3},{3,2},{4,5},{5,4},{6,7},{7,6},{8,9},{9,8},{10,11... | collective-permute-start | bytes 3145736 | tf_op jit(solution)/shard_map/ppermute | solution.py:38
  454.9 25.5 %collective-permute-start.71 = (bf16[3,64,2048]{2,1,0:T(8,128)(2,1)S(1)}, bf16[3,64,2048]{2,1,0:T(8,128)(2,1)S(1)}, u32[]{:S(2)}, u32[]{:S(2)}) collective-permute-start(bf16[3,64,2048]{2,1,0:T(8,128)(2,1)S(1)} %constant_dynamic-update-slice_fusion.40), channel_id=1, source_target_pairs={{0,4},{2,6},{4,0},{6,2},{8,12},{10,14},{12,8},{14,10},{16,20},{18,... | collective-permute-start | bytes 2359304 | tf_op jit(solution)/shard_map/ppermute | solution.py:34
  456.5 23.8 %collective-permute-start.70 = (bf16[3,64,2048]{2,1,0:T(8,128)(2,1)S(1)}, bf16[3,64,2048]{2,1,0:T(8,128)(2,1)S(1)}, u32[]{:S(2)}, u32[]{:S(2)}) collective-permute-start(bf16[3,64,2048]{2,1,0:T(8,128)(2,1)S(1)} %constant_dynamic-update-slice_fusion.40), channel_id=1, source_target_pairs={{0,2},{2,0},{4,6},{6,4},{8,10},{10,8},{12,14},{14,12},{16,18},{18,... | collective-permute-start | bytes 2359304 | tf_op jit(solution)/shard_map/ppermute | solution.py:34
  458.0 22.3 %collective-permute-start.73 = (bf16[2048,128]{0,1:T(8,128)(2,1)S(1)}, bf16[2048,128]{0,1:T(8,128)(2,1)S(1)}, u32[]{:S(2)}, u32[]{:S(2)}) collective-permute-start(bf16[2048,128]{0,1:T(8,128)(2,1)S(1)} %get-tuple-element.578), channel_id=1, source_target_pairs={{0,8},{2,10},{4,12},{6,14},{8,0},{10,2},{12,4},{14,6},{16,24},{18,... | collective-permute-start | bytes 1572872 | tf_op jit(solution)/shard_map/ppermute | solution.py:34
  458.1 22.2 %collective-permute-start.72 = (bf16[1,64,2048]{2,1,0:T(8,128)(2,1)S(1)}, bf16[1,64,2048]{2,1,0:T(8,128)(2,1)S(1)}, u32[]{:S(2)}, u32[]{:S(2)}) collective-permute-start(bf16[1,64,2048]{2,1,0:T(8,128)(2,1)S(1)} %collective-permute-done.67), channel_id=1, source_target_pairs={{0,2},{2,0},{4,6},{6,4},{8,10},{10,8},{12,14},{14,12},{16,18},{18,... | collective-permute-start | bytes 786440 | tf_op jit(solution)/shard_map/ppermute | solution.py:34
  461.8 27.2 %collective-permute-start.76 = (bf16[192,2048]{1,0:T(8,128)(2,1)}, bf16[192,2048]{1,0:T(8,128)(2,1)}, u32[]{:S(2)}, u32[]{:S(2)}) collective-permute-start(bf16[192,2048]{1,0:T(8,128)(2,1)} %slice.1028), channel_id=1, source_target_pairs={{0,8},{2,10},{4,12},{6,14},{8,0},{10,2},{12,4},{14,6},{16,24},{18,... | collective-permute-start | bytes 2359304 | tf_op jit(solution)/shard_map/ppermute | solution.py:34
  524.8 14.8 %collective-permute-start.84 = (f32[16,128]{1,0:T(8,128)}, f32[16,128]{1,0:T(8,128)S(1)}, u32[]{:S(2)}, u32[]{:S(2)}) collective-permute-start(f32[16,128]{1,0:T(8,128)} %gate_dots.1), channel_id=1, source_target_pairs={{0,6},{2,4},{4,2},{6,0},{8,14},{10,12},{12,10},{14,8},{16,22},{18,... | collective-permute-start | bytes 24584 | tf_op jit(solution)/shard_map/ppermute | solution.py:34
  541.0 85.0 %all-to-all-start.3 = ((bf16[16,688,128]{2,1,0:T(8,128)(2,1)}), bf16[16,688,128]{2,1,0:T(8,128)(2,1)}, u32[]{:S(2)}, u32[]{:S(2)}) async-start(bf16[16,688,128]{2,1,0:T(8,128)(2,1)} %pad_maximum_fusion.1), calls=%async_computation.3 | async-start | bytes 5636096 | tf_op jit(solution)/shard_map/all_to_all | solution.py:195
  546.7 32.0 %collective-permute-start.91 = (bf16[64,2048]{1,0:T(8,128)(2,1)S(1)}, bf16[64,2048]{1,0:T(8,128)(2,1)S(1)}, u32[]{:S(2)}, u32[]{:S(2)}) collective-permute-start(bf16[64,2048]{1,0:T(8,128)(2,1)S(1)} %add_convert_fusion.7), channel_id=1, source_target_pairs={{0,4},{2,6},{4,0},{6,2},{8,12},{10,14},{12,8},{14,10},{16,20},{18,... | collective-permute-start | bytes 786440 | tf_op jit(solution)/shard_map/ppermute | solution.py:34
  548.8 30.5 %collective-permute-start.90 = (bf16[64,2048]{1,0:T(8,128)(2,1)S(1)}, bf16[64,2048]{1,0:T(8,128)(2,1)S(1)}, u32[]{:S(2)}, u32[]{:S(2)}) collective-permute-start(bf16[64,2048]{1,0:T(8,128)(2,1)S(1)} %add_convert_fusion.8), channel_id=1, source_target_pairs={{0,2},{2,0},{4,6},{6,4},{8,10},{10,8},{12,14},{14,12},{16,18},{18,... | collective-permute-start | bytes 786440 | tf_op jit(solution)/shard_map/ppermute | solution.py:34
  550.3 49.8 %collective-permute-start.89 = (bf16[64,2048]{1,0:T(8,128)(2,1)S(1)}, bf16[64,2048]{1,0:T(8,128)(2,1)S(1)}, u32[]{:S(2)}, u32[]{:S(2)}) collective-permute-start(bf16[64,2048]{1,0:T(8,128)(2,1)S(1)} %add_convert_fusion.9), channel_id=1, source_target_pairs={{0,4},{2,6},{4,0},{6,2},{8,12},{10,14},{12,8},{14,10},{16,20},{18,... | collective-permute-start | bytes 786440 | tf_op jit(solution)/shard_map/ppermute | solution.py:34
  551.0 49.2 %collective-permute-start.88 = (bf16[64,2048]{1,0:T(8,128)(2,1)S(1)}, bf16[64,2048]{1,0:T(8,128)(2,1)S(1)}, u32[]{:S(2)}, u32[]{:S(2)}) collective-permute-start(bf16[64,2048]{1,0:T(8,128)(2,1)S(1)} %add_convert_fusion.10), channel_id=1, source_target_pairs={{0,2},{2,0},{4,6},{6,4},{8,10},{10,8},{12,14},{14,12},{16,18},{18,... | collective-permute-start | bytes 786440 | tf_op jit(solution)/shard_map/ppermute | solution.py:34
  575.9 24.3 %collective-permute-start.87 = (bf16[8,128,128]{2,1,0:T(8,128)(2,1)S(1)}, bf16[8,128,128]{2,1,0:T(8,128)(2,1)S(1)}, u32[]{:S(2)}, u32[]{:S(2)}) collective-permute-start(bf16[8,128,128]{2,1,0:T(8,128)(2,1)S(1)} %get-tuple-element.640), channel_id=1, source_target_pairs={{0,6},{2,4},{4,2},{6,0},{8,14},{10,12},{12,10},{14,8},{16,22},{18,... | collective-permute-start | bytes 786440 | tf_op jit(solution)/shard_map/ppermute | solution.py:34
  578.7 21.5 %collective-permute-start.86 = (bf16[8,128,128]{2,1,0:T(8,128)(2,1)S(1)}, bf16[8,128,128]{2,1,0:T(8,128)(2,1)S(1)}, u32[]{:S(2)}, u32[]{:S(2)}) collective-permute-start(bf16[8,128,128]{2,1,0:T(8,128)(2,1)S(1)} %get-tuple-element.641), channel_id=1, source_target_pairs={{0,4},{2,6},{4,0},{6,2},{8,12},{10,14},{12,8},{14,10},{16,20},{18,... | collective-permute-start | bytes 786440 | tf_op jit(solution)/shard_map/ppermute | solution.py:34
  579.3 25.1 %collective-permute-start.85 = (bf16[8,128,128]{2,1,0:T(8,128)(2,1)S(1)}, bf16[8,128,128]{2,1,0:T(8,128)(2,1)S(1)}, u32[]{:S(2)}, u32[]{:S(2)}) collective-permute-start(bf16[8,128,128]{2,1,0:T(8,128)(2,1)S(1)} %get-tuple-element.642), channel_id=1, source_target_pairs={{0,2},{2,0},{4,6},{6,4},{8,10},{10,8},{12,14},{14,12},{16,18},{18,... | collective-permute-start | bytes 786440 | tf_op jit(solution)/shard_map/ppermute | solution.py:34
  629.9 40.5 %collective-permute-start.95 = (bf16[512,2048]{1,0:T(8,128)(2,1)}, bf16[512,2048]{1,0:T(8,128)(2,1)}, u32[]{:S(2)}, u32[]{:S(2)}) collective-permute-start(bf16[512,2048]{1,0:T(8,128)(2,1)} %convolution_convert_fusion.3), channel_id=1, source_target_pairs={{0,1},{1,0},{2,3},{3,2},{4,5},{5,4},{6,7},{7,6},{8,9},{9,8},{10,11... | collective-permute-start | bytes 6291464 | tf_op jit(solution)/shard_map/ppermute | solution.py:38
  637.0 37.7 %collective-permute-start.98 = (bf16[512,2048]{1,0:T(8,128)(2,1)}, bf16[512,2048]{1,0:T(8,128)(2,1)}, u32[]{:S(2)}, u32[]{:S(2)}) collective-permute-start(bf16[512,2048]{1,0:T(8,128)(2,1)} %convolution_convert_fusion.2), channel_id=1, source_target_pairs={{0,1},{1,0},{2,3},{3,2},{4,5},{5,4},{6,7},{7,6},{8,9},{9,8},{10,11... | collective-permute-start | bytes 6291464 | tf_op jit(solution)/shard_map/ppermute | solution.py:38
  649.9 14.3 %collective-permute-start.111 = (f32[304,128]{1,0:T(8,128)}, f32[304,128]{1,0:T(8,128)S(1)}, u32[]{:S(2)}, u32[]{:S(2)}) collective-permute-start(f32[304,128]{1,0:T(8,128)} %pad_maximum_fusion.19), channel_id=1, source_target_pairs={{0,4},{2,6},{4,0},{6,2},{8,12},{10,14},{12,8},{14,10},{16,20},{18,... | collective-permute-start | bytes 466952 | tf_op jit(solution)/shard_map/ppermute | solution.py:34
  653.4 76.6 %all-to-all-start.4 = ((bf16[16,3,128,128]{3,2,1,0:T(8,128)(2,1)}), bf16[16,3,128,128]{3,2,1,0:T(8,128)(2,1)}, u32[]{:S(2)}, u32[]{:S(2)}) async-start(bf16[16,3,128,128]{3,2,1,0:T(8,128)(2,1)} %get-tuple-element.546), calls=%async_computation.4 | async-start | bytes 3145728 | tf_op jit(solution)/shard_map/all_to_all | solution.py:195
  665.3 36.4 %collective-permute-start.115 = (f32[304,128]{1,0:T(8,128)S(1)}, f32[304,128]{1,0:T(8,128)S(1)}, u32[]{:S(2)}, u32[]{:S(2)}) collective-permute-start(f32[304,128]{1,0:T(8,128)S(1)} %add_add_fusion.1), channel_id=1, source_target_pairs={{0,24},{2,26},{4,28},{6,30},{8,16},{10,18},{12,20},{14,22},{16,8},... | collective-permute-start | bytes 466952 | tf_op jit(solution)/shard_map/ppermute | solution.py:34
  669.0 43.5 %collective-permute-start.114 = (f32[304,128]{1,0:T(8,128)S(1)}, f32[304,128]{1,0:T(8,128)S(1)}, u32[]{:S(2)}, u32[]{:S(2)}) collective-permute-start(f32[304,128]{1,0:T(8,128)S(1)} %add_add_fusion.1), channel_id=1, source_target_pairs={{0,16},{2,18},{4,20},{6,22},{8,24},{10,26},{12,28},{14,30},{16,0},... | collective-permute-start | bytes 466952 | tf_op jit(solution)/shard_map/ppermute | solution.py:34
  669.8 42.7 %collective-permute-start.113 = (f32[304,128]{1,0:T(8,128)S(1)}, f32[304,128]{1,0:T(8,128)S(1)}, u32[]{:S(2)}, u32[]{:S(2)}) collective-permute-start(f32[304,128]{1,0:T(8,128)S(1)} %add_add_fusion.1), channel_id=1, source_target_pairs={{0,8},{2,10},{4,12},{6,14},{8,0},{10,2},{12,4},{14,6},{16,24},{18,... | collective-permute-start | bytes 466952 | tf_op jit(solution)/shard_map/ppermute | solution.py:34
  673.3 16.9 %collective-permute-start.105 = (bf16[128,1024]{1,0:T(8,128)(2,1)S(1)}, bf16[128,1024]{1,0:T(8,128)(2,1)S(1)}, u32[]{:S(2)}, u32[]{:S(2)}) collective-permute-start(bf16[128,1024]{1,0:T(8,128)(2,1)S(1)} %get-tuple-element.582), channel_id=1, source_target_pairs={{0,2},{2,0},{4,6},{6,4},{8,10},{10,8},{12,14},{14,12},{16,18},{18,... | collective-permute-start | bytes 786440 | tf_op jit(solution)/shard_map/ppermute | solution.py:34
  674.7 19.4 %collective-permute-start.96 = (bf16[128,1024]{1,0:T(8,128)(2,1)S(1)}, bf16[128,1024]{1,0:T(8,128)(2,1)S(1)}, u32[]{:S(2)}, u32[]{:S(2)}) collective-permute-start(bf16[128,1024]{1,0:T(8,128)(2,1)S(1)} %get-tuple-element.584), channel_id=1, source_target_pairs={{0,2},{2,0},{4,6},{6,4},{8,10},{10,8},{12,14},{14,12},{16,18},{18,... | collective-permute-start | bytes 786440 | tf_op jit(solution)/shard_map/ppermute | solution.py:34
  694.3 28.1 %collective-permute-start.106 = (bf16[128,2048]{1,0:T(8,128)(2,1)S(1)}, bf16[128,2048]{1,0:T(8,128)(2,1)S(1)}, u32[]{:S(2)}, u32[]{:S(2)}) collective-permute-start(bf16[128,2048]{1,0:T(8,128)(2,1)S(1)} %get-tuple-element.568), channel_id=1, source_target_pairs={{0,4},{2,6},{4,0},{6,2},{8,12},{10,14},{12,8},{14,10},{16,20},{18,... | collective-permute-start | bytes 1572872 | tf_op jit(solution)/shard_map/ppermute | solution.py:34
  700.5 21.9 %collective-permute-start.104 = (bf16[128,2048]{1,0:T(8,128)(2,1)S(1)}, bf16[128,2048]{1,0:T(8,128)(2,1)S(1)}, u32[]{:S(2)}, u32[]{:S(2)}) collective-permute-start(bf16[128,2048]{1,0:T(8,128)(2,1)S(1)} %fusion.10), channel_id=1, source_target_pairs={{0,2},{2,0},{4,6},{6,4},{8,10},{10,8},{12,14},{14,12},{16,18},{18,... | collective-permute-start | bytes 1572872 | tf_op jit(solution)/shard_map/ppermute | solution.py:34
  715.1 18.1 %collective-permute-start.101 = (bf16[128,2048]{1,0:T(8,128)(2,1)S(1)}, bf16[128,2048]{1,0:T(8,128)(2,1)}, u32[]{:S(2)}, u32[]{:S(2)}) collective-permute-start(bf16[128,2048]{1,0:T(8,128)(2,1)S(1)} %get-tuple-element.569), channel_id=1, source_target_pairs={{0,4},{2,6},{4,0},{6,2},{8,12},{10,14},{12,8},{14,10},{16,20},{18,... | collective-permute-start | bytes 1572872 | tf_op jit(solution)/shard_map/ppermute | solution.py:34
  727.4 18.1 %collective-permute-start.107 = (bf16[64,2048]{1,0:T(8,128)(2,1)}, bf16[64,2048]{1,0:T(8,128)(2,1)}, u32[]{:S(2)}, u32[]{:S(2)}) collective-permute-start(bf16[64,2048]{1,0:T(8,128)(2,1)} %get-tuple-element.650), channel_id=1, source_target_pairs={{0,24},{2,26},{4,28},{6,30},{8,16},{10,18},{12,20},{14,22},{16,8},... | collective-permute-start | bytes 786440 | tf_op jit(solution)/shard_map/ppermute | solution.py:34
  730.0 20.9 %collective-permute-start.108 = (bf16[64,2048]{1,0:T(8,128)(2,1)}, bf16[64,2048]{1,0:T(8,128)(2,1)}, u32[]{:S(2)}, u32[]{:S(2)}) collective-permute-start(bf16[64,2048]{1,0:T(8,128)(2,1)} %get-tuple-element.651), channel_id=1, source_target_pairs={{0,16},{2,18},{4,20},{6,22},{8,24},{10,26},{12,28},{14,30},{16,0},... | collective-permute-start | bytes 786440 | tf_op jit(solution)/shard_map/ppermute | solution.py:34
  (141 other events, 1494.5 us)
